TPU v7x, 256 devices: a whole 4x4x8 slice. The times are simulated.
256 devices in a mesh: dom: 128 (over z, y, x), grp: 2 (over core).
Axes of the slice: x: 4, y: 4, z: 8, core: 2. Of those that a mesh axis runs over, the one named last changes fastest.
Arguments:
- feats: bfloat16 [393216, 128], P(('dom', 'grp')), may hold values from -6 to 6
- local_adj: bfloat16 [393216, 1536], P(('dom', 'grp')), may hold values from 0 to 2, as said below
- bnd_adj: bfloat16 [256, 6, 1536, 256], P(('dom', 'grp')), may hold values from 0 to 2, as said below
- send_index: int32 [256, 6, 256], P(('dom', 'grp')), may hold values from 0 to 1535
- w_self: bfloat16 [128, 256], replicated, may hold values from -0.5 to 0.5
- w_neigh: bfloat16 [128, 256], replicated, may hold values from -4 to 4
- bias: float32 [256], replicated, may hold values from -3 to 3
- cotangent: bfloat16 [393216, 256], P(('dom', 'grp')), may hold values from -6 to 6
Outputs:
- output: bfloat16 [393216, 256], P(('dom', 'grp'))
- grad_feats: bfloat16 [393216, 128], P(('dom', 'grp'))
- grad_self: float32 [128, 256], replicated
- grad_neigh: float32 [128, 256], replicated
Inputs may be any that keep to these rules, and one draw needn't show every extreme that they name: `local_adj`: edge weights are zero or between 0.5 and 2; most entries are zero. `bnd_adj`: edge weights are zero or between 0.5 and 2; most entries are zero.
All inputs are finite; a program needn't handle non-finite values.
Results may differ from a plain program's by a relative error of at most 0.0064.
Values may be sent and summed in bfloat16 or wider, within the bound.
No kernel may reach another device: no remote copies, remote signals or barrier semaphores. Data moves between devices by JAX's collectives and lax.ppermute only.
A program may use at most 128 MiB of HBM per device.

v0:
```python
import math

import jax
import jax.numpy as jnp
from jax import lax
from jax.sharding import PartitionSpec as P


def swapped(block, axis, distance):
    count = lax.axis_size(axis)
    route = []
    for low in range(count):
        high = low | 1 << distance
        if high != low and high < count:
            route += [(low, high), (high, low)]
    return lax.ppermute(block, axis, route)


def contract_rows(left, right):
    return lax.dot_general(
        left, right, (((0,), (0,)), ((), ())), preferred_element_type=jnp.float32
    )


def contract_cols(left, right):
    return lax.dot_general(
        left, right, (((1,), (1,)), ((), ())), preferred_element_type=jnp.float32
    )


def per_device(feats, local_adj, bnd_adj, send_index, w_self, w_neigh, bias, cotangent):
    dom_count = lax.axis_size("dom")
    bit_count = dom_count.bit_length() - 1
    bnd_tiles = bnd_adj[0]
    index_lists = send_index[0]
    rounds = bnd_tiles.shape[0]
    node_rows = feats.shape[0]

    def round_bit(round_index):
        return bit_count - 1 - round_index % bit_count

    denominator = (
        1.0
        + jnp.sum(local_adj, axis=1, dtype=jnp.float32)
        + jnp.sum(bnd_tiles, axis=(0, 2), dtype=jnp.float32)
    )
    outgoing_rows = [
        jnp.take(feats, index_lists[round_index], axis=0) for round_index in range(rounds)
    ]
    incoming = [
        swapped(outgoing_rows[round_index], "dom", round_bit(round_index))
        for round_index in range(rounds)
    ]
    summed = jnp.dot(local_adj, feats, preferred_element_type=jnp.float32)
    for round_index in range(rounds):
        summed = summed + jnp.dot(
            bnd_tiles[round_index], incoming[round_index], preferred_element_type=jnp.float32
        )
    aggregated = (summed / denominator[:, None]).astype(jnp.bfloat16)
    preact = (
        jnp.dot(feats, w_self, preferred_element_type=jnp.float32)
        + jnp.dot(aggregated, w_neigh, preferred_element_type=jnp.float32)
        + bias
    )
    sigmoid_pre = jax.nn.sigmoid(preact)
    output = (preact * sigmoid_pre).astype(jnp.bfloat16)
    derivative = sigmoid_pre * (1.0 + preact * (1.0 - sigmoid_pre))
    grad_pre = (cotangent.astype(jnp.float32) * derivative).astype(jnp.bfloat16)
    grad_agg = (contract_cols(grad_pre, w_neigh) / denominator[:, None]).astype(jnp.bfloat16)
    grad_feats = contract_cols(grad_pre, w_self) + contract_rows(local_adj, grad_agg)
    back_rows = [
        contract_rows(bnd_tiles[round_index], grad_agg).astype(jnp.bfloat16)
        for round_index in range(rounds)
    ]
    returned = [
        swapped(back_rows[round_index], "dom", round_bit(round_index))
        for round_index in range(rounds)
    ]
    for round_index in range(rounds):
        grad_feats = grad_feats.at[index_lists[round_index]].add(
            returned[round_index].astype(jnp.float32)
        )
    sum_self, sum_neigh = lax.psum(
        (contract_rows(feats, grad_pre), contract_rows(aggregated, grad_pre)), ("dom", "grp")
    )
    norm_scale = 1.0 / math.sqrt(node_rows * dom_count * lax.axis_size("grp"))
    return (output, grad_feats.astype(jnp.bfloat16), sum_self * norm_scale, sum_neigh * norm_scale)


def solution(mesh):
    placed = (
        P(("dom", "grp"), None),
        P(("dom", "grp"), None),
        P(("dom", "grp"), None, None, None),
        P(("dom", "grp"), None, None),
        P(),
        P(),
        P(),
        P(("dom", "grp"), None),
    )
    return jax.shard_map(
        per_device,
        mesh=mesh,
        in_specs=placed,
        out_specs=(P(("dom", "grp"), None), P(("dom", "grp"), None), P(), P()),
        check_vma=False,
    )
```

profile of v0, /device:TPU:1, one launch (start us, length us, event | category | flops | bytes accessed | tf_op | source)
XLA Modules:
  0.0 318.2 jit_solution(4303328081837059536)
XLA Ops:
  7.2 0.8 fusion.40
  8.3 0.9 gather_fusion
  9.2 7.8 %collective-permute-start = (bf16[256,128]{1,0:T(8,128)(2,1)S(1)}, bf16[256,128]{1,0:T(8,128)(2,1)S(1)}, u32[]{:S(2)}, u32[]{:S(2)}) collective-permute-start(bf16[256,128]{1,0:T(8,128)(2,1)S(1)} %broadcast_select_fusion.5), channel_id=1, source_target_pairs={{0,128},{128,0},{2,130},{130,2},{4,132},{132,4},{6,134},{134,6},{8... | collective-permute-start | bytes 196616 | tf_op jit(solution)/shard_map/ppermute | solution.py:16
  17.1 0.9 gather_fusion.1
  18.0 1.3 collective-permute-start.1
  19.3 0.9 gather_fusion.5
  20.3 2.8 collective-permute-start.5
  23.2 0.9 gather_fusion.4
  24.1 1.4 collective-permute-start.4
  25.5 0.9 gather_fusion.3
  26.5 2.7 collective-permute-start.3
  29.2 3.7 %fusion.42 = f32[1536,128]{1,0:T(8,128)S(1)} fusion(bf16[1536,1536]{1,0:T(8,128)(2,1)} %param.11, bf16[1536,128]{1,0:T(8,128)(2,1)S(1)} %copy-done), kind=kOutput, calls=%fused_computation.109 | convolution fusion | flops 603979776 | bytes 5898240 | tf_op jit(solution)/shard_map/dot_general | solution.py:54
  33.7 0.9 gather_fusion.2
  34.6 3.2 convert_reduce_fusion
  39.6 1.5 fusion.7
  43.1 1.8 multiply_convert_fusion
  44.9 1.1 fusion.43
  46.0 1.1 convolution_bitcast_fusion.7
  47.4 4.5 %convolution_bitcast_fusion.6 = f32[1536,128]{1,0:T(8,128)S(1)} fusion(bf16[1536,128]{1,0:T(8,128)(2,1)S(1)} %fusion.9, bf16[1536,1536]{1,0:T(8,128)(2,1)} %param.11), kind=kOutput, calls=%fused_computation.31 | convolution fusion | flops 603979776 | bytes 5898240 | tf_op jit(solution)/shard_map/dot_general | solution.py:20
  53.7 1.3 collective-permute-start.6
  57.1 3.7 %collective-permute-done.6 = bf16[256,128]{0,1:T(8,128)(2,1)S(1)} collective-permute-done((bf16[256,128]{0,1:T(8,128)(2,1)S(1)}, bf16[256,128]{0,1:T(8,128)(2,1)S(1)}, u32[]{:S(2)}, u32[]{:S(2)}) %collective-permute-start.6) | collective-permute-done | bytes 65568 | tf_op jit(solution)/shard_map/ppermute | solution.py:16
  61.5 2.4 scatter_fusion
  64.0 2.6 scatter_fusion.1
  66.7 2.2 scatter_fusion.2
  69.0 2.2 scatter_fusion.3
  71.4 2.2 scatter_fusion.4
  73.7 2.2 scatter_fusion.5
  76.0 0.8 convert_element_type.104
  76.8 232.0 %all-reduce.3.cloned.1.call-done = (f32[128,256]{0,1:T(8,128)}, f32[128,256]{0,1:T(8,128)}) async-done(((f32[128,256]{0,1:T(8,128)}, f32[128,256]{0,1:T(8,128)}), (f32[128,256]{0,1:T(8,128)}, f32[128,256]{0,1:T(8,128)})) %all-reduce.3.cloned.1.call-update) | async-done | bytes 262160 | tf_op jit(solution)/shard_map/psum | solution.py:83
  308.8 1.0 broadcast_multiply_fusion
  309.8 0.8 copy.42
  310.6 0.8 copy.43
  (90 shorter events, 10.6 us)
Async XLA Ops:
  7.2 1.1 copy-start
  7.2 301.6 %all-reduce.3.cloned.1.call-start = ((), (), s32[]{:S(2)}) async-start(), calls=%async_computation | async-start | bytes 524288 | tf_op jit(solution)/shard_map/psum | solution.py:83
  9.2 29.6 %collective-permute-start = (bf16[256,128]{1,0:T(8,128)(2,1)S(1)}, bf16[256,128]{1,0:T(8,128)(2,1)S(1)}, u32[]{:S(2)}, u32[]{:S(2)}) collective-permute-start(bf16[256,128]{1,0:T(8,128)(2,1)S(1)} %broadcast_select_fusion.5), channel_id=1, source_target_pairs={{0,128},{128,0},{2,130},{130,2},{4,132},{132,4},{6,134},{134,6},{8... | collective-permute-start | bytes 196616 | tf_op jit(solution)/shard_map/ppermute | solution.py:16
  18.0 23.0 %collective-permute-start.1 = (bf16[256,128]{1,0:T(8,128)(2,1)S(1)}, bf16[256,128]{1,0:T(8,128)(2,1)S(1)}, u32[]{:S(2)}, u32[]{:S(2)}) collective-permute-start(bf16[256,128]{1,0:T(8,128)(2,1)S(1)} %broadcast_select_fusion.4), channel_id=1, source_target_pairs={{0,64},{64,0},{2,66},{66,2},{4,68},{68,4},{6,70},{70,6},{8,72},{72... | collective-permute-start | bytes 196616 | tf_op jit(solution)/shard_map/ppermute | solution.py:16
  20.3 21.2 %collective-permute-start.5 = (bf16[256,128]{1,0:T(8,128)(2,1)S(1)}, bf16[256,128]{1,0:T(8,128)(2,1)S(1)}, u32[]{:S(2)}, u32[]{:S(2)}) collective-permute-start(bf16[256,128]{1,0:T(8,128)(2,1)S(1)} %broadcast_select_fusion), channel_id=1, source_target_pairs={{0,4},{4,0},{2,6},{6,2},{8,12},{12,8},{10,14},{14,10},{16,20},{20,... | collective-permute-start | bytes 196616 | tf_op jit(solution)/shard_map/ppermute | solution.py:16
  24.1 17.7 %collective-permute-start.4 = (bf16[256,128]{1,0:T(8,128)(2,1)S(1)}, bf16[256,128]{1,0:T(8,128)(2,1)S(1)}, u32[]{:S(2)}, u32[]{:S(2)}) collective-permute-start(bf16[256,128]{1,0:T(8,128)(2,1)S(1)} %broadcast_select_fusion.1), channel_id=1, source_target_pairs={{0,8},{8,0},{2,10},{10,2},{4,12},{12,4},{6,14},{14,6},{16,24},{24,... | collective-permute-start | bytes 196616 | tf_op jit(solution)/shard_map/ppermute | solution.py:16
  26.4 6.6 %copy-start.1 = (bf16[1536,1536]{1,0:T(8,128)(2,1)S(1)}, bf16[1536,1536]{1,0:T(8,128)(2,1)}, u32[]{:S(2)}) copy-start(bf16[1536,1536]{1,0:T(8,128)(2,1)} %param.11) | copy-start | bytes 14155780
  26.5 15.7 %collective-permute-start.3 = (bf16[256,128]{1,0:T(8,128)(2,1)S(1)}, bf16[256,128]{1,0:T(8,128)(2,1)S(1)}, u32[]{:S(2)}, u32[]{:S(2)}) collective-permute-start(bf16[256,128]{1,0:T(8,128)(2,1)S(1)} %broadcast_select_fusion.2), channel_id=1, source_target_pairs={{0,16},{16,0},{2,18},{18,2},{4,20},{20,4},{6,22},{22,6},{8,24},{24... | collective-permute-start | bytes 196616 | tf_op jit(solution)/shard_map/ppermute | solution.py:16
  33.0 4.8 %copy-start.2 = (bf16[128,256]{1,0:T(8,128)(2,1)S(1)}, bf16[128,256]{1,0:T(8,128)(2,1)}, u32[]{:S(2)}) copy-start(bf16[128,256]{1,0:T(8,128)(2,1)} %param.14) | copy-start | bytes 196612
  33.7 4.6 %copy-start.3 = (s32[1,6,256]{2,0,1:T(1,128)S(1)}, s32[1,6,256]{2,0,1:T(1,128)}, u32[]{:S(2)}) copy-start(s32[1,6,256]{2,0,1:T(1,128)} %param.13) | copy-start | bytes 18436
  33.7 7.4 %slice-start = ((s8[4718592]{0:T(1024)(128)(4,1)}), s8[524288]{0:T(1024)(128)(4,1)S(1)}, s32[]{:S(2)}) async-start(s8[4718592]{0:T(1024)(128)(4,1)} %bitcast.126), calls=%async_computation.1 | async-start | bytes 1048576
  34.6 6.5 %slice-start.1 = ((s8[4718592]{0:T(1024)(128)(4,1)}), s8[4194304]{0:T(1024)(128)(4,1)S(1)}, s32[]{:S(2)}) async-start(s8[4718592]{0:T(1024)(128)(4,1)} %bitcast.126), calls=%async_computation.2 | async-start | bytes 8388608
  38.8 3.8 %collective-permute-start.2 = (bf16[256,128]{1,0:T(8,128)(2,1)S(1)}, bf16[256,128]{1,0:T(8,128)(2,1)S(1)}, u32[]{:S(2)}, u32[]{:S(2)}) collective-permute-start(bf16[256,128]{1,0:T(8,128)(2,1)S(1)} %broadcast_select_fusion.3), channel_id=1, source_target_pairs={{0,32},{32,0},{2,34},{34,2},{4,36},{36,4},{6,38},{38,6},{8,40},{40... | collective-permute-start | bytes 196616 | tf_op jit(solution)/shard_map/ppermute | solution.py:16
  41.5 1.6 copy-start.4
  41.5 1.6 copy-start.5
  41.5 1.6 copy-start.6
  44.9 7.0 %slice-start.2 = ((s8[4718592]{0:T(1024)(128)(4,1)}), s8[524288]{0:T(1024)(128)(4,1)S(1)}, s32[]{:S(2)}) async-start(s8[4718592]{0:T(1024)(128)(4,1)} %bitcast.128), calls=%async_computation.3 | async-start | bytes 1048576
  47.0 4.9 %slice-start.3 = ((s8[4718592]{0:T(1024)(128)(4,1)}), s8[4194304]{0:T(1024)(128)(4,1)S(1)}, s32[]{:S(2)}) async-start(s8[4718592]{0:T(1024)(128)(4,1)} %bitcast.128), calls=%async_computation.4 | async-start | bytes 8388608
  53.7 7.1 %collective-permute-start.6 = (bf16[256,128]{0,1:T(8,128)(2,1)S(1)}, bf16[256,128]{0,1:T(8,128)(2,1)S(1)}, u32[]{:S(2)}, u32[]{:S(2)}) collective-permute-start(bf16[256,128]{0,1:T(8,128)(2,1)S(1)} %fusion.10), channel_id=1, source_target_pairs={{0,128},{128,0},{2,130},{130,2},{4,132},{132,4},{6,134},{134,6},{8... | collective-permute-start | bytes 196616 | tf_op jit(solution)/shard_map/ppermute | solution.py:16
  55.2 8.6 %collective-permute-start.7 = (bf16[256,128]{0,1:T(8,128)(2,1)S(1)}, bf16[256,128]{0,1:T(8,128)(2,1)S(1)}, u32[]{:S(2)}, u32[]{:S(2)}) collective-permute-start(bf16[256,128]{0,1:T(8,128)(2,1)S(1)} %fusion.11), channel_id=1, source_target_pairs={{0,64},{64,0},{2,66},{66,2},{4,68},{68,4},{6,70},{70,6},{8,72},{72... | collective-permute-start | bytes 196616 | tf_op jit(solution)/shard_map/ppermute | solution.py:16
  55.4 11.2 %collective-permute-start.8 = (bf16[256,128]{0,1:T(8,128)(2,1)S(1)}, bf16[256,128]{0,1:T(8,128)(2,1)S(1)}, u32[]{:S(2)}, u32[]{:S(2)}) collective-permute-start(bf16[256,128]{0,1:T(8,128)(2,1)S(1)} %fusion.12), channel_id=1, source_target_pairs={{0,32},{32,0},{2,34},{34,2},{4,36},{36,4},{6,38},{38,6},{8,40},{40... | collective-permute-start | bytes 196616 | tf_op jit(solution)/shard_map/ppermute | solution.py:16
  56.1 12.8 %collective-permute-start.9 = (bf16[256,128]{0,1:T(8,128)(2,1)S(1)}, bf16[256,128]{0,1:T(8,128)(2,1)S(1)}, u32[]{:S(2)}, u32[]{:S(2)}) collective-permute-start(bf16[256,128]{0,1:T(8,128)(2,1)S(1)} %fusion.13), channel_id=1, source_target_pairs={{0,16},{16,0},{2,18},{18,2},{4,20},{20,4},{6,22},{22,6},{8,24},{24... | collective-permute-start | bytes 196616 | tf_op jit(solution)/shard_map/ppermute | solution.py:16
  56.7 14.5 %collective-permute-start.10 = (bf16[256,128]{0,1:T(8,128)(2,1)S(1)}, bf16[256,128]{0,1:T(8,128)(2,1)S(1)}, u32[]{:S(2)}, u32[]{:S(2)}) collective-permute-start(bf16[256,128]{0,1:T(8,128)(2,1)S(1)} %fusion.14), channel_id=1, source_target_pairs={{0,8},{8,0},{2,10},{10,2},{4,12},{12,4},{6,14},{14,6},{16,24},{24,... | collective-permute-start | bytes 196616 | tf_op jit(solution)/shard_map/ppermute | solution.py:16
  60.8 12.9 %collective-permute-start.11 = (bf16[256,128]{0,1:T(8,128)(2,1)S(1)}, bf16[256,128]{0,1:T(8,128)(2,1)S(1)}, u32[]{:S(2)}, u32[]{:S(2)}) collective-permute-start(bf16[256,128]{0,1:T(8,128)(2,1)S(1)} %fusion.15), channel_id=1, source_target_pairs={{0,4},{4,0},{2,6},{6,2},{8,12},{12,8},{10,14},{14,10},{16,20},{20,... | collective-permute-start | bytes 196616 | tf_op jit(solution)/shard_map/ppermute | solution.py:16
Sparse Core Ops, SparseCore 0:
  57.2 251.5 all-reduce.2
where the time goes:
time: 319 us; the launch traced here: 318 us
  waiting for transfers between devices  236 us (74%)
  other arithmetic  20.9 us (7%)
  starting transfers between devices  20.1 us (6%)
  matrix products  18.6 us (6%)
  between operations  14.6 us (5%)
  local copies, waits for them, and re-layouts  8.3 us (3%)
    psum x1, waiting for transfers between devices, per_device(): lax.psum((contract_rows(feats, grad_pre), contract_rows(aggregated, grad_...  232 us
    ppermute x12, starting transfers between devices, swapped(): return lax.ppermute(block, axis, route)  20 us
    scatter-add x6, other arithmetic, per_device(): grad_feats.at[index_lists[round_index]]  13.9 us
    dot_general x9, matrix products, contract_rows(): lax.dot_general(left, right, (((0,), (0,)), ((), ())), preferred_element_...  8.64 us
  transfers between devices with their start and end apart: 13, of which 2 were waited for; matrix products, arithmetic and copies ran while one was open for 10% of the time, Pallas kernels for 0%

commit v1 on v0

v1 whole, which is shorter than its diff:
```python
import functools
import math

import jax
import jax.numpy as jnp
from jax import lax
from jax.experimental import pallas as pl
from jax.experimental.pallas import tpu as pltpu
from jax.sharding import PartitionSpec as P

F32 = jnp.float32
BF16 = jnp.bfloat16
BLOCK = 256


def dot(left, right, left_dim=1, right_dim=0):
    return lax.dot_general(
        left, right, (((left_dim,), (right_dim,)), ((), ())), preferred_element_type=F32
    )


def whole(shape):
    return pl.BlockSpec(shape, lambda *_: (0,) * len(shape))


def rows_of(block, width):
    return pl.BlockSpec((block, width), lambda i: (i, 0))


def cost(flops, nbytes):
    return pl.CostEstimate(flops=int(flops), bytes_accessed=int(nbytes), transcendentals=0)


def params(mib):
    return pltpu.CompilerParams(vmem_limit_bytes=mib * 1024 * 1024)


def one_hot(index_row, count):
    places = lax.broadcasted_iota(jnp.int32, (count, index_row.shape[1]), 0)
    return (places == index_row).astype(F32).astype(BF16)


def gather_kernel(feats_ref, index_ref, *out_refs):
    turned = feats_ref[...].T
    for turn, out_ref in enumerate(out_refs):
        picked = dot(turned, one_hot(index_ref[turn : turn + 1, :], feats_ref.shape[0]))
        out_ref[...] = picked.T.astype(out_ref.dtype)


def gather_rows(feats, index_lists):
    rounds, picks = index_lists.shape
    rows, width = feats.shape
    shape = jax.ShapeDtypeStruct((picks, width), feats.dtype)
    return pl.pallas_call(
        gather_kernel,
        out_shape=(shape,) * rounds,
        compiler_params=params(32),
        cost_estimate=cost(2 * rows * picks * width * rounds, rows * width * 2),
        name="gather_rows",
    )(feats, index_lists)


def local_kernel(adj_ref, feats_ref, out_ref, wide_ref):
    width = feats_ref.shape[1]

    @pl.when(pl.program_id(0) == 0)
    def _():
        wide_ref[:, :width] = feats_ref[...]
        wide_ref[:, width:] = jnp.ones_like(feats_ref)

    out_ref[...] = dot(adj_ref[...], wide_ref[...])


def local_sum(local_adj, feats):
    rows, width = feats.shape
    return pl.pallas_call(
        local_kernel,
        grid=(rows // BLOCK,),
        in_specs=[rows_of(BLOCK, rows), whole((rows, width))],
        out_specs=rows_of(BLOCK, 2 * width),
        out_shape=jax.ShapeDtypeStruct((rows, 2 * width), F32),
        scratch_shapes=[pltpu.VMEM((rows, 2 * width), BF16)],
        compiler_params=params(32),
        cost_estimate=cost(4 * rows * rows * width, rows * rows * 2),
        name="local_sum",
    )(local_adj, feats)


def middle_kernel(rounds, *refs):
    local_ref, bnd_ref, feats_ref, cot_ref, self_ref, neigh_ref, bias_ref = refs[:7]
    recv_refs = refs[7 : 7 + rounds]
    out_ref, dagg_ref, gself_ref, gw_ref = refs[7 + rounds : 11 + rounds]
    back_refs = refs[11 + rounds : 11 + 2 * rounds]
    wide_ref, back_acc, gw_acc = refs[11 + 2 * rounds :]
    width = feats_ref.shape[1]
    step = pl.program_id(0)

    @pl.when(step == 0)
    def _():
        for turn in range(rounds):
            wide_ref[turn, :, :width] = recv_refs[turn][...]
            wide_ref[turn, :, width:] = jnp.ones_like(recv_refs[turn])
        back_acc[...] = jnp.zeros_like(back_acc)
        gw_acc[...] = jnp.zeros_like(gw_acc)

    total = local_ref[...]
    for turn in range(rounds):
        total = total + dot(bnd_ref[turn], wide_ref[turn])
    inverse = 1.0 / (1.0 + total[:, width:])
    agg = (total[:, :width] * inverse).astype(BF16)
    both = jnp.concatenate([feats_ref[...], agg], axis=1)
    weights = jnp.concatenate([self_ref[...], neigh_ref[...]], axis=0)
    pre = dot(both, weights) + bias_ref[...]
    sig = 1.0 / (1.0 + jnp.exp(-pre))
    out_ref[...] = (pre * sig).astype(out_ref.dtype)
    slope = sig * (1.0 + pre * (1.0 - sig))
    dpre = (cot_ref[...].astype(F32) * slope).astype(BF16)
    grads = dot(dpre, weights, 1, 1)
    gself_ref[...] = grads[:, :width]
    dagg = (grads[:, width:] * inverse).astype(BF16)
    dagg_ref[...] = dagg
    gw_acc[...] += dot(both, dpre, 0, 0)
    turned = dagg.T
    for turn in range(rounds):
        back_acc[turn] += dot(turned, bnd_ref[turn])

    @pl.when(step == pl.num_programs(0) - 1)
    def _():
        gw_ref[...] = gw_acc[...]
        for turn in range(rounds):
            back_refs[turn][...] = back_acc[turn].T.astype(BF16)


def middle(local, bnd_tiles, feats, cotangent, w_self, w_neigh, bias, incoming):
    rounds, rows, bnd = bnd_tiles.shape
    width, hidden = w_self.shape
    results = pl.pallas_call(
        functools.partial(middle_kernel, rounds),
        grid=(rows // BLOCK,),
        in_specs=[
            rows_of(BLOCK, 2 * width),
            pl.BlockSpec((rounds, BLOCK, bnd), lambda i: (0, i, 0)),
            rows_of(BLOCK, width),
            rows_of(BLOCK, hidden),
            whole((width, hidden)),
            whole((width, hidden)),
            whole((1, hidden)),
        ]
        + [whole((bnd, width))] * rounds,
        out_specs=[
            rows_of(BLOCK, hidden),
            rows_of(BLOCK, width),
            rows_of(BLOCK, width),
            whole((2 * width, hidden)),
        ]
        + [whole((bnd, width))] * rounds,
        out_shape=[
            jax.ShapeDtypeStruct((rows, hidden), BF16),
            jax.ShapeDtypeStruct((rows, width), BF16),
            jax.ShapeDtypeStruct((rows, width), F32),
            jax.ShapeDtypeStruct((2 * width, hidden), F32),
        ]
        + [jax.ShapeDtypeStruct((bnd, width), BF16)] * rounds,
        scratch_shapes=[
            pltpu.VMEM((rounds, bnd, 2 * width), BF16),
            pltpu.VMEM((rounds, width, bnd), F32),
            pltpu.VMEM((2 * width, hidden), F32),
        ],
        compiler_params=params(32),
        cost_estimate=cost(8 * rounds * rows * bnd * width, rounds * rows * bnd * 2),
        name="middle",
    )(local, bnd_tiles, feats, cotangent, w_self, w_neigh, bias.reshape(1, hidden), *incoming)
    return results[0], results[1], results[2], results[3], results[4:]


def turned_kernel(adj_ref, dagg_ref, gself_ref, out_ref, acc_ref):
    step = pl.program_id(0)

    @pl.when(step == 0)
    def _():
        acc_ref[...] = jnp.zeros_like(acc_ref)

    acc_ref[...] += dot(dagg_ref[...].T, adj_ref[...])

    @pl.when(step == pl.num_programs(0) - 1)
    def _():
        out_ref[...] = gself_ref[...] + acc_ref[...].T


def turned_sum(local_adj, dagg, gself):
    rows, width = dagg.shape
    return pl.pallas_call(
        turned_kernel,
        grid=(rows // BLOCK,),
        in_specs=[rows_of(BLOCK, rows), rows_of(BLOCK, width), whole((rows, width))],
        out_specs=whole((rows, width)),
        out_shape=jax.ShapeDtypeStruct((rows, width), F32),
        scratch_shapes=[pltpu.VMEM((width, rows), F32)],
        compiler_params=params(32),
        cost_estimate=cost(2 * rows * rows * width, rows * rows * 2),
        name="turned_sum",
    )(local_adj, dagg, gself)


def scatter_kernel(base_ref, index_ref, *refs):
    total = base_ref[...]
    for turn, back_ref in enumerate(refs[:-1]):
        total = total + dot(
            one_hot(index_ref[turn : turn + 1, :], base_ref.shape[0]), back_ref[...]
        )
    refs[-1][...] = total.astype(refs[-1].dtype)


def scatter_rows(base, index_lists, returned):
    rounds, picks = index_lists.shape
    rows, width = base.shape
    return pl.pallas_call(
        scatter_kernel,
        out_shape=jax.ShapeDtypeStruct((rows, width), BF16),
        compiler_params=params(32),
        cost_estimate=cost(2 * rows * picks * width * rounds, rows * width * 6),
        name="scatter_rows",
    )(base, index_lists, *returned)


def swapped(block, axis, distance):
    count = lax.axis_size(axis)
    route = [(low, low ^ 1 << distance) for low in range(count)]
    route = [(low, high) for low, high in route if high < count]
    return lax.ppermute(block, axis, route)


def summed_over_all(partial):
    bits = lax.axis_size("dom").bit_length() - 1
    own = lax.axis_index("grp") == 0
    half = jnp.where(own, partial[0], partial[1])
    other = jnp.where(own, partial[1], partial[0])
    half = half + swapped(other, "grp", 0)
    for bit in range(bits):
        half = half + swapped(half, "dom", bit)
    other = swapped(half, "grp", 0)
    return jnp.where(own, half, other), jnp.where(own, other, half)


def per_device(feats, local_adj, bnd_adj, send_index, w_self, w_neigh, bias, cotangent):
    dom_count = lax.axis_size("dom")
    bit_count = dom_count.bit_length() - 1
    bnd_tiles = bnd_adj[0]
    index_lists = send_index[0]
    rounds = bnd_tiles.shape[0]
    rows, width = feats.shape

    def round_bit(turn):
        return bit_count - 1 - turn % bit_count

    outgoing = gather_rows(feats, index_lists)
    incoming = [swapped(outgoing[turn], "dom", round_bit(turn)) for turn in range(rounds)]
    local = local_sum(local_adj, feats)
    output, dagg, gself, gw, back = middle(
        local, bnd_tiles, feats, cotangent, w_self, w_neigh, bias, incoming
    )
    returned = [swapped(back[turn], "dom", round_bit(turn)) for turn in range(rounds)]
    base = turned_sum(local_adj, dagg, gself)
    grad_feats = scatter_rows(base, index_lists, returned)
    sum_self, sum_neigh = summed_over_all(gw.reshape(2, width, gw.shape[1]))
    scale = 1.0 / math.sqrt(rows * dom_count * lax.axis_size("grp"))
    return output, grad_feats, sum_self * scale, sum_neigh * scale


def solution(mesh):
    placed = (
        P(("dom", "grp"), None),
        P(("dom", "grp"), None),
        P(("dom", "grp"), None, None, None),
        P(("dom", "grp"), None, None),
        P(),
        P(),
        P(),
        P(("dom", "grp"), None),
    )
    return jax.shard_map(
        per_device,
        mesh=mesh,
        in_specs=placed,
        out_specs=(P(("dom", "grp"), None), P(("dom", "grp"), None), P(), P()),
        check_vma=False,
    )
```

time: 319 us -> 101 us (0.32)
  waiting for transfers between devices: 236 us -> 30.8 us
  starting transfers between devices: 20.1 us -> 46.6 us
  other arithmetic: 20.9 us -> 0.88 us
  matrix products: 18.6 us -> 0 us
  Pallas kernels: 0 us -> 16.8 us
  between operations: 14.6 us -> 0.83 us
  local copies, waits for them, and re-layouts: 8.3 us -> 5.06 us
    psum x1 -> x0, waiting for transfers between devices: 232 us -> none  [per_device(): lax.psum((contract_rows(feats, grad_pre), contract_rows(aggregated, grad_...]
    ppermute x12 -> x21, waiting for transfers between devices: 3.73 us -> 30.8 us  [swapped(): return lax.ppermute(block, axis, route)]
    ppermute x12 -> x21, starting transfers between devices: 20 us -> 46.6 us  [swapped(): return lax.ppermute(block, axis, route)]
    dot_general x20 -> x0, matrix products: 18.6 us -> none  [the longest x9 8.64 us: contract_rows(): lax.dot_general(left, right, (((0,), (0,)), ((), ())), preferred_element_...]
    pallas_call x0 -> x5, Pallas kernels: none -> 16.8 us  [the longest x1 8.94 us: middle(): pl.pallas_call(functools.partial(middle_kernel, rounds), grid=(rows // BL...]
    scatter-add x6 -> x0, other arithmetic: 13.9 us -> none  [per_device(): grad_feats.at[index_lists[round_index]]]
    gather x6 -> x0, local copies, waits for them, and re-layouts: 5.13 us -> none  [per_device(): jnp.take(feats, index_lists[round_index], axis=0)]
    reduce_sum x2 -> x0, other arithmetic: 3.86 us -> none  [the longest x1 3.17 us: per_device(): jnp.sum(bnd_tiles, axis=(0, 2), dtype=jnp.float32)]
  transfers between devices with their start and end apart: 13 -> 21, of which waited for: 2 -> 9; matrix products, arithmetic and copies ran while one was open for 10% -> 0% of each run, Pallas kernels for 0% -> 7%
where the time goes in v1:
time: 101 us
  starting transfers between devices  46.6 us (46%)
  waiting for transfers between devices  30.8 us (30%)
  Pallas kernels  16.8 us (17%)
  local copies, waits for them, and re-layouts  5.06 us (5%)
    ppermute x21, starting transfers between devices, swapped(): return lax.ppermute(block, axis, route)  46.6 us
    ppermute x21, waiting for transfers between devices, swapped(): return lax.ppermute(block, axis, route)  30.8 us
    pallas_call x1, Pallas kernels, middle(): pl.pallas_call(functools.partial(middle_kernel, rounds), grid=(rows // BL...  8.94 us
    unnamed x23, local copies, waits for them, and re-layouts  5.06 us
    pallas_call x1, Pallas kernels, local_sum(): pl.pallas_call(local_kernel, grid=(rows // BLOCK,), in_specs=[rows_of(BLO...  2.39 us
    pallas_call x1, Pallas kernels, scatter_rows(): pl.pallas_call(scatter_kernel, out_shape=jax.ShapeDtypeStruct((rows, widt...  2.14 us
    pallas_call x1, Pallas kernels, turned_sum(): pl.pallas_call(turned_kernel, grid=(rows // BLOCK,), in_specs=[rows_of(BL...  2.12 us
  transfers between devices with their start and end apart: 21, of which 9 were waited for; matrix products, arithmetic and copies ran while one was open for 0% of the time, Pallas kernels for 7%

profile of v1, /device:TPU:1, one launch (start us, length us, event | category | flops | bytes accessed | tf_op | source)
XLA Modules:
  0.0 101.0 jit_solution(5212394664930140943)
XLA Ops:
  1.3 1.0 copy-done.1
  2.3 1.2 %gather_rows.1 = (bf16[256,128]{1,0:T(8,128)(2,1)S(1)}, bf16[256,128]{1,0:T(8,128)(2,1)S(1)}, bf16[256,128]{1,0:T(8,128)(2,1)S(1)}, bf16[256,128]{1,0:T(8,128)(2...) custom-call(bf16[1536,128]{1,0:T(8,128)(2,1)S(1)} %copy-done.1, s32[6,256]{1,0:T(8,128)S(1)} %bitcast.7), custom_call_target="tpu_custom_call" | custom-call | flops 603979776 | bytes 393216 | tf_op jit(solution)/shard_map/gather_rows/pallas_call | solution.py:54
  3.6 7.8 %collective-permute-start = (bf16[256,128]{1,0:T(8,128)(2,1)S(1)}, bf16[256,128]{1,0:T(8,128)(2,1)S(1)}, u32[]{:S(2)}, u32[]{:S(2)}) collective-permute-start(bf16[256,128]{1,0:T(8,128)(2,1)S(1)} %get-tuple-element.20), channel_id=1, source_target_pairs={{0,128},{2,130},{4,132},{6,134},{8,136},{10,138},{12,140},{14,142}... | collective-permute-start | bytes 196616 | tf_op jit(solution)/shard_map/ppermute | solution.py:230
  11.4 1.2 %collective-permute-start.1 = (bf16[256,128]{1,0:T(8,128)(2,1)S(1)}, bf16[256,128]{1,0:T(8,128)(2,1)S(1)}, u32[]{:S(2)}, u32[]{:S(2)}) collective-permute-start(bf16[256,128]{1,0:T(8,128)(2,1)S(1)} %get-tuple-element.21), channel_id=1, source_target_pairs={{0,64},{2,66},{4,68},{6,70},{8,72},{10,74},{12,76},{14,78},{16,80}... | collective-permute-start | bytes 196616 | tf_op jit(solution)/shard_map/ppermute | solution.py:230
  13.3 2.9 %collective-permute-start.3 = (bf16[256,128]{1,0:T(8,128)(2,1)S(1)}, bf16[256,128]{1,0:T(8,128)(2,1)S(1)}, u32[]{:S(2)}, u32[]{:S(2)}) collective-permute-start(bf16[256,128]{1,0:T(8,128)(2,1)S(1)} %get-tuple-element.23), channel_id=1, source_target_pairs={{0,16},{2,18},{4,20},{6,22},{8,24},{10,26},{12,28},{14,30},{16,0},... | collective-permute-start | bytes 196616 | tf_op jit(solution)/shard_map/ppermute | solution.py:230
  16.7 2.7 %collective-permute-start.5 = (bf16[256,128]{1,0:T(8,128)(2,1)S(1)}, bf16[256,128]{1,0:T(8,128)(2,1)S(1)}, u32[]{:S(2)}, u32[]{:S(2)}) collective-permute-start(bf16[256,128]{1,0:T(8,128)(2,1)S(1)} %get-tuple-element.25), channel_id=1, source_target_pairs={{0,4},{2,6},{4,0},{6,2},{8,12},{10,14},{12,8},{14,10},{16,20},{18,... | collective-permute-start | bytes 196616 | tf_op jit(solution)/shard_map/ppermute | solution.py:230
  19.4 2.3 %copy-done = bf16[1536,1536]{1,0:T(8,128)(2,1)S(1)} copy-done((bf16[1536,1536]{1,0:T(8,128)(2,1)S(1)}, bf16[1536,1536]{1,0:T(8,128)(2,1)}, u32[]{:S(2)}) %copy-start) | copy-done | bytes 4718616
  21.7 1.0 copy-done.2
  22.7 2.4 %local_sum.1.refs_0_ = f32[1536,256]{1,0:T(8,128)S(1)} custom-call(bf16[1536,1536]{1,0:T(8,128)(2,1)S(1)} %copy-done, bf16[1536,128]{1,0:T(8,128)(2,1)S(1)} %copy-done.2), custom_call_target="tpu_custom_call" | custom-call | flops 1207959552 | bytes 4718592 | tf_op jit(solution)/shard_map/local_sum/pallas_call | solution.py:76
  25.3 8.9 %middle.1 = (bf16[1536,256]{1,0:T(8,128)(2,1)}, bf16[1536,128]{1,0:T(8,128)(2,1)S(1)}, f32[1536,128]{1,0:T(8,128)S(1)}, f32[256,256]{1,0:T(8,128)S(1)}, bf16[256...) custom-call(f32[1536,256]{1,0:T(8,128)S(1)} %local_sum.1.refs_0_, ...), custom_call_target="tpu_custom_call" | custom-call | flops 2415919104 | bytes 4718592 | tf_op jit(solution)/shard_map/middle/pallas_call | solution.py:137
  34.2 2.4 %collective-permute-start.12 = (f32[128,256]{1,0:T(8,128)S(1)}, f32[128,256]{1,0:T(8,128)S(1)}, u32[]{:S(2)}, u32[]{:S(2)}) collective-permute-start(f32[128,256]{1,0:T(8,128)S(1)} %slice_select_fusion), channel_id=1, source_target_pairs={{0,1},{1,0},{2,3},{3,2},{4,5},{5,4},{6,7},{7,6},{8,9},{9,8},{10,11... | collective-permute-start | bytes 393224 | tf_op jit(solution)/shard_map/ppermute | solution.py:230
  36.7 1.0 collective-permute-done.12
  38.1 4.4 %collective-permute-done.13 = f32[128,256]{1,0:T(8,128)S(1)} collective-permute-done((f32[128,256]{1,0:T(8,128)S(1)}, f32[128,256]{1,0:T(8,128)S(1)}, u32[]{:S(2)}, u32[]{:S(2)}) %collective-permute-start.13) | collective-permute-done | bytes 131104 | tf_op jit(solution)/shard_map/ppermute | solution.py:230
  42.5 1.0 collective-permute-start.14
  43.5 4.4 %collective-permute-done.14 = f32[128,256]{1,0:T(8,128)S(1)} collective-permute-done((f32[128,256]{1,0:T(8,128)S(1)}, f32[128,256]{1,0:T(8,128)S(1)}, u32[]{:S(2)}, u32[]{:S(2)}) %collective-permute-start.14) | collective-permute-done | bytes 131104 | tf_op jit(solution)/shard_map/ppermute | solution.py:230
  47.9 1.2 %collective-permute-start.15 = (f32[128,256]{1,0:T(8,128)S(1)}, f32[128,256]{1,0:T(8,128)S(1)}, u32[]{:S(2)}, u32[]{:S(2)}) collective-permute-start(f32[128,256]{1,0:T(8,128)S(1)} %add.26), channel_id=1, source_target_pairs={{0,8},{2,10},{4,12},{6,14},{8,0},{10,2},{12,4},{14,6},{16,24},{18,... | collective-permute-start | bytes 393224 | tf_op jit(solution)/shard_map/ppermute | solution.py:230
  49.1 2.7 %collective-permute-done.15 = f32[128,256]{1,0:T(8,128)S(1)} collective-permute-done((f32[128,256]{1,0:T(8,128)S(1)}, f32[128,256]{1,0:T(8,128)S(1)}, u32[]{:S(2)}, u32[]{:S(2)}) %collective-permute-start.15) | collective-permute-done | bytes 131104 | tf_op jit(solution)/shard_map/ppermute | solution.py:230
  51.9 1.6 %collective-permute-start.16 = (f32[128,256]{1,0:T(8,128)S(1)}, f32[128,256]{1,0:T(8,128)S(1)}, u32[]{:S(2)}, u32[]{:S(2)}) collective-permute-start(f32[128,256]{1,0:T(8,128)S(1)} %add.27), channel_id=1, source_target_pairs={{0,16},{2,18},{4,20},{6,22},{8,24},{10,26},{12,28},{14,30},{16,0},... | collective-permute-start | bytes 393224 | tf_op jit(solution)/shard_map/ppermute | solution.py:230
  53.5 3.8 %collective-permute-done.16 = f32[128,256]{1,0:T(8,128)S(1)} collective-permute-done((f32[128,256]{1,0:T(8,128)S(1)}, f32[128,256]{1,0:T(8,128)S(1)}, u32[]{:S(2)}, u32[]{:S(2)}) %collective-permute-start.16) | collective-permute-done | bytes 131104 | tf_op jit(solution)/shard_map/ppermute | solution.py:230
  58.1 3.4 %collective-permute-done.17 = f32[128,256]{1,0:T(8,128)S(1)} collective-permute-done((f32[128,256]{1,0:T(8,128)S(1)}, f32[128,256]{1,0:T(8,128)S(1)}, u32[]{:S(2)}, u32[]{:S(2)}) %collective-permute-start.17) | collective-permute-done | bytes 131104 | tf_op jit(solution)/shard_map/ppermute | solution.py:230
  61.5 1.3 %collective-permute-start.18 = (f32[128,256]{1,0:T(8,128)S(1)}, f32[128,256]{1,0:T(8,128)S(1)}, u32[]{:S(2)}, u32[]{:S(2)}) collective-permute-start(f32[128,256]{1,0:T(8,128)S(1)} %add.29), channel_id=1, source_target_pairs={{0,64},{2,66},{4,68},{6,70},{8,72},{10,74},{12,76},{14,78},{16,80}... | collective-permute-start | bytes 393224 | tf_op jit(solution)/shard_map/ppermute | solution.py:230
  62.8 4.8 %collective-permute-done.18 = f32[128,256]{1,0:T(8,128)S(1)} collective-permute-done((f32[128,256]{1,0:T(8,128)S(1)}, f32[128,256]{1,0:T(8,128)S(1)}, u32[]{:S(2)}, u32[]{:S(2)}) %collective-permute-start.18) | collective-permute-done | bytes 131104 | tf_op jit(solution)/shard_map/ppermute | solution.py:230
  67.7 3.1 %collective-permute-start.19 = (f32[128,256]{1,0:T(8,128)S(1)}, f32[128,256]{1,0:T(8,128)S(1)}, u32[]{:S(2)}, u32[]{:S(2)}) collective-permute-start(f32[128,256]{1,0:T(8,128)S(1)} %add.30), channel_id=1, source_target_pairs={{0,128},{2,130},{4,132},{6,134},{8,136},{10,138},{12,140},{14,142}... | collective-permute-start | bytes 393224 | tf_op jit(solution)/shard_map/ppermute | solution.py:230
  70.8 1.2 %collective-permute-start.11 = (bf16[256,128]{1,0:T(8,128)(2,1)S(1)}, bf16[256,128]{1,0:T(8,128)(2,1)S(1)}, u32[]{:S(2)}, u32[]{:S(2)}) collective-permute-start(bf16[256,128]{1,0:T(8,128)(2,1)S(1)} %get-tuple-element.34), channel_id=1, source_target_pairs={{0,4},{2,6},{4,0},{6,2},{8,12},{10,14},{12,8},{14,10},{16,20},{18,... | collective-permute-start | bytes 196616 | tf_op jit(solution)/shard_map/ppermute | solution.py:230
  72.0 4.9 %collective-permute-done.19 = f32[128,256]{1,0:T(8,128)S(1)} collective-permute-done((f32[128,256]{1,0:T(8,128)S(1)}, f32[128,256]{1,0:T(8,128)S(1)}, u32[]{:S(2)}, u32[]{:S(2)}) %collective-permute-start.19) | collective-permute-done | bytes 131104 | tf_op jit(solution)/shard_map/ppermute | solution.py:230
  77.0 11.4 %collective-permute-start.20 = (f32[128,256]{1,0:T(8,128)S(1)}, f32[128,256]{1,0:T(8,128)S(1)}, u32[]{:S(2)}, u32[]{:S(2)}) collective-permute-start(f32[128,256]{1,0:T(8,128)S(1)} %add.31), channel_id=1, source_target_pairs={{0,1},{1,0},{2,3},{3,2},{4,5},{5,4},{6,7},{7,6},{8,9},{9,8},{10,11... | collective-permute-start | bytes 393224 | tf_op jit(solution)/shard_map/ppermute | solution.py:230
  88.4 3.1 %collective-permute-start.6 = (bf16[256,128]{1,0:T(8,128)(2,1)S(1)}, bf16[256,128]{1,0:T(8,128)(2,1)S(1)}, u32[]{:S(2)}, u32[]{:S(2)}) collective-permute-start(bf16[256,128]{1,0:T(8,128)(2,1)S(1)} %get-tuple-element.29), channel_id=1, source_target_pairs={{0,128},{2,130},{4,132},{6,134},{8,136},{10,138},{12,140},{14,142}... | collective-permute-start | bytes 196616 | tf_op jit(solution)/shard_map/ppermute | solution.py:230
  91.5 1.4 %collective-permute-start.8 = (bf16[256,128]{1,0:T(8,128)(2,1)S(1)}, bf16[256,128]{1,0:T(8,128)(2,1)S(1)}, u32[]{:S(2)}, u32[]{:S(2)}) collective-permute-start(bf16[256,128]{1,0:T(8,128)(2,1)S(1)} %get-tuple-element.31), channel_id=1, source_target_pairs={{0,32},{2,34},{4,36},{6,38},{8,40},{10,42},{12,44},{14,46},{16,48}... | collective-permute-start | bytes 196616 | tf_op jit(solution)/shard_map/ppermute | solution.py:230
  92.9 1.8 %collective-permute-start.9 = (bf16[256,128]{1,0:T(8,128)(2,1)S(1)}, bf16[256,128]{1,0:T(8,128)(2,1)S(1)}, u32[]{:S(2)}, u32[]{:S(2)}) collective-permute-start(bf16[256,128]{1,0:T(8,128)(2,1)S(1)} %get-tuple-element.32), channel_id=1, source_target_pairs={{0,16},{2,18},{4,20},{6,22},{8,24},{10,26},{12,28},{14,30},{16,0},... | collective-permute-start | bytes 196616 | tf_op jit(solution)/shard_map/ppermute | solution.py:230
  94.7 2.1 %turned_sum.1.base_ref = f32[1536,128]{1,0:T(8,128)S(1)} custom-call(bf16[1536,1536]{1,0:T(8,128)(2,1)S(1)} %bitcast.6, bf16[1536,128]{1,0:T(8,128)(2,1)S(1)} %get-tuple-element.27.dagg_ref, f32[1536,128]{1,0:T(8,128)S(1)} %get-tuple-element.28.gself_ref), custom_call_target="tpu_custom_call" | custom-call | flops 603979776 | bytes 4718592 | tf_op jit(solution)/shard_map/turned_sum/pallas_call | solution.py:192
  96.8 1.3 %collective-permute-done.7.refs_1_ = bf16[256,128]{1,0:T(8,128)(2,1)S(1)} collective-permute-done((bf16[256,128]{1,0:T(8,128)(2,1)S(1)}, bf16[256,128]{1,0:T(8,128)(2,1)S(1)}, u32[]{:S(2)}, u32[]{:S(2)}) %collective-permute-start.7) | collective-permute-done | bytes 65568 | tf_op jit(solution)/shard_map/ppermute | solution.py:230
  98.1 2.1 %scatter_rows.1 = bf16[1536,128]{1,0:T(8,128)(2,1)} custom-call(f32[1536,128]{1,0:T(8,128)S(1)} %turned_sum.1.base_ref, s32[6,256]{1,0:T(8,128)S(1)} %bitcast.8, bf16[256,128]{1,0:T(8,128)(2,1)S(1)} %collective-permute-done.6.refs_0_, bf16[256,128]{1,0:T(8,128)(2,1)S(1)} %collective-permute-done.7.refs_1_, ...), custom_call_target="tpu_custom_call" | custom-call | flops 603979776 | bytes 1179648 | tf_op jit(solution)/shard_map/scatter_rows/pallas_call | solution.py:217
  (49 shorter events, 4.0 us)
Async XLA Ops:
  0.6 24.6 %copy-start.8 = (f32[256]{0:T(256)S(1)}, f32[256]{0:T(256)}, u32[]{:S(2)}) copy-start(f32[256]{0:T(256)} %param.14) | copy-start | bytes 3076
  1.3 1.0 copy-start.1
  2.3 22.9 %copy-start.3 = (bf16[1536,128]{1,0:T(8,128)(2,1)S(1)}, bf16[1536,128]{1,0:T(8,128)(2,1)}, u32[]{:S(2)}) copy-start(bf16[1536,128]{1,0:T(8,128)(2,1)} %refs_2_.1) | copy-start | bytes 1179652
  2.3 22.9 %copy-start.5 = (bf16[1536,256]{1,0:T(8,128)(2,1)S(1)}, bf16[1536,256]{1,0:T(8,128)(2,1)}, u32[]{:S(2)}) copy-start(bf16[1536,256]{1,0:T(8,128)(2,1)} %refs_3_.1) | copy-start | bytes 2359300
  2.3 22.9 %copy-start.6 = (bf16[128,256]{1,0:T(8,128)(2,1)S(1)}, bf16[128,256]{1,0:T(8,128)(2,1)}, u32[]{:S(2)}) copy-start(bf16[128,256]{1,0:T(8,128)(2,1)} %refs_4_.1) | copy-start | bytes 196612
  2.3 22.9 %copy-start.7 = (bf16[128,256]{1,0:T(8,128)(2,1)S(1)}, bf16[128,256]{1,0:T(8,128)(2,1)}, u32[]{:S(2)}) copy-start(bf16[128,256]{1,0:T(8,128)(2,1)} %refs_5_.1) | copy-start | bytes 196612
  3.6 13.1 %collective-permute-start = (bf16[256,128]{1,0:T(8,128)(2,1)S(1)}, bf16[256,128]{1,0:T(8,128)(2,1)S(1)}, u32[]{:S(2)}, u32[]{:S(2)}) collective-permute-start(bf16[256,128]{1,0:T(8,128)(2,1)S(1)} %get-tuple-element.20), channel_id=1, source_target_pairs={{0,128},{2,130},{4,132},{6,134},{8,136},{10,138},{12,140},{14,142}... | collective-permute-start | bytes 196616 | tf_op jit(solution)/shard_map/ppermute | solution.py:230
  11.4 13.7 %collective-permute-start.1 = (bf16[256,128]{1,0:T(8,128)(2,1)S(1)}, bf16[256,128]{1,0:T(8,128)(2,1)S(1)}, u32[]{:S(2)}, u32[]{:S(2)}) collective-permute-start(bf16[256,128]{1,0:T(8,128)(2,1)S(1)} %get-tuple-element.21), channel_id=1, source_target_pairs={{0,64},{2,66},{4,68},{6,70},{8,72},{10,74},{12,76},{14,78},{16,80}... | collective-permute-start | bytes 196616 | tf_op jit(solution)/shard_map/ppermute | solution.py:230
  12.6 12.5 %collective-permute-start.2 = (bf16[256,128]{1,0:T(8,128)(2,1)S(1)}, bf16[256,128]{1,0:T(8,128)(2,1)S(1)}, u32[]{:S(2)}, u32[]{:S(2)}) collective-permute-start(bf16[256,128]{1,0:T(8,128)(2,1)S(1)} %get-tuple-element.22), channel_id=1, source_target_pairs={{0,32},{2,34},{4,36},{6,38},{8,40},{10,42},{12,44},{14,46},{16,48}... | collective-permute-start | bytes 196616 | tf_op jit(solution)/shard_map/ppermute | solution.py:230
  13.3 11.8 %collective-permute-start.3 = (bf16[256,128]{1,0:T(8,128)(2,1)S(1)}, bf16[256,128]{1,0:T(8,128)(2,1)S(1)}, u32[]{:S(2)}, u32[]{:S(2)}) collective-permute-start(bf16[256,128]{1,0:T(8,128)(2,1)S(1)} %get-tuple-element.23), channel_id=1, source_target_pairs={{0,16},{2,18},{4,20},{6,22},{8,24},{10,26},{12,28},{14,30},{16,0},... | collective-permute-start | bytes 196616 | tf_op jit(solution)/shard_map/ppermute | solution.py:230
  16.3 8.9 %collective-permute-start.4 = (bf16[256,128]{1,0:T(8,128)(2,1)S(1)}, bf16[256,128]{1,0:T(8,128)(2,1)S(1)}, u32[]{:S(2)}, u32[]{:S(2)}) collective-permute-start(bf16[256,128]{1,0:T(8,128)(2,1)S(1)} %get-tuple-element.24), channel_id=1, source_target_pairs={{0,8},{2,10},{4,12},{6,14},{8,0},{10,2},{12,4},{14,6},{16,24},{18,... | collective-permute-start | bytes 196616 | tf_op jit(solution)/shard_map/ppermute | solution.py:230
  16.7 8.5 %collective-permute-start.5 = (bf16[256,128]{1,0:T(8,128)(2,1)S(1)}, bf16[256,128]{1,0:T(8,128)(2,1)S(1)}, u32[]{:S(2)}, u32[]{:S(2)}) collective-permute-start(bf16[256,128]{1,0:T(8,128)(2,1)S(1)} %get-tuple-element.25), channel_id=1, source_target_pairs={{0,4},{2,6},{4,0},{6,2},{8,12},{10,14},{12,8},{14,10},{16,20},{18,... | collective-permute-start | bytes 196616 | tf_op jit(solution)/shard_map/ppermute | solution.py:230
  19.4 2.3 %copy-start = (bf16[1536,1536]{1,0:T(8,128)(2,1)S(1)}, bf16[1536,1536]{1,0:T(8,128)(2,1)}, u32[]{:S(2)}) copy-start(bf16[1536,1536]{1,0:T(8,128)(2,1)} %adj_ref.3) | copy-start | bytes 14155780
  21.7 1.0 copy-start.2
  22.7 2.5 %copy-start.4 = (bf16[1,6,1536,256]{3,2,1,0:T(8,128)(2,1)S(1)}, bf16[1,6,1536,256]{3,2,1,0:T(8,128)(2,1)}, u32[]{:S(2)}) copy-start(bf16[1,6,1536,256]{3,2,1,0:T(8,128)(2,1)} %param.10) | copy-start | bytes 14155780
  25.2 69.5 %slice-start = ((s8[4718592]{0:T(1024)(128)(4,1)}), s8[4194304]{0:T(1024)(128)(4,1)S(1)}, s32[]{:S(2)}) async-start(s8[4718592]{0:T(1024)(128)(4,1)} %bitcast.5), calls=%async_computation | async-start | bytes 8388608
  25.3 69.4 %slice-start.1 = ((s8[4718592]{0:T(1024)(128)(4,1)}), s8[524288]{0:T(1024)(128)(4,1)S(1)}, s32[]{:S(2)}) async-start(s8[4718592]{0:T(1024)(128)(4,1)} %bitcast.5), calls=%async_computation.1 | async-start | bytes 1048576
  34.2 3.4 %collective-permute-start.12 = (f32[128,256]{1,0:T(8,128)S(1)}, f32[128,256]{1,0:T(8,128)S(1)}, u32[]{:S(2)}, u32[]{:S(2)}) collective-permute-start(f32[128,256]{1,0:T(8,128)S(1)} %slice_select_fusion), channel_id=1, source_target_pairs={{0,1},{1,0},{2,3},{3,2},{4,5},{5,4},{6,7},{7,6},{8,9},{9,8},{10,11... | collective-permute-start | bytes 393224 | tf_op jit(solution)/shard_map/ppermute | solution.py:230
  37.7 4.8 %collective-permute-start.13 = (f32[128,256]{1,0:T(8,128)S(1)}, f32[128,256]{1,0:T(8,128)S(1)}, u32[]{:S(2)}, u32[]{:S(2)}) collective-permute-start(f32[128,256]{1,0:T(8,128)S(1)} %select_add_fusion), channel_id=1, source_target_pairs={{0,2},{2,0},{4,6},{6,4},{8,10},{10,8},{12,14},{14,12},{16,18},{18,... | collective-permute-start | bytes 393224 | tf_op jit(solution)/shard_map/ppermute | solution.py:230
  42.5 5.4 %collective-permute-start.14 = (f32[128,256]{1,0:T(8,128)S(1)}, f32[128,256]{1,0:T(8,128)S(1)}, u32[]{:S(2)}, u32[]{:S(2)}) collective-permute-start(f32[128,256]{1,0:T(8,128)S(1)} %add.25), channel_id=1, source_target_pairs={{0,4},{2,6},{4,0},{6,2},{8,12},{10,14},{12,8},{14,10},{16,20},{18,... | collective-permute-start | bytes 393224 | tf_op jit(solution)/shard_map/ppermute | solution.py:230
  47.9 3.9 %collective-permute-start.15 = (f32[128,256]{1,0:T(8,128)S(1)}, f32[128,256]{1,0:T(8,128)S(1)}, u32[]{:S(2)}, u32[]{:S(2)}) collective-permute-start(f32[128,256]{1,0:T(8,128)S(1)} %add.26), channel_id=1, source_target_pairs={{0,8},{2,10},{4,12},{6,14},{8,0},{10,2},{12,4},{14,6},{16,24},{18,... | collective-permute-start | bytes 393224 | tf_op jit(solution)/shard_map/ppermute | solution.py:230
  51.9 5.4 %collective-permute-start.16 = (f32[128,256]{1,0:T(8,128)S(1)}, f32[128,256]{1,0:T(8,128)S(1)}, u32[]{:S(2)}, u32[]{:S(2)}) collective-permute-start(f32[128,256]{1,0:T(8,128)S(1)} %add.27), channel_id=1, source_target_pairs={{0,16},{2,18},{4,20},{6,22},{8,24},{10,26},{12,28},{14,30},{16,0},... | collective-permute-start | bytes 393224 | tf_op jit(solution)/shard_map/ppermute | solution.py:230
  57.3 4.2 %collective-permute-start.17 = (f32[128,256]{1,0:T(8,128)S(1)}, f32[128,256]{1,0:T(8,128)S(1)}, u32[]{:S(2)}, u32[]{:S(2)}) collective-permute-start(f32[128,256]{1,0:T(8,128)S(1)} %add.28), channel_id=1, source_target_pairs={{0,32},{2,34},{4,36},{6,38},{8,40},{10,42},{12,44},{14,46},{16,48}... | collective-permute-start | bytes 393224 | tf_op jit(solution)/shard_map/ppermute | solution.py:230
  61.5 6.1 %collective-permute-start.18 = (f32[128,256]{1,0:T(8,128)S(1)}, f32[128,256]{1,0:T(8,128)S(1)}, u32[]{:S(2)}, u32[]{:S(2)}) collective-permute-start(f32[128,256]{1,0:T(8,128)S(1)} %add.29), channel_id=1, source_target_pairs={{0,64},{2,66},{4,68},{6,70},{8,72},{10,74},{12,76},{14,78},{16,80}... | collective-permute-start | bytes 393224 | tf_op jit(solution)/shard_map/ppermute | solution.py:230
  67.7 9.3 %collective-permute-start.19 = (f32[128,256]{1,0:T(8,128)S(1)}, f32[128,256]{1,0:T(8,128)S(1)}, u32[]{:S(2)}, u32[]{:S(2)}) collective-permute-start(f32[128,256]{1,0:T(8,128)S(1)} %add.30), channel_id=1, source_target_pairs={{0,128},{2,130},{4,132},{6,134},{8,136},{10,138},{12,140},{14,142}... | collective-permute-start | bytes 393224 | tf_op jit(solution)/shard_map/ppermute | solution.py:230
  70.8 20.7 %collective-permute-start.10 = (bf16[256,128]{1,0:T(8,128)(2,1)S(1)}, bf16[256,128]{1,0:T(8,128)(2,1)S(1)}, u32[]{:S(2)}, u32[]{:S(2)}) collective-permute-start(bf16[256,128]{1,0:T(8,128)(2,1)S(1)} %get-tuple-element.33), channel_id=1, source_target_pairs={{0,8},{2,10},{4,12},{6,14},{8,0},{10,2},{12,4},{14,6},{16,24},{18,... | collective-permute-start | bytes 196616 | tf_op jit(solution)/shard_map/ppermute | solution.py:230
  70.8 22.1 %collective-permute-start.11 = (bf16[256,128]{1,0:T(8,128)(2,1)S(1)}, bf16[256,128]{1,0:T(8,128)(2,1)S(1)}, u32[]{:S(2)}, u32[]{:S(2)}) collective-permute-start(bf16[256,128]{1,0:T(8,128)(2,1)S(1)} %get-tuple-element.34), channel_id=1, source_target_pairs={{0,4},{2,6},{4,0},{6,2},{8,12},{10,14},{12,8},{14,10},{16,20},{18,... | collective-permute-start | bytes 196616 | tf_op jit(solution)/shard_map/ppermute | solution.py:230
  77.0 23.3 %collective-permute-start.20 = (f32[128,256]{1,0:T(8,128)S(1)}, f32[128,256]{1,0:T(8,128)S(1)}, u32[]{:S(2)}, u32[]{:S(2)}) collective-permute-start(f32[128,256]{1,0:T(8,128)S(1)} %add.31), channel_id=1, source_target_pairs={{0,1},{1,0},{2,3},{3,2},{4,5},{5,4},{6,7},{7,6},{8,9},{9,8},{10,11... | collective-permute-start | bytes 393224 | tf_op jit(solution)/shard_map/ppermute | solution.py:230
  88.4 8.5 %collective-permute-start.6 = (bf16[256,128]{1,0:T(8,128)(2,1)S(1)}, bf16[256,128]{1,0:T(8,128)(2,1)S(1)}, u32[]{:S(2)}, u32[]{:S(2)}) collective-permute-start(bf16[256,128]{1,0:T(8,128)(2,1)S(1)} %get-tuple-element.29), channel_id=1, source_target_pairs={{0,128},{2,130},{4,132},{6,134},{8,136},{10,138},{12,140},{14,142}... | collective-permute-start | bytes 196616 | tf_op jit(solution)/shard_map/ppermute | solution.py:230
  91.5 6.6 %collective-permute-start.7 = (bf16[256,128]{1,0:T(8,128)(2,1)S(1)}, bf16[256,128]{1,0:T(8,128)(2,1)S(1)}, u32[]{:S(2)}, u32[]{:S(2)}) collective-permute-start(bf16[256,128]{1,0:T(8,128)(2,1)S(1)} %get-tuple-element.30), channel_id=1, source_target_pairs={{0,64},{2,66},{4,68},{6,70},{8,72},{10,74},{12,76},{14,78},{16,80}... | collective-permute-start | bytes 196616 | tf_op jit(solution)/shard_map/ppermute | solution.py:230
  91.5 6.6 %collective-permute-start.8 = (bf16[256,128]{1,0:T(8,128)(2,1)S(1)}, bf16[256,128]{1,0:T(8,128)(2,1)S(1)}, u32[]{:S(2)}, u32[]{:S(2)}) collective-permute-start(bf16[256,128]{1,0:T(8,128)(2,1)S(1)} %get-tuple-element.31), channel_id=1, source_target_pairs={{0,32},{2,34},{4,36},{6,38},{8,40},{10,42},{12,44},{14,46},{16,48}... | collective-permute-start | bytes 196616 | tf_op jit(solution)/shard_map/ppermute | solution.py:230
  92.9 5.2 %collective-permute-start.9 = (bf16[256,128]{1,0:T(8,128)(2,1)S(1)}, bf16[256,128]{1,0:T(8,128)(2,1)S(1)}, u32[]{:S(2)}, u32[]{:S(2)}) collective-permute-start(bf16[256,128]{1,0:T(8,128)(2,1)S(1)} %get-tuple-element.32), channel_id=1, source_target_pairs={{0,16},{2,18},{4,20},{6,22},{8,24},{10,26},{12,28},{14,30},{16,0},... | collective-permute-start | bytes 196616 | tf_op jit(solution)/shard_map/ppermute | solution.py:230

commit v2 on v0

v2 whole, which is shorter than its diff:
```python
import functools
import math

import jax
import jax.numpy as jnp
from jax import lax
from jax.experimental import pallas as pl
from jax.experimental.pallas import tpu as pltpu
from jax.sharding import Mesh
from jax.sharding import PartitionSpec as P

F32 = jnp.float32
BF16 = jnp.bfloat16
BLOCK = 384
SIDE = 4
AXES = ("z", "y", "x", "core")
PLANE = AXES[1:]


def dot(left, right, left_dim=1, right_dim=0):
    return lax.dot_general(
        left, right, (((left_dim,), (right_dim,)), ((), ())), preferred_element_type=F32
    )


def cost(flops, nbytes):
    return pl.CostEstimate(flops=int(flops), bytes_accessed=int(nbytes), transcendentals=0)


def params(mib):
    return pltpu.CompilerParams(vmem_limit_bytes=mib * 1024 * 1024)


def one_hot(index_row, count):
    places = lax.broadcasted_iota(jnp.int32, (count, index_row.shape[1]), 0)
    return (places == index_row).astype(F32).astype(BF16)


def in_hbm(array):
    return pltpu.with_memory_space_constraint(array, pltpu.HBM)


ANY = pl.BlockSpec(memory_space=pl.ANY)
VMEM = pl.BlockSpec(memory_space=pltpu.VMEM)
DMA = pltpu.SemaphoreType.DMA


def gather_kernel(rounds, feats_hbm, index_hbm, adj_hbm, *refs):
    out_refs, (wide_ref, adj_ref, index_ref, sems) = refs[:rounds], refs[rounds:]
    rows, width = feats_hbm.shape
    copies = [
        pltpu.make_async_copy(index_hbm, index_ref, sems.at[0]),
        pltpu.make_async_copy(feats_hbm, wide_ref.at[:, pl.ds(0, width)], sems.at[1]),
        pltpu.make_async_copy(adj_hbm, adj_ref, sems.at[2]),
    ]
    for copy in copies:
        copy.start()
    wide_ref[:, width:] = jnp.ones((rows, width), BF16)
    copies[0].wait()
    copies[1].wait()
    turned = wide_ref[:, :width].T
    for turn, out_ref in enumerate(out_refs):
        out_ref[...] = dot(turned, one_hot(index_ref[turn], rows)).T.astype(BF16)
    copies[2].wait()


def gather_rows(feats, index_lists, local_adj):
    rounds, _, picks = index_lists.shape
    rows, width = feats.shape
    results = pl.pallas_call(
        functools.partial(gather_kernel, rounds),
        in_specs=[ANY, ANY, ANY],
        out_specs=[VMEM] * (rounds + 2),
        out_shape=[jax.ShapeDtypeStruct((picks, width), BF16)] * rounds
        + [pltpu.VMEM((rows, 2 * width), BF16), pltpu.VMEM(local_adj.shape, BF16)],
        scratch_shapes=[pltpu.VMEM(index_lists.shape, jnp.int32), DMA((3,))],
        compiler_params=params(24),
        cost_estimate=cost(2 * rows * picks * width * rounds, rows * width * 2),
        name="gather_rows",
    )(in_hbm(feats), in_hbm(index_lists), in_hbm(local_adj))
    return results[:rounds], results[rounds], results[rounds + 1]


def local_kernel(adj_ref, wide_ref, out_ref):
    for start in range(0, adj_ref.shape[0], BLOCK):
        span = slice(start, start + BLOCK)
        out_ref[span, :] = dot(adj_ref[span, :], wide_ref[...])


def local_sum(local_adj, wide):
    rows = local_adj.shape[0]
    return pl.pallas_call(
        local_kernel,
        out_shape=jax.ShapeDtypeStruct(wide.shape, F32),
        compiler_params=params(16),
        cost_estimate=cost(2 * rows * rows * wide.shape[1], rows * rows * 2),
        name="local_sum",
    )(local_adj, wide)


def middle_kernel(rounds, *refs):
    local_ref, bnd_ref, feats_ref, cot_ref, self_ref, neigh_ref, bias_ref = refs[:7]
    recv_refs = refs[7 : 7 + rounds]
    out_hbm, dagg_ref, gself_ref, gw_hbm = refs[7 + rounds : 11 + rounds]
    back_refs = refs[11 + rounds : 11 + 2 * rounds]
    wide_ref, both_ref, dpre_ref, inverse_ref, out_ref, gw_ref, sems = refs[11 + 2 * rounds :]
    rows, width = dagg_ref.shape
    bnd = bnd_ref.shape[2]
    spans = [slice(start, start + BLOCK) for start in range(0, rows, BLOCK)]

    for turn in range(rounds):
        span = slice(turn * bnd, (turn + 1) * bnd)
        wide_ref[span, :width] = recv_refs[turn][...]
        wide_ref[span, width:] = jnp.ones_like(recv_refs[turn])
    both_ref[:, :width] = feats_ref[:, :width]
    for span in spans:
        tiles = jnp.concatenate([bnd_ref[turn, span, :] for turn in range(rounds)], axis=1)
        total = local_ref[span, :] + dot(tiles, wide_ref[...])
        inverse = 1.0 / (1.0 + total[:, width:])
        inverse_ref[span, :] = inverse
        both_ref[span, width:] = (total[:, :width] * inverse).astype(BF16)

    weights = jnp.concatenate([self_ref[...], neigh_ref[...]], axis=0)
    for span in spans:
        pre = dot(both_ref[span, :], weights) + bias_ref[...]
        sig = 0.5 + 0.5 * jnp.tanh(0.5 * pre)
        out = pre * sig
        out_ref[span, :] = out.astype(BF16)
        slope = sig * (1.0 + (pre - out))
        dpre_ref[span, :] = (cot_ref[span, :].astype(F32) * slope).astype(BF16)

    gw = dot(both_ref[...], dpre_ref[...], 0, 0).astype(BF16)
    for half in range(gw.shape[1] // width):
        gw_ref[half] = gw[:, half * width : (half + 1) * width]
    gw_copy = pltpu.make_async_copy(gw_ref, gw_hbm, sems.at[0])
    gw_copy.start()
    out_copy = pltpu.make_async_copy(out_ref, out_hbm, sems.at[1])
    out_copy.start()

    for span in spans:
        grads = dot(dpre_ref[span, :], weights, 1, 1)
        gself_ref[span, :] = grads[:, :width]
        dagg_ref[span, :] = (grads[:, width:] * inverse_ref[span, :]).astype(BF16)

    turned = dagg_ref[...].T
    for turn in range(rounds):
        back_refs[turn][...] = dot(turned, bnd_ref[turn]).T.astype(BF16)
    gw_copy.wait()
    out_copy.wait()


def middle(local, bnd_tiles, wide, cotangent, w_self, w_neigh, bias, incoming):
    rounds, rows, bnd = bnd_tiles.shape
    width, hidden = w_self.shape
    results = pl.pallas_call(
        functools.partial(middle_kernel, rounds),
        in_specs=[VMEM] * (7 + rounds),
        out_specs=[ANY, VMEM, VMEM, ANY] + [VMEM] * rounds,
        out_shape=[
            pltpu.HBM((rows, hidden), BF16),
            jax.ShapeDtypeStruct((rows, width), BF16),
            jax.ShapeDtypeStruct((rows, width), F32),
            pltpu.HBM((hidden // width, 2 * width, width), BF16),
        ]
        + [jax.ShapeDtypeStruct((bnd, width), BF16)] * rounds,
        scratch_shapes=[
            pltpu.VMEM((rounds * bnd, 2 * width), BF16),
            pltpu.VMEM((rows, 2 * width), BF16),
            pltpu.VMEM((rows, hidden), BF16),
            pltpu.VMEM((rows, width), F32),
            pltpu.VMEM((rows, hidden), BF16),
            pltpu.VMEM((hidden // width, 2 * width, width), BF16),
            DMA((2,)),
        ],
        compiler_params=params(32),
        cost_estimate=cost(8 * rounds * rows * bnd * width, rounds * rows * bnd * 2),
        name="middle",
    )(
        local,
        bnd_tiles,
        wide,
        cotangent,
        w_self,
        w_neigh,
        bias.reshape(1, hidden),
        *incoming,
    )
    return results[0], results[1], results[2], results[3], results[4:]


def turned_kernel(adj_ref, dagg_ref, gself_ref, out_ref):
    out_ref[...] = gself_ref[...] + dot(dagg_ref[...].T, adj_ref[...]).T


def turned_sum(local_adj, dagg, gself):
    rows, width = dagg.shape
    return pl.pallas_call(
        turned_kernel,
        out_shape=jax.ShapeDtypeStruct((rows, width), F32),
        compiler_params=params(32),
        cost_estimate=cost(2 * rows * rows * width, rows * rows * 2),
        name="turned_sum",
    )(local_adj, dagg, gself)


def spread_kernel(scale, parts_ref, out_hbm, wide_ref, sem):
    total = parts_ref[0].astype(F32)
    for number in range(1, parts_ref.shape[0]):
        total = total + parts_ref[number].astype(F32)
    total = (total * scale).astype(wide_ref.dtype)
    for number in range(wide_ref.shape[0]):
        wide_ref[number] = total
    copy = pltpu.make_async_copy(wide_ref, out_hbm, sem)
    copy.start()
    copy.wait()


def sum_and_spread(parts, copies, dtype, scale):
    shape = (copies,) + parts.shape[1:]
    return pl.pallas_call(
        functools.partial(spread_kernel, scale),
        in_specs=[VMEM],
        out_specs=ANY,
        out_shape=pltpu.HBM(shape, dtype),
        scratch_shapes=[pltpu.VMEM(shape, dtype), DMA(())],
        compiler_params=params(16),
        name="sum_and_spread",
    )(parts)


def scatter_kernel(base_ref, index_ref, *refs):
    total = base_ref[...]
    for turn, back_ref in enumerate(refs[:-1]):
        total = total + dot(one_hot(index_ref[turn], base_ref.shape[0]), back_ref[...])
    refs[-1][...] = total.astype(refs[-1].dtype)


def scatter_rows(base, index_lists, returned):
    rounds, _, picks = index_lists.shape
    rows, width = base.shape
    return pl.pallas_call(
        scatter_kernel,
        out_shape=jax.ShapeDtypeStruct((rows, width), BF16),
        compiler_params=params(32),
        cost_estimate=cost(2 * rows * picks * width * rounds, rows * width * 6),
        name="scatter_rows",
    )(base, index_lists, *returned)


def swapped(block, bit):
    count = math.prod(lax.axis_size(axis) for axis in AXES)
    return lax.ppermute(block, AXES, [(low, low ^ 1 << bit) for low in range(count)])


def after(value, *others):
    return lax.optimization_barrier((value, *others))[0]


def per_device(feats, local_adj, bnd_adj, send_index, w_self, w_neigh, bias, cotangent):
    chips = math.prod(lax.axis_size(axis) for axis in AXES[:-1])
    cores = lax.axis_size(AXES[-1])
    bits = chips.bit_length() - 1
    bnd_tiles = bnd_adj[0]
    rounds, _, picks = bnd_tiles.shape
    index_lists = send_index.reshape(rounds, 1, -1)
    rows, width = feats.shape

    def partner(turn):
        return bits - turn % bits

    outgoing, wide, near_adj = gather_rows(feats, index_lists, local_adj)
    incoming = [swapped(outgoing[turn], partner(turn)) for turn in range(rounds)]
    local = local_sum(near_adj, wide)
    output, dagg, gself, gw, back = middle(
        local, bnd_tiles, wide, cotangent, w_self, w_neigh, bias, incoming
    )
    base = turned_sum(local_adj, dagg, gself)

    plane = math.prod(lax.axis_size(axis) for axis in PLANE)
    planes = chips * cores // plane
    pieces = gw.reshape(plane, -1, width)
    pieces = lax.all_to_all(pieces, PLANE, 0, 0, tiled=True)
    near = [turn for turn in range(rounds) if partner(turn) < plane.bit_length() - 1]
    far = [turn for turn in range(rounds) if turn not in near]
    returned = {turn: swapped(back[turn], partner(turn)) for turn in far}
    pieces = sum_and_spread(pieces, planes, F32, 1.0)
    pieces = after(pieces, *[returned[turn] for turn in far])
    pieces = lax.all_to_all(pieces, AXES[:1], 0, 0, tiled=True)
    returned |= {turn: swapped(back[turn], partner(turn)) for turn in near}
    scale = 1.0 / math.sqrt(rows * chips * cores)
    pieces = sum_and_spread(pieces, plane, BF16, scale)
    pieces = after(pieces, *[returned[turn] for turn in near])
    pieces = lax.all_to_all(pieces, PLANE, 0, 0, tiled=True)
    grad_feats = scatter_rows(base, index_lists, [returned[turn] for turn in range(rounds)])
    sums = jnp.concatenate([*pieces.reshape(gw.shape)], axis=1).astype(F32)
    return output, grad_feats, sums[:width], sums[width:]


def solution(mesh):
    chips = mesh.shape["dom"] // SIDE**2
    shape = (chips, SIDE, SIDE, mesh.shape["grp"])
    mesh = Mesh(mesh.devices.reshape(shape), AXES)
    placed = (
        P(AXES, None),
        P(AXES, None),
        P(AXES, None, None, None),
        P(AXES, None, None),
        P(),
        P(),
        P(),
        P(AXES, None),
    )
    return jax.shard_map(
        per_device,
        mesh=mesh,
        in_specs=placed,
        out_specs=(P(AXES, None), P(AXES, None), P(), P()),
        check_vma=False,
    )
```

time: 319 us -> 75.7 us (0.24)
  waiting for transfers between devices: 236 us -> 9.33 us
  starting transfers between devices: 20.1 us -> 49.7 us
  other arithmetic: 20.9 us -> 0.02 us
  matrix products: 18.6 us -> 0 us
  between operations: 14.6 us -> 0.86 us
  Pallas kernels: 0 us -> 12.4 us
  local copies, waits for them, and re-layouts: 8.3 us -> 3.1 us
    psum x1 -> x0, waiting for transfers between devices: 232 us -> none  [per_device(): lax.psum((contract_rows(feats, grad_pre), contract_rows(aggregated, grad_...]
    all_to_all x0 -> x3, starting transfers between devices: none -> 21.6 us  [the longest x2 18.3 us: per_device(): pieces = lax.all_to_all(pieces, PLANE, 0, 0, tiled=True)]
    dot_general x20 -> x0, matrix products: 18.6 us -> none  [the longest x9 8.64 us: contract_rows(): lax.dot_general(left, right, (((0,), (0,)), ((), ())), preferred_element_...]
    scatter-add x6 -> x0, other arithmetic: 13.9 us -> none  [per_device(): grad_feats.at[index_lists[round_index]]]
    pallas_call x0 -> x7, Pallas kernels: none -> 12.4 us  [the longest x1 4.07 us: middle(): pl.pallas_call(functools.partial(middle_kernel, rounds), in_specs=[VMEM]...]
    ppermute x12, starting transfers between devices: 20 us -> 28.1 us  [swapped(): lax.ppermute(block, AXES, [(low, low ^ 1 << bit) for low in range(count)])]
    gather x6 -> x0, local copies, waits for them, and re-layouts: 5.13 us -> none  [per_device(): jnp.take(feats, index_lists[round_index], axis=0)]
    all_to_all x0 -> x3, waiting for transfers between devices: none -> 4.79 us  [the longest x2 3.56 us: per_device(): pieces = lax.all_to_all(pieces, PLANE, 0, 0, tiled=True)]
  transfers between devices with their start and end apart: 13 -> 15, of which waited for: 2 -> 6; matrix products, arithmetic and copies ran while one was open for 10% -> 0% of each run, Pallas kernels for 0% -> 8%
where the time goes in v2:
time: 75.7 us; the launch traced here: 75.3 us
  starting transfers between devices  49.7 us (66%)
  Pallas kernels  12.4 us (16%)
  waiting for transfers between devices  9.33 us (12%)
  local copies, waits for them, and re-layouts  3.1 us (4%)
  between operations  0.86 us (1%)
    ppermute x12, starting transfers between devices, swapped(): lax.ppermute(block, AXES, [(low, low ^ 1 << bit) for low in range(count)])  28.1 us
    all_to_all x2, starting transfers between devices, per_device(): pieces = lax.all_to_all(pieces, PLANE, 0, 0, tiled=True)  18.3 us
    ppermute x12, waiting for transfers between devices, swapped(): lax.ppermute(block, AXES, [(low, low ^ 1 << bit) for low in range(count)])  4.54 us
    pallas_call x1, Pallas kernels, middle(): pl.pallas_call(functools.partial(middle_kernel, rounds), in_specs=[VMEM]...  4.07 us
    all_to_all x2, waiting for transfers between devices, per_device(): pieces = lax.all_to_all(pieces, PLANE, 0, 0, tiled=True)  3.56 us
    all_to_all x1, starting transfers between devices, per_device(): pieces = lax.all_to_all(pieces, AXES[:1], 0, 0, tiled=True)  3.35 us
    pallas_call x1, Pallas kernels, gather_rows(): pl.pallas_call(functools.partial(gather_kernel, rounds), in_specs=[ANY, A...  2.51 us
    unnamed x14, local copies, waits for them, and re-layouts  2.37 us
  transfers between devices with their start and end apart: 15, of which 6 were waited for; matrix products, arithmetic and copies ran while one was open for 0% of the time, Pallas kernels for 8%

profile of v2, /device:TPU:1, one launch (start us, length us, event | category | flops | bytes accessed | tf_op | source)
XLA Modules:
  0.0 75.3 jit_solution(5560959430683668190)
XLA Ops:
  0.6 2.5 %gather_rows.1 = (bf16[256,128]{1,0:T(8,128)(2,1)S(1)}, bf16[256,128]{1,0:T(8,128)(2,1)S(1)}, bf16[256,128]{1,0:T(8,128)(2,1)S(1)}, bf16[256,128]{1,0:T(8,128)(2...) custom-call(bf16[1536,128]{1,0:T(8,128)(2,1)} %feats_hbm.1, ...), custom_call_target="tpu_custom_call" | custom-call | flops 603979776 | bytes 393216 | tf_op jit(solution)/shard_map/gather_rows/pallas_call | solution.py:70
  3.1 0.0 copy-start.2
  3.2 0.0 copy-start.3
  3.2 0.0 copy-start.4
  3.2 7.8 %collective-permute-start = (bf16[256,128]{1,0:T(8,128)(2,1)S(1)}, bf16[256,128]{1,0:T(8,128)(2,1)S(1)}, u32[]{:S(2)}, u32[]{:S(2)}) collective-permute-start(bf16[256,128]{1,0:T(8,128)(2,1)S(1)} %get-tuple-element.26), channel_id=1, source_target_pairs={{0,128},{1,129},{2,130},{3,131},{4,132},{5,133},{6,134},{7,135},{8... | collective-permute-start | bytes 196616 | tf_op jit(solution)/shard_map/ppermute | solution.py:252
  11.0 1.2 %collective-permute-start.1 = (bf16[256,128]{1,0:T(8,128)(2,1)S(1)}, bf16[256,128]{1,0:T(8,128)(2,1)S(1)}, u32[]{:S(2)}, u32[]{:S(2)}) collective-permute-start(bf16[256,128]{1,0:T(8,128)(2,1)S(1)} %get-tuple-element.27), channel_id=1, source_target_pairs={{0,64},{1,65},{2,66},{3,67},{4,68},{5,69},{6,70},{7,71},{8,72},{9,... | collective-permute-start | bytes 196616 | tf_op jit(solution)/shard_map/ppermute | solution.py:252
  12.2 0.7 collective-permute-start.2
  13.0 2.9 %collective-permute-start.3 = (bf16[256,128]{1,0:T(8,128)(2,1)S(1)}, bf16[256,128]{1,0:T(8,128)(2,1)S(1)}, u32[]{:S(2)}, u32[]{:S(2)}) collective-permute-start(bf16[256,128]{1,0:T(8,128)(2,1)S(1)} %get-tuple-element.29), channel_id=1, source_target_pairs={{0,16},{1,17},{2,18},{3,19},{4,20},{5,21},{6,22},{7,23},{8,24},{9,... | collective-permute-start | bytes 196616 | tf_op jit(solution)/shard_map/ppermute | solution.py:252
  15.9 0.4 collective-permute-start.4
  16.3 2.7 %collective-permute-start.5 = (bf16[256,128]{1,0:T(8,128)(2,1)S(1)}, bf16[256,128]{1,0:T(8,128)(2,1)S(1)}, u32[]{:S(2)}, u32[]{:S(2)}) collective-permute-start(bf16[256,128]{1,0:T(8,128)(2,1)S(1)} %get-tuple-element.31), channel_id=1, source_target_pairs={{0,4},{1,5},{2,6},{3,7},{4,0},{5,1},{6,2},{7,3},{8,12},{9,13},{10,... | collective-permute-start | bytes 196616 | tf_op jit(solution)/shard_map/ppermute | solution.py:252
  19.0 1.4 %local_sum.1.refs_0_ = f32[1536,256]{1,0:T(8,128)S(1)} custom-call(bf16[1536,1536]{1,0:T(8,128)(2,1)S(1)} %get-tuple-element.24.adj_ref, bf16[1536,256]{1,0:T(8,128)(2,1)S(1)} %get-tuple-element.25.wide_ref.refs_2_), custom_call_target="tpu_custom_call" | custom-call | flops 1207959552 | bytes 4718592 | tf_op jit(solution)/shard_map/local_sum/pallas_call | solution.py:92
  20.4 0.5 collective-permute-done.5.refs_12_
  20.9 4.1 %middle.1 = (bf16[1536,256]{1,0:T(8,128)(2,1)}, bf16[1536,128]{1,0:T(8,128)(2,1)S(1)}, f32[1536,128]{1,0:T(8,128)S(1)}, bf16[2,256,128]{2,1,0:T(8,128)(2,1)}, bf...) custom-call(f32[1536,256]{1,0:T(8,128)S(1)} %local_sum.1.refs_0_, ...), custom_call_target="tpu_custom_call" | custom-call | flops 2415919104 | bytes 4718592 | tf_op jit(solution)/shard_map/middle/pallas_call | solution.py:155
  25.0 9.0 %all-to-all-start = ((bf16[32,16,128]{2,1,0:T(8,128)(2,1)}), bf16[32,16,128]{2,1,0:T(8,128)(2,1)S(1)}, u32[]{:S(2)}, u32[]{:S(2)}) async-start(bf16[32,16,128]{2,1,0:T(8,128)(2,1)} %bitcast.12), calls=%async_computation | async-start | bytes 262144 | tf_op jit(solution)/shard_map/all_to_all | solution.py:282
  34.0 4.1 %collective-permute-start.6 = (bf16[256,128]{1,0:T(8,128)(2,1)S(1)}, bf16[256,128]{1,0:T(8,128)(2,1)S(1)}, u32[]{:S(2)}, u32[]{:S(2)}) collective-permute-start(bf16[256,128]{1,0:T(8,128)(2,1)S(1)} %get-tuple-element.35), channel_id=1, source_target_pairs={{0,128},{1,129},{2,130},{3,131},{4,132},{5,133},{6,134},{7,135},{8... | collective-permute-start | bytes 196616 | tf_op jit(solution)/shard_map/ppermute | solution.py:252
  38.1 2.2 %collective-permute-start.7 = (bf16[256,128]{1,0:T(8,128)(2,1)S(1)}, bf16[256,128]{1,0:T(8,128)(2,1)S(1)}, u32[]{:S(2)}, u32[]{:S(2)}) collective-permute-start(bf16[256,128]{1,0:T(8,128)(2,1)S(1)} %get-tuple-element.36), channel_id=1, source_target_pairs={{0,64},{1,65},{2,66},{3,67},{4,68},{5,69},{6,70},{7,71},{8,72},{9,... | collective-permute-start | bytes 196616 | tf_op jit(solution)/shard_map/ppermute | solution.py:252
  40.3 1.4 %all-to-all-done.parts_ref = bf16[32,16,128]{2,1,0:T(8,128)(2,1)S(1)} async-done(((bf16[32,16,128]{2,1,0:T(8,128)(2,1)}), bf16[32,16,128]{2,1,0:T(8,128)(2,1)S(1)}, u32[]{:S(2)}, u32[]{:S(2)}) %all-to-all-start) | async-done | bytes 131104 | tf_op jit(solution)/shard_map/all_to_all | solution.py:282
  41.6 0.7 sum_and_spread.2
  42.3 3.8 %collective-permute-done.7.refs_1_ = bf16[256,128]{1,0:T(8,128)(2,1)S(1)} collective-permute-done((bf16[256,128]{1,0:T(8,128)(2,1)S(1)}, bf16[256,128]{1,0:T(8,128)(2,1)S(1)}, u32[]{:S(2)}, u32[]{:S(2)}) %collective-permute-start.7) | collective-permute-done | bytes 65568 | tf_op jit(solution)/shard_map/ppermute | solution.py:252
  46.1 3.4 %all-to-all-start.1 = ((f32[8,16,128]{2,1,0:T(8,128)}), f32[8,16,128]{2,1,0:T(8,128)S(1)}, u32[]{:S(2)}, u32[]{:S(2)}) async-start(f32[8,16,128]{2,1,0:T(8,128)} %sum_and_spread.2), calls=%async_computation.1 | async-start | bytes 131072 | tf_op jit(solution)/shard_map/all_to_all | solution.py:288
  49.5 2.9 %collective-permute-start.9 = (bf16[256,128]{1,0:T(8,128)(2,1)S(1)}, bf16[256,128]{1,0:T(8,128)(2,1)S(1)}, u32[]{:S(2)}, u32[]{:S(2)}) collective-permute-start(bf16[256,128]{1,0:T(8,128)(2,1)S(1)} %get-tuple-element.38), channel_id=1, source_target_pairs={{0,16},{1,17},{2,18},{3,19},{4,20},{5,21},{6,22},{7,23},{8,24},{9,... | collective-permute-start | bytes 196616 | tf_op jit(solution)/shard_map/ppermute | solution.py:252
  52.4 0.3 collective-permute-start.10
  52.7 2.7 %collective-permute-start.11 = (bf16[256,128]{1,0:T(8,128)(2,1)S(1)}, bf16[256,128]{1,0:T(8,128)(2,1)S(1)}, u32[]{:S(2)}, u32[]{:S(2)}) collective-permute-start(bf16[256,128]{1,0:T(8,128)(2,1)S(1)} %get-tuple-element.40), channel_id=1, source_target_pairs={{0,4},{1,5},{2,6},{3,7},{4,0},{5,1},{6,2},{7,3},{8,12},{9,13},{10,... | collective-permute-start | bytes 196616 | tf_op jit(solution)/shard_map/ppermute | solution.py:252
  55.5 1.2 %all-to-all-done.1.parts_ref = f32[8,16,128]{2,1,0:T(8,128)S(1)} async-done(((f32[8,16,128]{2,1,0:T(8,128)}), f32[8,16,128]{2,1,0:T(8,128)S(1)}, u32[]{:S(2)}, u32[]{:S(2)}) %all-to-all-start.1) | async-done | bytes 65568 | tf_op jit(solution)/shard_map/all_to_all | solution.py:288
  56.7 0.7 sum_and_spread.3
  57.4 0.3 collective-permute-done.11.refs_5_
  57.7 9.3 %all-to-all-start.2 = ((bf16[32,16,128]{2,1,0:T(8,128)(2,1)}), bf16[32,16,128]{2,1,0:T(8,128)(2,1)S(1)}, u32[]{:S(2)}, u32[]{:S(2)}) async-start(bf16[32,16,128]{2,1,0:T(8,128)(2,1)} %sum_and_spread.3), calls=%async_computation.2 | async-start | bytes 262144 | tf_op jit(solution)/shard_map/all_to_all | solution.py:293
  67.0 2.3 %copy-done = bf16[1536,1536]{1,0:T(8,128)(2,1)S(1)} copy-done((bf16[1536,1536]{1,0:T(8,128)(2,1)S(1)}, bf16[1536,1536]{1,0:T(8,128)(2,1)}, u32[]{:S(2)}) %copy-start) | copy-done | bytes 4718616
  69.3 0.9 %turned_sum.1.base_ref = f32[1536,128]{1,0:T(8,128)S(1)} custom-call(bf16[1536,1536]{1,0:T(8,128)(2,1)S(1)} %copy-done, bf16[1536,128]{1,0:T(8,128)(2,1)S(1)} %get-tuple-element.33.dagg_ref, f32[1536,128]{1,0:T(8,128)S(1)} %get-tuple-element.34.gself_ref), custom_call_target="tpu_custom_call" | custom-call | flops 603979776 | bytes 4718592 | tf_op jit(solution)/shard_map/turned_sum/pallas_call | solution.py:197
  70.2 2.1 %scatter_rows.1 = bf16[1536,128]{1,0:T(8,128)(2,1)} custom-call(f32[1536,128]{1,0:T(8,128)S(1)} %turned_sum.1.base_ref, s32[6,1,256]{2,1,0:T(1,128)S(1)} %bitcast.7, bf16[256,128]{1,0:T(8,128)(2,1)S(1)} %collective-permute-done.6.refs_0_, bf16[256,128]{1,0:T(8,128)(2,1)S(1)} %collective-permute-done.7.refs_1_, ...), custom_call_target="tpu_custom_call" | custom-call | flops 603979776 | bytes 1179648 | tf_op jit(solution)/shard_map/scatter_rows/pallas_call | solution.py:241
  72.4 2.2 %all-to-all-done.2 = bf16[32,16,128]{2,1,0:T(8,128)(2,1)S(1)} async-done(((bf16[32,16,128]{2,1,0:T(8,128)(2,1)}), bf16[32,16,128]{2,1,0:T(8,128)(2,1)S(1)}, u32[]{:S(2)}, u32[]{:S(2)}) %all-to-all-start.2) | async-done | bytes 131104 | tf_op jit(solution)/shard_map/all_to_all | solution.py:293
  74.6 0.7 fusion
  (22 shorter events, 0.1 us)
Async XLA Ops:
  3.1 17.8 %copy-start.2 = (bf16[1,6,1536,256]{3,2,1,0:T(8,128)(2,1)S(1)}, bf16[1,6,1536,256]{3,2,1,0:T(8,128)(2,1)}, u32[]{:S(2)}) copy-start(bf16[1,6,1536,256]{3,2,1,0:T(8,128)(2,1)} %param.10) | copy-start | bytes 14155780
  3.2 17.7 %copy-start.3 = (bf16[1536,256]{1,0:T(8,128)(2,1)S(1)}, bf16[1536,256]{1,0:T(8,128)(2,1)}, u32[]{:S(2)}) copy-start(bf16[1536,256]{1,0:T(8,128)(2,1)} %refs_3_.1) | copy-start | bytes 2359300
  3.2 17.7 %copy-start.4 = (bf16[128,256]{1,0:T(8,128)(2,1)S(1)}, bf16[128,256]{1,0:T(8,128)(2,1)}, u32[]{:S(2)}) copy-start(bf16[128,256]{1,0:T(8,128)(2,1)} %refs_4_.1) | copy-start | bytes 196612
  3.2 17.7 %copy-start.5 = (bf16[128,256]{1,0:T(8,128)(2,1)S(1)}, bf16[128,256]{1,0:T(8,128)(2,1)}, u32[]{:S(2)}) copy-start(bf16[128,256]{1,0:T(8,128)(2,1)} %refs_5_.1) | copy-start | bytes 196612
  3.2 17.7 %copy-start.6 = (f32[256]{0:T(256)S(1)}, f32[256]{0:T(256)}, u32[]{:S(2)}) copy-start(f32[256]{0:T(256)} %param.14) | copy-start | bytes 3076
  3.2 13.1 %collective-permute-start = (bf16[256,128]{1,0:T(8,128)(2,1)S(1)}, bf16[256,128]{1,0:T(8,128)(2,1)S(1)}, u32[]{:S(2)}, u32[]{:S(2)}) collective-permute-start(bf16[256,128]{1,0:T(8,128)(2,1)S(1)} %get-tuple-element.26), channel_id=1, source_target_pairs={{0,128},{1,129},{2,130},{3,131},{4,132},{5,133},{6,134},{7,135},{8... | collective-permute-start | bytes 196616 | tf_op jit(solution)/shard_map/ppermute | solution.py:252
  11.0 9.4 %collective-permute-start.1 = (bf16[256,128]{1,0:T(8,128)(2,1)S(1)}, bf16[256,128]{1,0:T(8,128)(2,1)S(1)}, u32[]{:S(2)}, u32[]{:S(2)}) collective-permute-start(bf16[256,128]{1,0:T(8,128)(2,1)S(1)} %get-tuple-element.27), channel_id=1, source_target_pairs={{0,64},{1,65},{2,66},{3,67},{4,68},{5,69},{6,70},{7,71},{8,72},{9,... | collective-permute-start | bytes 196616 | tf_op jit(solution)/shard_map/ppermute | solution.py:252
  12.2 8.2 %collective-permute-start.2 = (bf16[256,128]{1,0:T(8,128)(2,1)S(1)}, bf16[256,128]{1,0:T(8,128)(2,1)S(1)}, u32[]{:S(2)}, u32[]{:S(2)}) collective-permute-start(bf16[256,128]{1,0:T(8,128)(2,1)S(1)} %get-tuple-element.28), channel_id=1, source_target_pairs={{0,32},{1,33},{2,34},{3,35},{4,36},{5,37},{6,38},{7,39},{8,40},{9,... | collective-permute-start | bytes 196616 | tf_op jit(solution)/shard_map/ppermute | solution.py:252
  13.0 7.5 %collective-permute-start.3 = (bf16[256,128]{1,0:T(8,128)(2,1)S(1)}, bf16[256,128]{1,0:T(8,128)(2,1)S(1)}, u32[]{:S(2)}, u32[]{:S(2)}) collective-permute-start(bf16[256,128]{1,0:T(8,128)(2,1)S(1)} %get-tuple-element.29), channel_id=1, source_target_pairs={{0,16},{1,17},{2,18},{3,19},{4,20},{5,21},{6,22},{7,23},{8,24},{9,... | collective-permute-start | bytes 196616 | tf_op jit(solution)/shard_map/ppermute | solution.py:252
  15.9 4.6 %collective-permute-start.4 = (bf16[256,128]{1,0:T(8,128)(2,1)S(1)}, bf16[256,128]{1,0:T(8,128)(2,1)S(1)}, u32[]{:S(2)}, u32[]{:S(2)}) collective-permute-start(bf16[256,128]{1,0:T(8,128)(2,1)S(1)} %get-tuple-element.30), channel_id=1, source_target_pairs={{0,8},{1,9},{2,10},{3,11},{4,12},{5,13},{6,14},{7,15},{8,0},{9,1},... | collective-permute-start | bytes 196616 | tf_op jit(solution)/shard_map/ppermute | solution.py:252
  16.3 4.6 %collective-permute-start.5 = (bf16[256,128]{1,0:T(8,128)(2,1)S(1)}, bf16[256,128]{1,0:T(8,128)(2,1)S(1)}, u32[]{:S(2)}, u32[]{:S(2)}) collective-permute-start(bf16[256,128]{1,0:T(8,128)(2,1)S(1)} %get-tuple-element.31), channel_id=1, source_target_pairs={{0,4},{1,5},{2,6},{3,7},{4,0},{5,1},{6,2},{7,3},{8,12},{9,13},{10,... | collective-permute-start | bytes 196616 | tf_op jit(solution)/shard_map/ppermute | solution.py:252
  25.0 45.2 %copy-start.1 = (s32[1,6,256]{2,0,1:T(1,128)S(1)}, s32[1,6,256]{2,0,1:T(1,128)}, u32[]{:S(2)}) copy-start(s32[1,6,256]{2,0,1:T(1,128)} %param.11) | copy-start | bytes 18436
  25.0 16.6 %all-to-all-start = ((bf16[32,16,128]{2,1,0:T(8,128)(2,1)}), bf16[32,16,128]{2,1,0:T(8,128)(2,1)S(1)}, u32[]{:S(2)}, u32[]{:S(2)}) async-start(bf16[32,16,128]{2,1,0:T(8,128)(2,1)} %bitcast.12), calls=%async_computation | async-start | bytes 262144 | tf_op jit(solution)/shard_map/all_to_all | solution.py:282
  34.0 8.3 %collective-permute-start.6 = (bf16[256,128]{1,0:T(8,128)(2,1)S(1)}, bf16[256,128]{1,0:T(8,128)(2,1)S(1)}, u32[]{:S(2)}, u32[]{:S(2)}) collective-permute-start(bf16[256,128]{1,0:T(8,128)(2,1)S(1)} %get-tuple-element.35), channel_id=1, source_target_pairs={{0,128},{1,129},{2,130},{3,131},{4,132},{5,133},{6,134},{7,135},{8... | collective-permute-start | bytes 196616 | tf_op jit(solution)/shard_map/ppermute | solution.py:252
  38.1 8.0 %collective-permute-start.7 = (bf16[256,128]{1,0:T(8,128)(2,1)S(1)}, bf16[256,128]{1,0:T(8,128)(2,1)S(1)}, u32[]{:S(2)}, u32[]{:S(2)}) collective-permute-start(bf16[256,128]{1,0:T(8,128)(2,1)S(1)} %get-tuple-element.36), channel_id=1, source_target_pairs={{0,64},{1,65},{2,66},{3,67},{4,68},{5,69},{6,70},{7,71},{8,72},{9,... | collective-permute-start | bytes 196616 | tf_op jit(solution)/shard_map/ppermute | solution.py:252
  40.3 5.9 %collective-permute-start.8 = (bf16[256,128]{1,0:T(8,128)(2,1)S(1)}, bf16[256,128]{1,0:T(8,128)(2,1)S(1)}, u32[]{:S(2)}, u32[]{:S(2)}) collective-permute-start(bf16[256,128]{1,0:T(8,128)(2,1)S(1)} %get-tuple-element.37), channel_id=1, source_target_pairs={{0,32},{1,33},{2,34},{3,35},{4,36},{5,37},{6,38},{7,39},{8,40},{9,... | collective-permute-start | bytes 196616 | tf_op jit(solution)/shard_map/ppermute | solution.py:252
  46.1 10.6 %all-to-all-start.1 = ((f32[8,16,128]{2,1,0:T(8,128)}), f32[8,16,128]{2,1,0:T(8,128)S(1)}, u32[]{:S(2)}, u32[]{:S(2)}) async-start(f32[8,16,128]{2,1,0:T(8,128)} %sum_and_spread.2), calls=%async_computation.1 | async-start | bytes 131072 | tf_op jit(solution)/shard_map/all_to_all | solution.py:288
  49.5 7.9 %collective-permute-start.9 = (bf16[256,128]{1,0:T(8,128)(2,1)S(1)}, bf16[256,128]{1,0:T(8,128)(2,1)S(1)}, u32[]{:S(2)}, u32[]{:S(2)}) collective-permute-start(bf16[256,128]{1,0:T(8,128)(2,1)S(1)} %get-tuple-element.38), channel_id=1, source_target_pairs={{0,16},{1,17},{2,18},{3,19},{4,20},{5,21},{6,22},{7,23},{8,24},{9,... | collective-permute-start | bytes 196616 | tf_op jit(solution)/shard_map/ppermute | solution.py:252
  52.4 5.0 %collective-permute-start.10 = (bf16[256,128]{1,0:T(8,128)(2,1)S(1)}, bf16[256,128]{1,0:T(8,128)(2,1)S(1)}, u32[]{:S(2)}, u32[]{:S(2)}) collective-permute-start(bf16[256,128]{1,0:T(8,128)(2,1)S(1)} %get-tuple-element.39), channel_id=1, source_target_pairs={{0,8},{1,9},{2,10},{3,11},{4,12},{5,13},{6,14},{7,15},{8,0},{9,1},... | collective-permute-start | bytes 196616 | tf_op jit(solution)/shard_map/ppermute | solution.py:252
  52.7 4.9 %collective-permute-start.11 = (bf16[256,128]{1,0:T(8,128)(2,1)S(1)}, bf16[256,128]{1,0:T(8,128)(2,1)S(1)}, u32[]{:S(2)}, u32[]{:S(2)}) collective-permute-start(bf16[256,128]{1,0:T(8,128)(2,1)S(1)} %get-tuple-element.40), channel_id=1, source_target_pairs={{0,4},{1,5},{2,6},{3,7},{4,0},{5,1},{6,2},{7,3},{8,12},{9,13},{10,... | collective-permute-start | bytes 196616 | tf_op jit(solution)/shard_map/ppermute | solution.py:252
  57.7 16.9 %all-to-all-start.2 = ((bf16[32,16,128]{2,1,0:T(8,128)(2,1)}), bf16[32,16,128]{2,1,0:T(8,128)(2,1)S(1)}, u32[]{:S(2)}, u32[]{:S(2)}) async-start(bf16[32,16,128]{2,1,0:T(8,128)(2,1)} %sum_and_spread.3), calls=%async_computation.2 | async-start | bytes 262144 | tf_op jit(solution)/shard_map/all_to_all | solution.py:293
  67.0 2.3 %copy-start = (bf16[1536,1536]{1,0:T(8,128)(2,1)S(1)}, bf16[1536,1536]{1,0:T(8,128)(2,1)}, u32[]{:S(2)}) copy-start(bf16[1536,1536]{1,0:T(8,128)(2,1)} %adj_ref.1) | copy-start | bytes 14155780

commit v3 on v2

--- a/solution.py
+++ b/solution.py
@@ -12,6 +12,8 @@
 F32 = jnp.float32
 BF16 = jnp.bfloat16
 BLOCK = 384
+ORDER = (2, 3, 0, 1, 5, 4)
+EARLY = 2
 SIDE = 4
 AXES = ("z", "y", "x", "core")
 PLANE = AXES[1:]
@@ -81,41 +83,53 @@
     return results[:rounds], results[rounds], results[rounds + 1]
 
 
-def local_kernel(adj_ref, wide_ref, out_ref):
+def widen(wide_ref, recv_refs):
+    picks, width = recv_refs[0].shape
+    for number, recv_ref in enumerate(recv_refs):
+        span = slice(number * picks, (number + 1) * picks)
+        wide_ref[span, :width] = recv_ref[...]
+        wide_ref[span, width:] = jnp.ones((picks, width), BF16)
+
+
+def tiles_of(bnd_ref, span, turns):
+    return jnp.concatenate([bnd_ref[turn, span, :] for turn in turns], axis=1)
+
+
+def early_kernel(turns, adj_ref, wide_ref, bnd_ref, *refs):
+    recv_refs, (out_ref, recv_wide_ref) = refs[: len(turns)], refs[len(turns) :]
+    widen(recv_wide_ref, recv_refs)
     for start in range(0, adj_ref.shape[0], BLOCK):
         span = slice(start, start + BLOCK)
-        out_ref[span, :] = dot(adj_ref[span, :], wide_ref[...])
-
-
-def local_sum(local_adj, wide):
-    rows = local_adj.shape[0]
+        total = dot(adj_ref[span, :], wide_ref[...])
+        out_ref[span, :] = total + dot(tiles_of(bnd_ref, span, turns), recv_wide_ref[...])
+
+
+def early_sum(local_adj, wide, bnd_tiles, turns, incoming):
+    rows, picks = local_adj.shape[0], bnd_tiles.shape[2]
     return pl.pallas_call(
-        local_kernel,
+        functools.partial(early_kernel, turns),
         out_shape=jax.ShapeDtypeStruct(wide.shape, F32),
+        scratch_shapes=[pltpu.VMEM((len(turns) * picks, wide.shape[1]), BF16)],
         compiler_params=params(16),
         cost_estimate=cost(2 * rows * rows * wide.shape[1], rows * rows * 2),
-        name="local_sum",
-    )(local_adj, wide)
-
-
-def middle_kernel(rounds, *refs):
+        name="early_sum",
+    )(local_adj, wide, bnd_tiles, *incoming)
+
+
+def middle_kernel(turns, *refs):
     local_ref, bnd_ref, feats_ref, cot_ref, self_ref, neigh_ref, bias_ref = refs[:7]
-    recv_refs = refs[7 : 7 + rounds]
-    out_hbm, dagg_ref, gself_ref, gw_hbm = refs[7 + rounds : 11 + rounds]
-    back_refs = refs[11 + rounds : 11 + 2 * rounds]
-    wide_ref, both_ref, dpre_ref, inverse_ref, out_ref, gw_ref, sems = refs[11 + 2 * rounds :]
+    rounds = bnd_ref.shape[0]
+    recv_refs, refs = refs[7 : 7 + len(turns)], refs[7 + len(turns) :]
+    out_hbm, dagg_ref, gself_ref, gw_hbm = refs[:4]
+    back_refs = refs[4 : 4 + rounds]
+    wide_ref, both_ref, dpre_ref, inverse_ref, out_ref, gw_ref, sems = refs[4 + rounds :]
     rows, width = dagg_ref.shape
-    bnd = bnd_ref.shape[2]
     spans = [slice(start, start + BLOCK) for start in range(0, rows, BLOCK)]
 
-    for turn in range(rounds):
-        span = slice(turn * bnd, (turn + 1) * bnd)
-        wide_ref[span, :width] = recv_refs[turn][...]
-        wide_ref[span, width:] = jnp.ones_like(recv_refs[turn])
+    widen(wide_ref, recv_refs)
     both_ref[:, :width] = feats_ref[:, :width]
     for span in spans:
-        tiles = jnp.concatenate([bnd_ref[turn, span, :] for turn in range(rounds)], axis=1)
-        total = local_ref[span, :] + dot(tiles, wide_ref[...])
+        total = local_ref[span, :] + dot(tiles_of(bnd_ref, span, turns), wide_ref[...])
         inverse = 1.0 / (1.0 + total[:, width:])
         inverse_ref[span, :] = inverse
         both_ref[span, width:] = (total[:, :width] * inverse).astype(BF16)
@@ -149,12 +163,12 @@
     out_copy.wait()
 
 
-def middle(local, bnd_tiles, wide, cotangent, w_self, w_neigh, bias, incoming):
+def middle(local, bnd_tiles, wide, cotangent, w_self, w_neigh, bias, turns, incoming):
     rounds, rows, bnd = bnd_tiles.shape
     width, hidden = w_self.shape
     results = pl.pallas_call(
-        functools.partial(middle_kernel, rounds),
-        in_specs=[VMEM] * (7 + rounds),
+        functools.partial(middle_kernel, turns),
+        in_specs=[VMEM] * (7 + len(turns)),
         out_specs=[ANY, VMEM, VMEM, ANY] + [VMEM] * rounds,
         out_shape=[
             pltpu.HBM((rows, hidden), BF16),
@@ -164,7 +178,7 @@
         ]
         + [jax.ShapeDtypeStruct((bnd, width), BF16)] * rounds,
         scratch_shapes=[
-            pltpu.VMEM((rounds * bnd, 2 * width), BF16),
+            pltpu.VMEM((len(turns) * bnd, 2 * width), BF16),
             pltpu.VMEM((rows, 2 * width), BF16),
             pltpu.VMEM((rows, hidden), BF16),
             pltpu.VMEM((rows, width), F32),
@@ -269,28 +283,28 @@
         return bits - turn % bits
 
     outgoing, wide, near_adj = gather_rows(feats, index_lists, local_adj)
-    incoming = [swapped(outgoing[turn], partner(turn)) for turn in range(rounds)]
-    local = local_sum(near_adj, wide)
+    incoming = [swapped(outgoing[turn], partner(turn)) for turn in ORDER]
+    first, last = ORDER[:EARLY], ORDER[EARLY:]
+    local = early_sum(near_adj, wide, bnd_tiles, first, incoming[:EARLY])
     output, dagg, gself, gw, back = middle(
-        local, bnd_tiles, wide, cotangent, w_self, w_neigh, bias, incoming
-    )
-    base = turned_sum(local_adj, dagg, gself)
+        local, bnd_tiles, wide, cotangent, w_self, w_neigh, bias, last, incoming[EARLY:]
+    )
 
     plane = math.prod(lax.axis_size(axis) for axis in PLANE)
     planes = chips * cores // plane
     pieces = gw.reshape(plane, -1, width)
     pieces = lax.all_to_all(pieces, PLANE, 0, 0, tiled=True)
-    near = [turn for turn in range(rounds) if partner(turn) < plane.bit_length() - 1]
-    far = [turn for turn in range(rounds) if turn not in near]
+    far = (2, 0, 4)
+    near = (1, 3, 5)
     returned = {turn: swapped(back[turn], partner(turn)) for turn in far}
     pieces = sum_and_spread(pieces, planes, F32, 1.0)
-    pieces = after(pieces, *[returned[turn] for turn in far])
     pieces = lax.all_to_all(pieces, AXES[:1], 0, 0, tiled=True)
-    returned |= {turn: swapped(back[turn], partner(turn)) for turn in near}
+    for turn in near:
+        returned[turn] = swapped(after(back[turn], *[returned[other] for other in far]), partner(turn))
     scale = 1.0 / math.sqrt(rows * chips * cores)
     pieces = sum_and_spread(pieces, plane, BF16, scale)
-    pieces = after(pieces, *[returned[turn] for turn in near])
     pieces = lax.all_to_all(pieces, PLANE, 0, 0, tiled=True)
+    base = turned_sum(local_adj, after(dagg, *[returned[turn] for turn in near]), gself)
     grad_feats = scatter_rows(base, index_lists, [returned[turn] for turn in range(rounds)])
     sums = jnp.concatenate([*pieces.reshape(gw.shape)], axis=1).astype(F32)
     return output, grad_feats, sums[:width], sums[width:]

time: 75.7 us -> 68 us (0.90)
  starting transfers between devices: 49.7 us -> 41.7 us
    all_to_all x2, starting transfers between devices: 18.3 us -> 13.7 us  [per_device(): pieces = lax.all_to_all(pieces, PLANE, 0, 0, tiled=True)]
    ppermute x12, starting transfers between devices: 28.1 us -> 24.6 us  [swapped(): lax.ppermute(block, AXES, [(low, low ^ 1 << bit) for low in range(count)])]
    ppermute x12, waiting for transfers between devices: 4.54 us -> 1.33 us  [swapped(): lax.ppermute(block, AXES, [(low, low ^ 1 << bit) for low in range(count)])]
    all_to_all x2, waiting for transfers between devices: 3.56 us -> 6.57 us  [per_device(): pieces = lax.all_to_all(pieces, PLANE, 0, 0, tiled=True)]
  transfers between devices with their start and end apart: 15 -> 15, of which waited for: 6 -> 4; matrix products, arithmetic and copies ran while one was open for 0% -> 0% of each run, Pallas kernels for 8% -> 9%
where the time goes in v3:
time: 68 us; the launch traced here: 67.6 us
  starting transfers between devices  41.7 us (61%)
  Pallas kernels  12.5 us (18%)
  waiting for transfers between devices  9.5 us (14%)
  local copies, waits for them, and re-layouts  3.09 us (5%)
  between operations  0.86 us (1%)
    ppermute x12, starting transfers between devices, swapped(): lax.ppermute(block, AXES, [(low, low ^ 1 << bit) for low in range(count)])  24.6 us
    all_to_all x2, starting transfers between devices, per_device(): pieces = lax.all_to_all(pieces, PLANE, 0, 0, tiled=True)  13.7 us
    all_to_all x2, waiting for transfers between devices, per_device(): pieces = lax.all_to_all(pieces, PLANE, 0, 0, tiled=True)  6.57 us
    pallas_call x1, Pallas kernels, middle(): pl.pallas_call(functools.partial(middle_kernel, turns), in_specs=[VMEM] *...  3.63 us
    all_to_all x1, starting transfers between devices, per_device(): pieces = lax.all_to_all(pieces, AXES[:1], 0, 0, tiled=True)  3.36 us
    pallas_call x1, Pallas kernels, gather_rows(): pl.pallas_call(functools.partial(gather_kernel, rounds), in_specs=[ANY, A...  2.65 us
    unnamed x14, local copies, waits for them, and re-layouts  2.36 us
    pallas_call x1, Pallas kernels, scatter_rows(): pl.pallas_call(scatter_kernel, out_shape=jax.ShapeDtypeStruct((rows, widt...  2.14 us
  transfers between devices with their start and end apart: 15, of which 4 were waited for; matrix products, arithmetic and copies ran while one was open for 0% of the time, Pallas kernels for 9%

profile of v3, /device:TPU:1, one launch (start us, length us, event | category | flops | bytes accessed | tf_op | source)
XLA Modules:
  0.0 67.6 jit_solution(2118815400514734012)
XLA Ops:
  0.6 2.7 %gather_rows.1 = (bf16[256,128]{1,0:T(8,128)(2,1)S(1)}, bf16[256,128]{1,0:T(8,128)(2,1)S(1)}, bf16[256,128]{1,0:T(8,128)(2,1)S(1)}, bf16[256,128]{1,0:T(8,128)(2...) custom-call(bf16[1536,128]{1,0:T(8,128)(2,1)} %feats_hbm.1, ...), custom_call_target="tpu_custom_call" | custom-call | flops 603979776 | bytes 393216 | tf_op jit(solution)/shard_map/gather_rows/pallas_call | solution.py:72
  3.3 2.6 %collective-permute-start = (bf16[256,128]{1,0:T(8,128)(2,1)S(1)}, bf16[256,128]{1,0:T(8,128)(2,1)S(1)}, u32[]{:S(2)}, u32[]{:S(2)}) collective-permute-start(bf16[256,128]{1,0:T(8,128)(2,1)S(1)} %get-tuple-element.28), channel_id=1, source_target_pairs={{0,32},{1,33},{2,34},{3,35},{4,36},{5,37},{6,38},{7,39},{8,40},{9,... | collective-permute-start | bytes 196616 | tf_op jit(solution)/shard_map/ppermute | solution.py:266
  5.9 2.9 %collective-permute-start.1 = (bf16[256,128]{1,0:T(8,128)(2,1)S(1)}, bf16[256,128]{1,0:T(8,128)(2,1)S(1)}, u32[]{:S(2)}, u32[]{:S(2)}) collective-permute-start(bf16[256,128]{1,0:T(8,128)(2,1)S(1)} %get-tuple-element.29), channel_id=1, source_target_pairs={{0,16},{1,17},{2,18},{3,19},{4,20},{5,21},{6,22},{7,23},{8,24},{9,... | collective-permute-start | bytes 196616 | tf_op jit(solution)/shard_map/ppermute | solution.py:266
  8.8 6.0 %collective-permute-start.2 = (bf16[256,128]{1,0:T(8,128)(2,1)S(1)}, bf16[256,128]{1,0:T(8,128)(2,1)S(1)}, u32[]{:S(2)}, u32[]{:S(2)}) collective-permute-start(bf16[256,128]{1,0:T(8,128)(2,1)S(1)} %get-tuple-element.30), channel_id=1, source_target_pairs={{0,128},{1,129},{2,130},{3,131},{4,132},{5,133},{6,134},{7,135},{8... | collective-permute-start | bytes 196616 | tf_op jit(solution)/shard_map/ppermute | solution.py:266
  14.8 1.2 %collective-permute-start.3 = (bf16[256,128]{1,0:T(8,128)(2,1)S(1)}, bf16[256,128]{1,0:T(8,128)(2,1)S(1)}, u32[]{:S(2)}, u32[]{:S(2)}) collective-permute-start(bf16[256,128]{1,0:T(8,128)(2,1)S(1)} %get-tuple-element.31), channel_id=1, source_target_pairs={{0,64},{1,65},{2,66},{3,67},{4,68},{5,69},{6,70},{7,71},{8,72},{9,... | collective-permute-start | bytes 196616 | tf_op jit(solution)/shard_map/ppermute | solution.py:266
  16.0 2.7 %collective-permute-start.4 = (bf16[256,128]{1,0:T(8,128)(2,1)S(1)}, bf16[256,128]{1,0:T(8,128)(2,1)S(1)}, u32[]{:S(2)}, u32[]{:S(2)}) collective-permute-start(bf16[256,128]{1,0:T(8,128)(2,1)S(1)} %get-tuple-element.32), channel_id=1, source_target_pairs={{0,4},{1,5},{2,6},{3,7},{4,0},{5,1},{6,2},{7,3},{8,12},{9,13},{10,... | collective-permute-start | bytes 196616 | tf_op jit(solution)/shard_map/ppermute | solution.py:266
  18.7 0.4 collective-permute-start.5
  19.1 0.0 copy-start.5
  19.1 0.0 copy-start.6
  19.2 1.8 %early_sum.1.refs_0_ = f32[1536,256]{1,0:T(8,128)S(1)} custom-call(bf16[1536,1536]{1,0:T(8,128)(2,1)S(1)} %get-tuple-element.26.adj_ref, bf16[1536,256]{1,0:T(8,128)(2,1)S(1)} %get-tuple-element.27.wide_ref.refs_2_, bf16[6,1536,256]{2,1,0:T(8,128)(2,1)S(1)} %bitcast.6, bf16[256,128]{1,0:T(8,128)(2,1)S(1)} %collective-permute-done.refs_0_, ...), custom_call_target="tpu_custom_call" | custom-call | flops 1207959552 | bytes 4718592 | tf_op jit(solution)/shard_map/early_sum/pallas_call | solution.py:109
  21.0 1.3 %collective-permute-done.3.refs_8_ = bf16[256,128]{1,0:T(8,128)(2,1)S(1)} collective-permute-done((bf16[256,128]{1,0:T(8,128)(2,1)S(1)}, bf16[256,128]{1,0:T(8,128)(2,1)S(1)}, u32[]{:S(2)}, u32[]{:S(2)}) %collective-permute-start.3) | collective-permute-done | bytes 65568 | tf_op jit(solution)/shard_map/ppermute | solution.py:266
  22.3 3.6 %middle.1 = (bf16[1536,256]{1,0:T(8,128)(2,1)}, bf16[1536,128]{1,0:T(8,128)(2,1)S(1)}, f32[1536,128]{1,0:T(8,128)S(1)}, bf16[2,256,128]{2,1,0:T(8,128)(2,1)}, bf...) custom-call(f32[1536,256]{1,0:T(8,128)S(1)} %early_sum.1.refs_0_, ...), custom_call_target="tpu_custom_call" | custom-call | flops 2415919104 | bytes 4718592 | tf_op jit(solution)/shard_map/middle/pallas_call | solution.py:169
  26.0 0.0 copy-start.2
  26.0 6.3 %all-to-all-start = ((bf16[32,16,128]{2,1,0:T(8,128)(2,1)}), bf16[32,16,128]{2,1,0:T(8,128)(2,1)S(1)}, u32[]{:S(2)}, u32[]{:S(2)}) async-start(bf16[32,16,128]{2,1,0:T(8,128)(2,1)} %bitcast.13), calls=%async_computation | async-start | bytes 262144 | tf_op jit(solution)/shard_map/all_to_all | solution.py:296
  32.3 0.8 %collective-permute-start.6 = (bf16[256,128]{1,0:T(8,128)(2,1)S(1)}, bf16[256,128]{1,0:T(8,128)(2,1)S(1)}, u32[]{:S(2)}, u32[]{:S(2)}) collective-permute-start(bf16[256,128]{1,0:T(8,128)(2,1)S(1)} %get-tuple-element.37), channel_id=1, source_target_pairs={{0,32},{1,33},{2,34},{3,35},{4,36},{5,37},{6,38},{7,39},{8,40},{9,... | collective-permute-start | bytes 196616 | tf_op jit(solution)/shard_map/ppermute | solution.py:266
  33.1 1.1 %collective-permute-start.7 = (bf16[256,128]{1,0:T(8,128)(2,1)S(1)}, bf16[256,128]{1,0:T(8,128)(2,1)S(1)}, u32[]{:S(2)}, u32[]{:S(2)}) collective-permute-start(bf16[256,128]{1,0:T(8,128)(2,1)S(1)} %get-tuple-element.38), channel_id=1, source_target_pairs={{0,128},{1,129},{2,130},{3,131},{4,132},{5,133},{6,134},{7,135},{8... | collective-permute-start | bytes 196616 | tf_op jit(solution)/shard_map/ppermute | solution.py:266
  34.2 1.4 %collective-permute-start.8 = (bf16[256,128]{1,0:T(8,128)(2,1)S(1)}, bf16[256,128]{1,0:T(8,128)(2,1)S(1)}, u32[]{:S(2)}, u32[]{:S(2)}) collective-permute-start(bf16[256,128]{1,0:T(8,128)(2,1)S(1)} %get-tuple-element.39), channel_id=1, source_target_pairs={{0,8},{1,9},{2,10},{3,11},{4,12},{5,13},{6,14},{7,15},{8,0},{9,1},... | collective-permute-start | bytes 196616 | tf_op jit(solution)/shard_map/ppermute | solution.py:266
  35.6 4.4 %all-to-all-done.parts_ref = bf16[32,16,128]{2,1,0:T(8,128)(2,1)S(1)} async-done(((bf16[32,16,128]{2,1,0:T(8,128)(2,1)}), bf16[32,16,128]{2,1,0:T(8,128)(2,1)S(1)}, u32[]{:S(2)}, u32[]{:S(2)}) %all-to-all-start) | async-done | bytes 131104 | tf_op jit(solution)/shard_map/all_to_all | solution.py:296
  40.0 0.7 sum_and_spread.2
  40.7 3.4 %all-to-all-start.1 = ((f32[8,16,128]{2,1,0:T(8,128)}), f32[8,16,128]{2,1,0:T(8,128)S(1)}, u32[]{:S(2)}, u32[]{:S(2)}) async-start(f32[8,16,128]{2,1,0:T(8,128)} %sum_and_spread.2), calls=%async_computation.1 | async-start | bytes 131072 | tf_op jit(solution)/shard_map/all_to_all | solution.py:301
  44.1 2.3 %collective-permute-start.9 = (bf16[256,128]{1,0:T(8,128)(2,1)S(1)}, bf16[256,128]{1,0:T(8,128)(2,1)S(1)}, u32[]{:S(2)}, u32[]{:S(2)}) collective-permute-start(bf16[256,128]{1,0:T(8,128)(2,1)S(1)} %get-tuple-element.40), channel_id=1, source_target_pairs={{0,64},{1,65},{2,66},{3,67},{4,68},{5,69},{6,70},{7,71},{8,72},{9,... | collective-permute-start | bytes 196616 | tf_op jit(solution)/shard_map/ppermute | solution.py:266
  46.4 1.0 %collective-permute-start.10 = (bf16[256,128]{1,0:T(8,128)(2,1)S(1)}, bf16[256,128]{1,0:T(8,128)(2,1)S(1)}, u32[]{:S(2)}, u32[]{:S(2)}) collective-permute-start(bf16[256,128]{1,0:T(8,128)(2,1)S(1)} %get-tuple-element.42), channel_id=1, source_target_pairs={{0,16},{1,17},{2,18},{3,19},{4,20},{5,21},{6,22},{7,23},{8,24},{9,... | collective-permute-start | bytes 196616 | tf_op jit(solution)/shard_map/ppermute | solution.py:266
  47.5 2.1 %collective-permute-start.11 = (bf16[256,128]{1,0:T(8,128)(2,1)S(1)}, bf16[256,128]{1,0:T(8,128)(2,1)S(1)}, u32[]{:S(2)}, u32[]{:S(2)}) collective-permute-start(bf16[256,128]{1,0:T(8,128)(2,1)S(1)} %get-tuple-element.44), channel_id=1, source_target_pairs={{0,4},{1,5},{2,6},{3,7},{4,0},{5,1},{6,2},{7,3},{8,12},{9,13},{10,... | collective-permute-start | bytes 196616 | tf_op jit(solution)/shard_map/ppermute | solution.py:266
  49.5 1.6 %all-to-all-done.1.parts_ref = f32[8,16,128]{2,1,0:T(8,128)S(1)} async-done(((f32[8,16,128]{2,1,0:T(8,128)}), f32[8,16,128]{2,1,0:T(8,128)S(1)}, u32[]{:S(2)}, u32[]{:S(2)}) %all-to-all-start.1) | async-done | bytes 65568 | tf_op jit(solution)/shard_map/all_to_all | solution.py:301
  51.1 0.7 %sum_and_spread.3 = bf16[32,16,128]{2,1,0:T(8,128)(2,1)} custom-call(f32[8,16,128]{2,1,0:T(8,128)S(1)} %all-to-all-done.1.parts_ref), custom_call_target="tpu_custom_call" | custom-call | tf_op jit(solution)/shard_map/sum_and_spread/pallas_call | solution.py:234
  51.8 7.4 %all-to-all-start.2 = ((bf16[32,16,128]{2,1,0:T(8,128)(2,1)}), bf16[32,16,128]{2,1,0:T(8,128)(2,1)S(1)}, u32[]{:S(2)}, u32[]{:S(2)}) async-start(bf16[32,16,128]{2,1,0:T(8,128)(2,1)} %sum_and_spread.3), calls=%async_computation.2 | async-start | bytes 262144 | tf_op jit(solution)/shard_map/all_to_all | solution.py:306
  59.3 0.0 copy-start
  59.3 2.3 %copy-done = bf16[1536,1536]{1,0:T(8,128)(2,1)S(1)} copy-done((bf16[1536,1536]{1,0:T(8,128)(2,1)S(1)}, bf16[1536,1536]{1,0:T(8,128)(2,1)}, u32[]{:S(2)}) %copy-start) | copy-done | bytes 4718616
  61.6 0.9 %turned_sum.1.base_ref = f32[1536,128]{1,0:T(8,128)S(1)} custom-call(bf16[1536,1536]{1,0:T(8,128)(2,1)S(1)} %copy-done, bf16[1536,128]{1,0:T(8,128)(2,1)S(1)} %get-tuple-element.45.dagg_ref, f32[1536,128]{1,0:T(8,128)S(1)} %get-tuple-element.46.gself_ref), custom_call_target="tpu_custom_call" | custom-call | flops 603979776 | bytes 4718592 | tf_op jit(solution)/shard_map/turned_sum/pallas_call | solution.py:211
  62.6 2.1 %scatter_rows.1 = bf16[1536,128]{1,0:T(8,128)(2,1)} custom-call(f32[1536,128]{1,0:T(8,128)S(1)} %turned_sum.1.base_ref, s32[6,1,256]{2,1,0:T(1,128)S(1)} %bitcast.9, bf16[256,128]{1,0:T(8,128)(2,1)S(1)} %collective-permute-done.7.refs_0_, bf16[256,128]{1,0:T(8,128)(2,1)S(1)} %collective-permute-done.9.refs_1_, ...), custom_call_target="tpu_custom_call" | custom-call | flops 603979776 | bytes 1179648 | tf_op jit(solution)/shard_map/scatter_rows/pallas_call | solution.py:255
  64.7 2.2 %all-to-all-done.2 = bf16[32,16,128]{2,1,0:T(8,128)(2,1)S(1)} async-done(((bf16[32,16,128]{2,1,0:T(8,128)(2,1)}), bf16[32,16,128]{2,1,0:T(8,128)(2,1)S(1)}, u32[]{:S(2)}, u32[]{:S(2)}) %all-to-all-start.2) | async-done | bytes 131104 | tf_op jit(solution)/shard_map/all_to_all | solution.py:306
  66.9 0.7 %fusion = (f32[128,256]{1,0:T(8,128)}, f32[128,256]{1,0:T(8,128)}) fusion(f32[256,256]{1,0:T(8,128)S(1)} %maximum_convert_fusion), kind=kLoop, calls=%fused_computation.1 | loop fusion | bytes 524288 | tf_op jit(solution)/shard_map/slice | solution.py:310
  (22 shorter events, 0.1 us)
Async XLA Ops:
  0.6 18.5 %copy-start.1 = (bf16[1,6,1536,256]{3,2,1,0:T(8,128)(2,1)S(1)}, bf16[1,6,1536,256]{3,2,1,0:T(8,128)(2,1)}, u32[]{:S(2)}) copy-start(bf16[1,6,1536,256]{3,2,1,0:T(8,128)(2,1)} %param.10) | copy-start | bytes 14155780
  3.3 15.4 %collective-permute-start = (bf16[256,128]{1,0:T(8,128)(2,1)S(1)}, bf16[256,128]{1,0:T(8,128)(2,1)S(1)}, u32[]{:S(2)}, u32[]{:S(2)}) collective-permute-start(bf16[256,128]{1,0:T(8,128)(2,1)S(1)} %get-tuple-element.28), channel_id=1, source_target_pairs={{0,32},{1,33},{2,34},{3,35},{4,36},{5,37},{6,38},{7,39},{8,40},{9,... | collective-permute-start | bytes 196616 | tf_op jit(solution)/shard_map/ppermute | solution.py:266
  5.9 13.3 %collective-permute-start.1 = (bf16[256,128]{1,0:T(8,128)(2,1)S(1)}, bf16[256,128]{1,0:T(8,128)(2,1)S(1)}, u32[]{:S(2)}, u32[]{:S(2)}) collective-permute-start(bf16[256,128]{1,0:T(8,128)(2,1)S(1)} %get-tuple-element.29), channel_id=1, source_target_pairs={{0,16},{1,17},{2,18},{3,19},{4,20},{5,21},{6,22},{7,23},{8,24},{9,... | collective-permute-start | bytes 196616 | tf_op jit(solution)/shard_map/ppermute | solution.py:266
  8.8 12.2 %collective-permute-start.2 = (bf16[256,128]{1,0:T(8,128)(2,1)S(1)}, bf16[256,128]{1,0:T(8,128)(2,1)S(1)}, u32[]{:S(2)}, u32[]{:S(2)}) collective-permute-start(bf16[256,128]{1,0:T(8,128)(2,1)S(1)} %get-tuple-element.30), channel_id=1, source_target_pairs={{0,128},{1,129},{2,130},{3,131},{4,132},{5,133},{6,134},{7,135},{8... | collective-permute-start | bytes 196616 | tf_op jit(solution)/shard_map/ppermute | solution.py:266
  14.8 7.5 %collective-permute-start.3 = (bf16[256,128]{1,0:T(8,128)(2,1)S(1)}, bf16[256,128]{1,0:T(8,128)(2,1)S(1)}, u32[]{:S(2)}, u32[]{:S(2)}) collective-permute-start(bf16[256,128]{1,0:T(8,128)(2,1)S(1)} %get-tuple-element.31), channel_id=1, source_target_pairs={{0,64},{1,65},{2,66},{3,67},{4,68},{5,69},{6,70},{7,71},{8,72},{9,... | collective-permute-start | bytes 196616 | tf_op jit(solution)/shard_map/ppermute | solution.py:266
  16.0 6.3 %collective-permute-start.4 = (bf16[256,128]{1,0:T(8,128)(2,1)S(1)}, bf16[256,128]{1,0:T(8,128)(2,1)S(1)}, u32[]{:S(2)}, u32[]{:S(2)}) collective-permute-start(bf16[256,128]{1,0:T(8,128)(2,1)S(1)} %get-tuple-element.32), channel_id=1, source_target_pairs={{0,4},{1,5},{2,6},{3,7},{4,0},{5,1},{6,2},{7,3},{8,12},{9,13},{10,... | collective-permute-start | bytes 196616 | tf_op jit(solution)/shard_map/ppermute | solution.py:266
  18.7 3.6 %collective-permute-start.5 = (bf16[256,128]{1,0:T(8,128)(2,1)S(1)}, bf16[256,128]{1,0:T(8,128)(2,1)S(1)}, u32[]{:S(2)}, u32[]{:S(2)}) collective-permute-start(bf16[256,128]{1,0:T(8,128)(2,1)S(1)} %get-tuple-element.33), channel_id=1, source_target_pairs={{0,8},{1,9},{2,10},{3,11},{4,12},{5,13},{6,14},{7,15},{8,0},{9,1},... | collective-permute-start | bytes 196616 | tf_op jit(solution)/shard_map/ppermute | solution.py:266
  19.1 3.2 %copy-start.3 = (bf16[1536,256]{1,0:T(8,128)(2,1)S(1)}, bf16[1536,256]{1,0:T(8,128)(2,1)}, u32[]{:S(2)}) copy-start(bf16[1536,256]{1,0:T(8,128)(2,1)} %refs_3_.1) | copy-start | bytes 2359300
  19.1 3.2 %copy-start.4 = (bf16[128,256]{1,0:T(8,128)(2,1)S(1)}, bf16[128,256]{1,0:T(8,128)(2,1)}, u32[]{:S(2)}) copy-start(bf16[128,256]{1,0:T(8,128)(2,1)} %refs_4_.1) | copy-start | bytes 196612
  19.1 3.2 %copy-start.5 = (bf16[128,256]{1,0:T(8,128)(2,1)S(1)}, bf16[128,256]{1,0:T(8,128)(2,1)}, u32[]{:S(2)}) copy-start(bf16[128,256]{1,0:T(8,128)(2,1)} %refs_5_.1) | copy-start | bytes 196612
  19.1 3.2 %copy-start.6 = (f32[256]{0:T(256)S(1)}, f32[256]{0:T(256)}, u32[]{:S(2)}) copy-start(f32[256]{0:T(256)} %param.14) | copy-start | bytes 3076
  26.0 36.6 %copy-start.2 = (s32[1,6,256]{2,0,1:T(1,128)S(1)}, s32[1,6,256]{2,0,1:T(1,128)}, u32[]{:S(2)}) copy-start(s32[1,6,256]{2,0,1:T(1,128)} %param.11) | copy-start | bytes 18436
  26.0 14.0 %all-to-all-start = ((bf16[32,16,128]{2,1,0:T(8,128)(2,1)}), bf16[32,16,128]{2,1,0:T(8,128)(2,1)S(1)}, u32[]{:S(2)}, u32[]{:S(2)}) async-start(bf16[32,16,128]{2,1,0:T(8,128)(2,1)} %bitcast.13), calls=%async_computation | async-start | bytes 262144 | tf_op jit(solution)/shard_map/all_to_all | solution.py:296
  32.3 11.8 %collective-permute-start.6 = (bf16[256,128]{1,0:T(8,128)(2,1)S(1)}, bf16[256,128]{1,0:T(8,128)(2,1)S(1)}, u32[]{:S(2)}, u32[]{:S(2)}) collective-permute-start(bf16[256,128]{1,0:T(8,128)(2,1)S(1)} %get-tuple-element.37), channel_id=1, source_target_pairs={{0,32},{1,33},{2,34},{3,35},{4,36},{5,37},{6,38},{7,39},{8,40},{9,... | collective-permute-start | bytes 196616 | tf_op jit(solution)/shard_map/ppermute | solution.py:266
  33.1 11.0 %collective-permute-start.7 = (bf16[256,128]{1,0:T(8,128)(2,1)S(1)}, bf16[256,128]{1,0:T(8,128)(2,1)S(1)}, u32[]{:S(2)}, u32[]{:S(2)}) collective-permute-start(bf16[256,128]{1,0:T(8,128)(2,1)S(1)} %get-tuple-element.38), channel_id=1, source_target_pairs={{0,128},{1,129},{2,130},{3,131},{4,132},{5,133},{6,134},{7,135},{8... | collective-permute-start | bytes 196616 | tf_op jit(solution)/shard_map/ppermute | solution.py:266
  34.2 9.9 %collective-permute-start.8 = (bf16[256,128]{1,0:T(8,128)(2,1)S(1)}, bf16[256,128]{1,0:T(8,128)(2,1)S(1)}, u32[]{:S(2)}, u32[]{:S(2)}) collective-permute-start(bf16[256,128]{1,0:T(8,128)(2,1)S(1)} %get-tuple-element.39), channel_id=1, source_target_pairs={{0,8},{1,9},{2,10},{3,11},{4,12},{5,13},{6,14},{7,15},{8,0},{9,1},... | collective-permute-start | bytes 196616 | tf_op jit(solution)/shard_map/ppermute | solution.py:266
  40.7 10.5 %all-to-all-start.1 = ((f32[8,16,128]{2,1,0:T(8,128)}), f32[8,16,128]{2,1,0:T(8,128)S(1)}, u32[]{:S(2)}, u32[]{:S(2)}) async-start(f32[8,16,128]{2,1,0:T(8,128)} %sum_and_spread.2), calls=%async_computation.1 | async-start | bytes 131072 | tf_op jit(solution)/shard_map/all_to_all | solution.py:301
  44.1 15.2 %collective-permute-start.9 = (bf16[256,128]{1,0:T(8,128)(2,1)S(1)}, bf16[256,128]{1,0:T(8,128)(2,1)S(1)}, u32[]{:S(2)}, u32[]{:S(2)}) collective-permute-start(bf16[256,128]{1,0:T(8,128)(2,1)S(1)} %get-tuple-element.40), channel_id=1, source_target_pairs={{0,64},{1,65},{2,66},{3,67},{4,68},{5,69},{6,70},{7,71},{8,72},{9,... | collective-permute-start | bytes 196616 | tf_op jit(solution)/shard_map/ppermute | solution.py:266
  46.4 12.8 %collective-permute-start.10 = (bf16[256,128]{1,0:T(8,128)(2,1)S(1)}, bf16[256,128]{1,0:T(8,128)(2,1)S(1)}, u32[]{:S(2)}, u32[]{:S(2)}) collective-permute-start(bf16[256,128]{1,0:T(8,128)(2,1)S(1)} %get-tuple-element.42), channel_id=1, source_target_pairs={{0,16},{1,17},{2,18},{3,19},{4,20},{5,21},{6,22},{7,23},{8,24},{9,... | collective-permute-start | bytes 196616 | tf_op jit(solution)/shard_map/ppermute | solution.py:266
  47.5 11.8 %collective-permute-start.11 = (bf16[256,128]{1,0:T(8,128)(2,1)S(1)}, bf16[256,128]{1,0:T(8,128)(2,1)S(1)}, u32[]{:S(2)}, u32[]{:S(2)}) collective-permute-start(bf16[256,128]{1,0:T(8,128)(2,1)S(1)} %get-tuple-element.44), channel_id=1, source_target_pairs={{0,4},{1,5},{2,6},{3,7},{4,0},{5,1},{6,2},{7,3},{8,12},{9,13},{10,... | collective-permute-start | bytes 196616 | tf_op jit(solution)/shard_map/ppermute | solution.py:266
  51.8 15.0 %all-to-all-start.2 = ((bf16[32,16,128]{2,1,0:T(8,128)(2,1)}), bf16[32,16,128]{2,1,0:T(8,128)(2,1)S(1)}, u32[]{:S(2)}, u32[]{:S(2)}) async-start(bf16[32,16,128]{2,1,0:T(8,128)(2,1)} %sum_and_spread.3), calls=%async_computation.2 | async-start | bytes 262144 | tf_op jit(solution)/shard_map/all_to_all | solution.py:306
  59.3 2.3 %copy-start = (bf16[1536,1536]{1,0:T(8,128)(2,1)S(1)}, bf16[1536,1536]{1,0:T(8,128)(2,1)}, u32[]{:S(2)}) copy-start(bf16[1536,1536]{1,0:T(8,128)(2,1)} %adj_ref.1) | copy-start | bytes 14155780

commit v4 on v3

--- a/solution.py
+++ b/solution.py
@@ -12,8 +12,8 @@
 F32 = jnp.float32
 BF16 = jnp.bfloat16
 BLOCK = 384
-ORDER = (2, 3, 0, 1, 5, 4)
-EARLY = 2
+ORDER = (2, 3, 1, 0, 5, 4)
+EARLY = 3
 SIDE = 4
 AXES = ("z", "y", "x", "core")
 PLANE = AXES[1:]
@@ -202,21 +202,6 @@
     return results[0], results[1], results[2], results[3], results[4:]
 
 
-def turned_kernel(adj_ref, dagg_ref, gself_ref, out_ref):
-    out_ref[...] = gself_ref[...] + dot(dagg_ref[...].T, adj_ref[...]).T
-
-
-def turned_sum(local_adj, dagg, gself):
-    rows, width = dagg.shape
-    return pl.pallas_call(
-        turned_kernel,
-        out_shape=jax.ShapeDtypeStruct((rows, width), F32),
-        compiler_params=params(32),
-        cost_estimate=cost(2 * rows * rows * width, rows * rows * 2),
-        name="turned_sum",
-    )(local_adj, dagg, gself)
-
-
 def spread_kernel(scale, parts_ref, out_hbm, wide_ref, sem):
     total = parts_ref[0].astype(F32)
     for number in range(1, parts_ref.shape[0]):
@@ -242,23 +227,44 @@
     )(parts)
 
 
-def scatter_kernel(base_ref, index_ref, *refs):
-    total = base_ref[...]
-    for turn, back_ref in enumerate(refs[:-1]):
-        total = total + dot(one_hot(index_ref[turn], base_ref.shape[0]), back_ref[...])
-    refs[-1][...] = total.astype(refs[-1].dtype)
-
-
-def scatter_rows(base, index_lists, returned):
-    rounds, _, picks = index_lists.shape
-    rows, width = base.shape
+def finish_kernel(adj_hbm, dagg_ref, gself_ref, index_ref, *refs):
+    back_refs, (out_ref, adj_ref, base_ref, sems) = refs[:-4], refs[-4:]
+    rows = adj_hbm.shape[0]
+    spans = [pl.ds(start, BLOCK) for start in range(0, rows, BLOCK)]
+    copies = [
+        pltpu.make_async_copy(adj_hbm.at[span, :], adj_ref.at[span, :], sems.at[number])
+        for number, span in enumerate(spans)
+    ]
+    for copy in copies:
+        copy.start()
+    base = gself_ref[...]
+    for turn, back_ref in enumerate(back_refs):
+        base = base + dot(one_hot(index_ref[turn], rows), back_ref[...])
+    base_ref[...] = base
+    turned = dagg_ref[...].T
+    total = None
+    for copy, span in zip(copies, spans):
+        copy.wait()
+        part = dot(turned[:, span.start : span.start + BLOCK], adj_ref[span, :])
+        total = part if total is None else total + part
+    out_ref[...] = (base_ref[...] + total.T).astype(out_ref.dtype)
+
+
+def finish(local_adj, dagg, gself, index_lists, returned):
+    rows, width = dagg.shape
     return pl.pallas_call(
-        scatter_kernel,
+        finish_kernel,
+        in_specs=[ANY] + [VMEM] * (3 + len(returned)),
         out_shape=jax.ShapeDtypeStruct((rows, width), BF16),
-        compiler_params=params(32),
-        cost_estimate=cost(2 * rows * picks * width * rounds, rows * width * 6),
-        name="scatter_rows",
-    )(base, index_lists, *returned)
+        scratch_shapes=[
+            pltpu.VMEM((rows, rows), BF16),
+            pltpu.VMEM((rows, width), F32),
+            DMA((rows // BLOCK,)),
+        ],
+        compiler_params=params(24),
+        cost_estimate=cost(4 * rows * rows * width, rows * rows * 2),
+        name="finish",
+    )(in_hbm(local_adj), dagg, gself, index_lists, *returned)
 
 
 def swapped(block, bit):
@@ -304,8 +310,9 @@
     scale = 1.0 / math.sqrt(rows * chips * cores)
     pieces = sum_and_spread(pieces, plane, BF16, scale)
     pieces = lax.all_to_all(pieces, PLANE, 0, 0, tiled=True)
-    base = turned_sum(local_adj, after(dagg, *[returned[turn] for turn in near]), gself)
-    grad_feats = scatter_rows(base, index_lists, [returned[turn] for turn in range(rounds)])
+    grad_feats = finish(
+        local_adj, dagg, gself, index_lists, [returned[turn] for turn in range(rounds)]
+    )
     sums = jnp.concatenate([*pieces.reshape(gw.shape)], axis=1).astype(F32)
     return output, grad_feats, sums[:width], sums[width:]
 

time: 68 us -> 67.8 us (level)
  local copies, waits for them, and re-layouts: 3.09 us -> 0.76 us
  Pallas kernels: 12.5 us -> 14.3 us
  starting transfers between devices: 41.7 us -> 42.8 us
  waiting for transfers between devices: 9.5 us -> 8.68 us
    unnamed x14 -> x12, local copies, waits for them, and re-layouts: 2.36 us -> 0.04 us
    pallas_call x2 -> x1, Pallas kernels: 3.06 us -> 4.87 us  [finish(): pl.pallas_call(finish_kernel, in_specs=[ANY] + [VMEM] * (3 + len(returned...]
    ppermute x12, starting transfers between devices: 24.6 us -> 25.7 us  [swapped(): lax.ppermute(block, AXES, [(low, low ^ 1 << bit) for low in range(count)])]
  transfers between devices with their start and end apart: 15 -> 15, of which waited for: 4 -> 4; matrix products, arithmetic and copies ran while one was open for 0% -> 0% of each run, Pallas kernels for 9% -> 12%
where the time goes in v4:
time: 67.8 us; the launch traced here: 67.4 us
  starting transfers between devices  42.8 us (63%)
  Pallas kernels  14.3 us (21%)
  waiting for transfers between devices  8.68 us (13%)
  between operations  0.86 us (1%)
  local copies, waits for them, and re-layouts  0.76 us (1%)
    ppermute x12, starting transfers between devices, swapped(): lax.ppermute(block, AXES, [(low, low ^ 1 << bit) for low in range(count)])  25.7 us
    all_to_all x2, starting transfers between devices, per_device(): pieces = lax.all_to_all(pieces, PLANE, 0, 0, tiled=True)  13.8 us
    all_to_all x2, waiting for transfers between devices, per_device(): pieces = lax.all_to_all(pieces, PLANE, 0, 0, tiled=True)  6.06 us
    pallas_call x1, Pallas kernels, finish(): pl.pallas_call(finish_kernel, in_specs=[ANY] + [VMEM] * (3 + len(returned...  4.87 us
    pallas_call x1, Pallas kernels, middle(): pl.pallas_call(functools.partial(middle_kernel, turns), in_specs=[VMEM] *...  3.42 us
    all_to_all x1, starting transfers between devices, per_device(): pieces = lax.all_to_all(pieces, AXES[:1], 0, 0, tiled=True)  3.36 us
    pallas_call x1, Pallas kernels, gather_rows(): pl.pallas_call(functools.partial(gather_kernel, rounds), in_specs=[ANY, A...  2.65 us
    pallas_call x1, Pallas kernels, early_sum(): pl.pallas_call(functools.partial(early_kernel, turns), out_shape=jax.Shap...  2.02 us
  transfers between devices with their start and end apart: 15, of which 4 were waited for; matrix products, arithmetic and copies ran while one was open for 0% of the time, Pallas kernels for 12%

profile of v4, /device:TPU:1, one launch (start us, length us, event | category | flops | bytes accessed | tf_op | source)
XLA Modules:
  0.0 67.4 jit_solution(16654365322416805018)
XLA Ops:
  0.6 2.7 %gather_rows.1 = (bf16[256,128]{1,0:T(8,128)(2,1)S(1)}, bf16[256,128]{1,0:T(8,128)(2,1)S(1)}, bf16[256,128]{1,0:T(8,128)(2,1)S(1)}, bf16[256,128]{1,0:T(8,128)(2...) custom-call(bf16[1536,128]{1,0:T(8,128)(2,1)} %feats_hbm.1, ...), custom_call_target="tpu_custom_call" | custom-call | flops 603979776 | bytes 393216 | tf_op jit(solution)/shard_map/gather_rows/pallas_call | solution.py:72
  3.3 2.6 %collective-permute-start = (bf16[256,128]{1,0:T(8,128)(2,1)S(1)}, bf16[256,128]{1,0:T(8,128)(2,1)S(1)}, u32[]{:S(2)}, u32[]{:S(2)}) collective-permute-start(bf16[256,128]{1,0:T(8,128)(2,1)S(1)} %get-tuple-element.27), channel_id=1, source_target_pairs={{0,32},{1,33},{2,34},{3,35},{4,36},{5,37},{6,38},{7,39},{8,40},{9,... | collective-permute-start | bytes 196616 | tf_op jit(solution)/shard_map/ppermute | solution.py:272
  5.9 2.9 %collective-permute-start.1 = (bf16[256,128]{1,0:T(8,128)(2,1)S(1)}, bf16[256,128]{1,0:T(8,128)(2,1)S(1)}, u32[]{:S(2)}, u32[]{:S(2)}) collective-permute-start(bf16[256,128]{1,0:T(8,128)(2,1)S(1)} %get-tuple-element.28), channel_id=1, source_target_pairs={{0,16},{1,17},{2,18},{3,19},{4,20},{5,21},{6,22},{7,23},{8,24},{9,... | collective-permute-start | bytes 196616 | tf_op jit(solution)/shard_map/ppermute | solution.py:272
  8.8 3.0 %collective-permute-start.2 = (bf16[256,128]{1,0:T(8,128)(2,1)S(1)}, bf16[256,128]{1,0:T(8,128)(2,1)S(1)}, u32[]{:S(2)}, u32[]{:S(2)}) collective-permute-start(bf16[256,128]{1,0:T(8,128)(2,1)S(1)} %get-tuple-element.29), channel_id=1, source_target_pairs={{0,64},{1,65},{2,66},{3,67},{4,68},{5,69},{6,70},{7,71},{8,72},{9,... | collective-permute-start | bytes 196616 | tf_op jit(solution)/shard_map/ppermute | solution.py:272
  11.8 4.2 %collective-permute-start.3 = (bf16[256,128]{1,0:T(8,128)(2,1)S(1)}, bf16[256,128]{1,0:T(8,128)(2,1)S(1)}, u32[]{:S(2)}, u32[]{:S(2)}) collective-permute-start(bf16[256,128]{1,0:T(8,128)(2,1)S(1)} %get-tuple-element.30), channel_id=1, source_target_pairs={{0,128},{1,129},{2,130},{3,131},{4,132},{5,133},{6,134},{7,135},{8... | collective-permute-start | bytes 196616 | tf_op jit(solution)/shard_map/ppermute | solution.py:272
  16.0 2.7 %collective-permute-start.4 = (bf16[256,128]{1,0:T(8,128)(2,1)S(1)}, bf16[256,128]{1,0:T(8,128)(2,1)S(1)}, u32[]{:S(2)}, u32[]{:S(2)}) collective-permute-start(bf16[256,128]{1,0:T(8,128)(2,1)S(1)} %get-tuple-element.31), channel_id=1, source_target_pairs={{0,4},{1,5},{2,6},{3,7},{4,0},{5,1},{6,2},{7,3},{8,12},{9,13},{10,... | collective-permute-start | bytes 196616 | tf_op jit(solution)/shard_map/ppermute | solution.py:272
  18.7 0.0 collective-permute-done.refs_0_
  18.7 0.4 collective-permute-start.5
  19.1 0.0 copy-start.2
  19.1 0.0 copy-start.3
  19.2 0.0 copy-start.4
  19.2 0.0 copy-start.5
  19.2 2.0 %early_sum.1.refs_0_ = f32[1536,256]{1,0:T(8,128)S(1)} custom-call(bf16[1536,1536]{1,0:T(8,128)(2,1)S(1)} %get-tuple-element.25.adj_ref, bf16[1536,256]{1,0:T(8,128)(2,1)S(1)} %get-tuple-element.26.wide_ref.refs_2_, bf16[6,1536,256]{2,1,0:T(8,128)(2,1)S(1)} %bitcast.6, bf16[256,128]{1,0:T(8,128)(2,1)S(1)} %collective-permute-done.refs_0_, ...), custom_call_target="tpu_custom_call" | custom-call | flops 1207959552 | bytes 4718592 | tf_op jit(solution)/shard_map/early_sum/pallas_call | solution.py:109
  21.2 0.9 %collective-permute-done.5.refs_9_ = bf16[256,128]{1,0:T(8,128)(2,1)S(1)} collective-permute-done((bf16[256,128]{1,0:T(8,128)(2,1)S(1)}, bf16[256,128]{1,0:T(8,128)(2,1)S(1)}, u32[]{:S(2)}, u32[]{:S(2)}) %collective-permute-start.5) | collective-permute-done | bytes 65568 | tf_op jit(solution)/shard_map/ppermute | solution.py:272
  22.2 0.0 copy-start.1
  22.2 3.4 %middle.1 = (bf16[1536,256]{1,0:T(8,128)(2,1)}, bf16[1536,128]{1,0:T(8,128)(2,1)S(1)}, f32[1536,128]{1,0:T(8,128)S(1)}, bf16[2,256,128]{2,1,0:T(8,128)(2,1)}, bf...) custom-call(f32[1536,256]{1,0:T(8,128)S(1)} %early_sum.1.refs_0_, ...), custom_call_target="tpu_custom_call" | custom-call | flops 2415919104 | bytes 4718592 | tf_op jit(solution)/shard_map/middle/pallas_call | solution.py:169
  25.6 6.5 %all-to-all-start = ((bf16[32,16,128]{2,1,0:T(8,128)(2,1)}), bf16[32,16,128]{2,1,0:T(8,128)(2,1)S(1)}, u32[]{:S(2)}, u32[]{:S(2)}) async-start(bf16[32,16,128]{2,1,0:T(8,128)(2,1)} %bitcast.13), calls=%async_computation | async-start | bytes 262144 | tf_op jit(solution)/shard_map/all_to_all | solution.py:302
  32.0 2.2 %collective-permute-start.6 = (bf16[256,128]{1,0:T(8,128)(2,1)S(1)}, bf16[256,128]{1,0:T(8,128)(2,1)S(1)}, u32[]{:S(2)}, u32[]{:S(2)}) collective-permute-start(bf16[256,128]{1,0:T(8,128)(2,1)S(1)} %get-tuple-element.36), channel_id=1, source_target_pairs={{0,128},{1,129},{2,130},{3,131},{4,132},{5,133},{6,134},{7,135},{8... | collective-permute-start | bytes 196616 | tf_op jit(solution)/shard_map/ppermute | solution.py:272
  34.3 0.8 %collective-permute-start.7 = (bf16[256,128]{1,0:T(8,128)(2,1)S(1)}, bf16[256,128]{1,0:T(8,128)(2,1)S(1)}, u32[]{:S(2)}, u32[]{:S(2)}) collective-permute-start(bf16[256,128]{1,0:T(8,128)(2,1)S(1)} %get-tuple-element.38), channel_id=1, source_target_pairs={{0,32},{1,33},{2,34},{3,35},{4,36},{5,37},{6,38},{7,39},{8,40},{9,... | collective-permute-start | bytes 196616 | tf_op jit(solution)/shard_map/ppermute | solution.py:272
  35.0 1.4 %collective-permute-start.8 = (bf16[256,128]{1,0:T(8,128)(2,1)S(1)}, bf16[256,128]{1,0:T(8,128)(2,1)S(1)}, u32[]{:S(2)}, u32[]{:S(2)}) collective-permute-start(bf16[256,128]{1,0:T(8,128)(2,1)S(1)} %get-tuple-element.39), channel_id=1, source_target_pairs={{0,8},{1,9},{2,10},{3,11},{4,12},{5,13},{6,14},{7,15},{8,0},{9,1},... | collective-permute-start | bytes 196616 | tf_op jit(solution)/shard_map/ppermute | solution.py:272
  36.4 3.4 %all-to-all-done.parts_ref = bf16[32,16,128]{2,1,0:T(8,128)(2,1)S(1)} async-done(((bf16[32,16,128]{2,1,0:T(8,128)(2,1)}), bf16[32,16,128]{2,1,0:T(8,128)(2,1)S(1)}, u32[]{:S(2)}, u32[]{:S(2)}) %all-to-all-start) | async-done | bytes 131104 | tf_op jit(solution)/shard_map/all_to_all | solution.py:302
  39.8 0.7 %sum_and_spread.2 = f32[8,16,128]{2,1,0:T(8,128)} custom-call(bf16[32,16,128]{2,1,0:T(8,128)(2,1)S(1)} %all-to-all-done.parts_ref), custom_call_target="tpu_custom_call" | custom-call | tf_op jit(solution)/shard_map/sum_and_spread/pallas_call | solution.py:219
  40.5 3.4 %all-to-all-start.1 = ((f32[8,16,128]{2,1,0:T(8,128)}), f32[8,16,128]{2,1,0:T(8,128)S(1)}, u32[]{:S(2)}, u32[]{:S(2)}) async-start(f32[8,16,128]{2,1,0:T(8,128)} %sum_and_spread.2), calls=%async_computation.1 | async-start | bytes 131072 | tf_op jit(solution)/shard_map/all_to_all | solution.py:307
  43.9 2.4 %collective-permute-start.9 = (bf16[256,128]{1,0:T(8,128)(2,1)S(1)}, bf16[256,128]{1,0:T(8,128)(2,1)S(1)}, u32[]{:S(2)}, u32[]{:S(2)}) collective-permute-start(bf16[256,128]{1,0:T(8,128)(2,1)S(1)} %get-tuple-element.40), channel_id=1, source_target_pairs={{0,64},{1,65},{2,66},{3,67},{4,68},{5,69},{6,70},{7,71},{8,72},{9,... | collective-permute-start | bytes 196616 | tf_op jit(solution)/shard_map/ppermute | solution.py:272
  46.3 1.0 %collective-permute-start.10 = (bf16[256,128]{1,0:T(8,128)(2,1)S(1)}, bf16[256,128]{1,0:T(8,128)(2,1)S(1)}, u32[]{:S(2)}, u32[]{:S(2)}) collective-permute-start(bf16[256,128]{1,0:T(8,128)(2,1)S(1)} %get-tuple-element.42), channel_id=1, source_target_pairs={{0,16},{1,17},{2,18},{3,19},{4,20},{5,21},{6,22},{7,23},{8,24},{9,... | collective-permute-start | bytes 196616 | tf_op jit(solution)/shard_map/ppermute | solution.py:272
  47.3 2.0 %collective-permute-start.11 = (bf16[256,128]{1,0:T(8,128)(2,1)S(1)}, bf16[256,128]{1,0:T(8,128)(2,1)S(1)}, u32[]{:S(2)}, u32[]{:S(2)}) collective-permute-start(bf16[256,128]{1,0:T(8,128)(2,1)S(1)} %get-tuple-element.44), channel_id=1, source_target_pairs={{0,4},{1,5},{2,6},{3,7},{4,0},{5,1},{6,2},{7,3},{8,12},{9,13},{10,... | collective-permute-start | bytes 196616 | tf_op jit(solution)/shard_map/ppermute | solution.py:272
  49.3 1.7 %all-to-all-done.1.parts_ref = f32[8,16,128]{2,1,0:T(8,128)S(1)} async-done(((f32[8,16,128]{2,1,0:T(8,128)}), f32[8,16,128]{2,1,0:T(8,128)S(1)}, u32[]{:S(2)}, u32[]{:S(2)}) %all-to-all-start.1) | async-done | bytes 65568 | tf_op jit(solution)/shard_map/all_to_all | solution.py:307
  51.0 0.7 %sum_and_spread.3 = bf16[32,16,128]{2,1,0:T(8,128)(2,1)} custom-call(f32[8,16,128]{2,1,0:T(8,128)S(1)} %all-to-all-done.1.parts_ref), custom_call_target="tpu_custom_call" | custom-call | tf_op jit(solution)/shard_map/sum_and_spread/pallas_call | solution.py:219
  51.7 7.3 %all-to-all-start.2 = ((bf16[32,16,128]{2,1,0:T(8,128)(2,1)}), bf16[32,16,128]{2,1,0:T(8,128)(2,1)S(1)}, u32[]{:S(2)}, u32[]{:S(2)}) async-start(bf16[32,16,128]{2,1,0:T(8,128)(2,1)} %sum_and_spread.3), calls=%async_computation.2 | async-start | bytes 262144 | tf_op jit(solution)/shard_map/all_to_all | solution.py:312
  59.1 4.9 %finish.1 = bf16[1536,128]{1,0:T(8,128)(2,1)} custom-call(bf16[1536,1536]{1,0:T(8,128)(2,1)} %adj_hbm.3, bf16[1536,128]{1,0:T(8,128)(2,1)S(1)} %get-tuple-element.34.dagg_ref, f32[1536,128]{1,0:T(8,128)S(1)} %get-tuple-element.35.gself_ref, s32[6,1,256]{2,1,0:T(1,128)S(1)} %bitcast.9, bf16[256,128]{1,0:T(8,128)(2,1)S(1)} %collective-permute-done.6.refs_0_, ...), custom_call_target="tpu_custom_call" | custom-call | flops 1207959552 | bytes 4718592 | tf_op jit(solution)/shard_map/finish/pallas_call | solution.py:255
  64.0 2.7 %all-to-all-done.2 = bf16[32,16,128]{2,1,0:T(8,128)(2,1)S(1)} async-done(((bf16[32,16,128]{2,1,0:T(8,128)(2,1)}), bf16[32,16,128]{2,1,0:T(8,128)(2,1)S(1)}, u32[]{:S(2)}, u32[]{:S(2)}) %all-to-all-start.2) | async-done | bytes 131104 | tf_op jit(solution)/shard_map/all_to_all | solution.py:312
  66.7 0.7 %fusion = (f32[128,256]{1,0:T(8,128)}, f32[128,256]{1,0:T(8,128)}) fusion(f32[256,256]{1,0:T(8,128)S(1)} %maximum_convert_fusion), kind=kLoop, calls=%fused_computation.1 | loop fusion | bytes 524288 | tf_op jit(solution)/shard_map/slice | solution.py:317
  (19 shorter events, 0.1 us)
Async XLA Ops:
  0.6 18.5 %copy-start = (bf16[1,6,1536,256]{3,2,1,0:T(8,128)(2,1)S(1)}, bf16[1,6,1536,256]{3,2,1,0:T(8,128)(2,1)}, u32[]{:S(2)}) copy-start(bf16[1,6,1536,256]{3,2,1,0:T(8,128)(2,1)} %param.10) | copy-start | bytes 14155780
  3.3 15.4 %collective-permute-start = (bf16[256,128]{1,0:T(8,128)(2,1)S(1)}, bf16[256,128]{1,0:T(8,128)(2,1)S(1)}, u32[]{:S(2)}, u32[]{:S(2)}) collective-permute-start(bf16[256,128]{1,0:T(8,128)(2,1)S(1)} %get-tuple-element.27), channel_id=1, source_target_pairs={{0,32},{1,33},{2,34},{3,35},{4,36},{5,37},{6,38},{7,39},{8,40},{9,... | collective-permute-start | bytes 196616 | tf_op jit(solution)/shard_map/ppermute | solution.py:272
  5.9 13.3 %collective-permute-start.1 = (bf16[256,128]{1,0:T(8,128)(2,1)S(1)}, bf16[256,128]{1,0:T(8,128)(2,1)S(1)}, u32[]{:S(2)}, u32[]{:S(2)}) collective-permute-start(bf16[256,128]{1,0:T(8,128)(2,1)S(1)} %get-tuple-element.28), channel_id=1, source_target_pairs={{0,16},{1,17},{2,18},{3,19},{4,20},{5,21},{6,22},{7,23},{8,24},{9,... | collective-permute-start | bytes 196616 | tf_op jit(solution)/shard_map/ppermute | solution.py:272
  8.8 10.4 %collective-permute-start.2 = (bf16[256,128]{1,0:T(8,128)(2,1)S(1)}, bf16[256,128]{1,0:T(8,128)(2,1)S(1)}, u32[]{:S(2)}, u32[]{:S(2)}) collective-permute-start(bf16[256,128]{1,0:T(8,128)(2,1)S(1)} %get-tuple-element.29), channel_id=1, source_target_pairs={{0,64},{1,65},{2,66},{3,67},{4,68},{5,69},{6,70},{7,71},{8,72},{9,... | collective-permute-start | bytes 196616 | tf_op jit(solution)/shard_map/ppermute | solution.py:272
  11.8 9.4 %collective-permute-start.3 = (bf16[256,128]{1,0:T(8,128)(2,1)S(1)}, bf16[256,128]{1,0:T(8,128)(2,1)S(1)}, u32[]{:S(2)}, u32[]{:S(2)}) collective-permute-start(bf16[256,128]{1,0:T(8,128)(2,1)S(1)} %get-tuple-element.30), channel_id=1, source_target_pairs={{0,128},{1,129},{2,130},{3,131},{4,132},{5,133},{6,134},{7,135},{8... | collective-permute-start | bytes 196616 | tf_op jit(solution)/shard_map/ppermute | solution.py:272
  16.0 5.2 %collective-permute-start.4 = (bf16[256,128]{1,0:T(8,128)(2,1)S(1)}, bf16[256,128]{1,0:T(8,128)(2,1)S(1)}, u32[]{:S(2)}, u32[]{:S(2)}) collective-permute-start(bf16[256,128]{1,0:T(8,128)(2,1)S(1)} %get-tuple-element.31), channel_id=1, source_target_pairs={{0,4},{1,5},{2,6},{3,7},{4,0},{5,1},{6,2},{7,3},{8,12},{9,13},{10,... | collective-permute-start | bytes 196616 | tf_op jit(solution)/shard_map/ppermute | solution.py:272
  18.7 3.4 %collective-permute-start.5 = (bf16[256,128]{1,0:T(8,128)(2,1)S(1)}, bf16[256,128]{1,0:T(8,128)(2,1)S(1)}, u32[]{:S(2)}, u32[]{:S(2)}) collective-permute-start(bf16[256,128]{1,0:T(8,128)(2,1)S(1)} %get-tuple-element.32), channel_id=1, source_target_pairs={{0,8},{1,9},{2,10},{3,11},{4,12},{5,13},{6,14},{7,15},{8,0},{9,1},... | collective-permute-start | bytes 196616 | tf_op jit(solution)/shard_map/ppermute | solution.py:272
  19.1 3.0 %copy-start.2 = (bf16[1536,256]{1,0:T(8,128)(2,1)S(1)}, bf16[1536,256]{1,0:T(8,128)(2,1)}, u32[]{:S(2)}) copy-start(bf16[1536,256]{1,0:T(8,128)(2,1)} %refs_3_.1) | copy-start | bytes 2359300
  19.1 3.0 %copy-start.3 = (bf16[128,256]{1,0:T(8,128)(2,1)S(1)}, bf16[128,256]{1,0:T(8,128)(2,1)}, u32[]{:S(2)}) copy-start(bf16[128,256]{1,0:T(8,128)(2,1)} %refs_4_.1) | copy-start | bytes 196612
  19.2 3.0 %copy-start.4 = (bf16[128,256]{1,0:T(8,128)(2,1)S(1)}, bf16[128,256]{1,0:T(8,128)(2,1)}, u32[]{:S(2)}) copy-start(bf16[128,256]{1,0:T(8,128)(2,1)} %refs_5_.1) | copy-start | bytes 196612
  19.2 3.0 %copy-start.5 = (f32[256]{0:T(256)S(1)}, f32[256]{0:T(256)}, u32[]{:S(2)}) copy-start(f32[256]{0:T(256)} %param.14) | copy-start | bytes 3076
  22.2 36.9 %copy-start.1 = (s32[1,6,256]{2,0,1:T(1,128)S(1)}, s32[1,6,256]{2,0,1:T(1,128)}, u32[]{:S(2)}) copy-start(s32[1,6,256]{2,0,1:T(1,128)} %param.11) | copy-start | bytes 18436
  25.6 14.2 %all-to-all-start = ((bf16[32,16,128]{2,1,0:T(8,128)(2,1)}), bf16[32,16,128]{2,1,0:T(8,128)(2,1)S(1)}, u32[]{:S(2)}, u32[]{:S(2)}) async-start(bf16[32,16,128]{2,1,0:T(8,128)(2,1)} %bitcast.13), calls=%async_computation | async-start | bytes 262144 | tf_op jit(solution)/shard_map/all_to_all | solution.py:302
  32.0 11.8 %collective-permute-start.6 = (bf16[256,128]{1,0:T(8,128)(2,1)S(1)}, bf16[256,128]{1,0:T(8,128)(2,1)S(1)}, u32[]{:S(2)}, u32[]{:S(2)}) collective-permute-start(bf16[256,128]{1,0:T(8,128)(2,1)S(1)} %get-tuple-element.36), channel_id=1, source_target_pairs={{0,128},{1,129},{2,130},{3,131},{4,132},{5,133},{6,134},{7,135},{8... | collective-permute-start | bytes 196616 | tf_op jit(solution)/shard_map/ppermute | solution.py:272
  34.3 9.6 %collective-permute-start.7 = (bf16[256,128]{1,0:T(8,128)(2,1)S(1)}, bf16[256,128]{1,0:T(8,128)(2,1)S(1)}, u32[]{:S(2)}, u32[]{:S(2)}) collective-permute-start(bf16[256,128]{1,0:T(8,128)(2,1)S(1)} %get-tuple-element.38), channel_id=1, source_target_pairs={{0,32},{1,33},{2,34},{3,35},{4,36},{5,37},{6,38},{7,39},{8,40},{9,... | collective-permute-start | bytes 196616 | tf_op jit(solution)/shard_map/ppermute | solution.py:272
  35.0 8.8 %collective-permute-start.8 = (bf16[256,128]{1,0:T(8,128)(2,1)S(1)}, bf16[256,128]{1,0:T(8,128)(2,1)S(1)}, u32[]{:S(2)}, u32[]{:S(2)}) collective-permute-start(bf16[256,128]{1,0:T(8,128)(2,1)S(1)} %get-tuple-element.39), channel_id=1, source_target_pairs={{0,8},{1,9},{2,10},{3,11},{4,12},{5,13},{6,14},{7,15},{8,0},{9,1},... | collective-permute-start | bytes 196616 | tf_op jit(solution)/shard_map/ppermute | solution.py:272
  40.5 10.5 %all-to-all-start.1 = ((f32[8,16,128]{2,1,0:T(8,128)}), f32[8,16,128]{2,1,0:T(8,128)S(1)}, u32[]{:S(2)}, u32[]{:S(2)}) async-start(f32[8,16,128]{2,1,0:T(8,128)} %sum_and_spread.2), calls=%async_computation.1 | async-start | bytes 131072 | tf_op jit(solution)/shard_map/all_to_all | solution.py:307
  43.9 15.2 %collective-permute-start.9 = (bf16[256,128]{1,0:T(8,128)(2,1)S(1)}, bf16[256,128]{1,0:T(8,128)(2,1)S(1)}, u32[]{:S(2)}, u32[]{:S(2)}) collective-permute-start(bf16[256,128]{1,0:T(8,128)(2,1)S(1)} %get-tuple-element.40), channel_id=1, source_target_pairs={{0,64},{1,65},{2,66},{3,67},{4,68},{5,69},{6,70},{7,71},{8,72},{9,... | collective-permute-start | bytes 196616 | tf_op jit(solution)/shard_map/ppermute | solution.py:272
  46.3 12.8 %collective-permute-start.10 = (bf16[256,128]{1,0:T(8,128)(2,1)S(1)}, bf16[256,128]{1,0:T(8,128)(2,1)S(1)}, u32[]{:S(2)}, u32[]{:S(2)}) collective-permute-start(bf16[256,128]{1,0:T(8,128)(2,1)S(1)} %get-tuple-element.42), channel_id=1, source_target_pairs={{0,16},{1,17},{2,18},{3,19},{4,20},{5,21},{6,22},{7,23},{8,24},{9,... | collective-permute-start | bytes 196616 | tf_op jit(solution)/shard_map/ppermute | solution.py:272
  47.3 11.8 %collective-permute-start.11 = (bf16[256,128]{1,0:T(8,128)(2,1)S(1)}, bf16[256,128]{1,0:T(8,128)(2,1)S(1)}, u32[]{:S(2)}, u32[]{:S(2)}) collective-permute-start(bf16[256,128]{1,0:T(8,128)(2,1)S(1)} %get-tuple-element.44), channel_id=1, source_target_pairs={{0,4},{1,5},{2,6},{3,7},{4,0},{5,1},{6,2},{7,3},{8,12},{9,13},{10,... | collective-permute-start | bytes 196616 | tf_op jit(solution)/shard_map/ppermute | solution.py:272
  51.7 15.0 %all-to-all-start.2 = ((bf16[32,16,128]{2,1,0:T(8,128)(2,1)}), bf16[32,16,128]{2,1,0:T(8,128)(2,1)S(1)}, u32[]{:S(2)}, u32[]{:S(2)}) async-start(bf16[32,16,128]{2,1,0:T(8,128)(2,1)} %sum_and_spread.3), calls=%async_computation.2 | async-start | bytes 262144 | tf_op jit(solution)/shard_map/all_to_all | solution.py:312

commit v5 on v4

--- a/solution.py
+++ b/solution.py
@@ -237,17 +237,15 @@
     ]
     for copy in copies:
         copy.start()
-    base = gself_ref[...]
-    for turn, back_ref in enumerate(back_refs):
-        base = base + dot(one_hot(index_ref[turn], rows), back_ref[...])
-    base_ref[...] = base
+    picked = jnp.concatenate([index_ref[turn] for turn in range(len(back_refs))], axis=1)
+    backs = jnp.concatenate([back_ref[...] for back_ref in back_refs], axis=0)
+    for start in range(0, rows, BLOCK):
+        span = slice(start, start + BLOCK)
+        base_ref[span, :] = gself_ref[span, :] + dot(one_hot(picked - start, BLOCK), backs)
     turned = dagg_ref[...].T
-    total = None
-    for copy, span in zip(copies, spans):
+    for copy in copies:
         copy.wait()
-        part = dot(turned[:, span.start : span.start + BLOCK], adj_ref[span, :])
-        total = part if total is None else total + part
-    out_ref[...] = (base_ref[...] + total.T).astype(out_ref.dtype)
+    out_ref[...] = (base_ref[...] + dot(turned, adj_ref[...]).T).astype(out_ref.dtype)
 
 
 def finish(local_adj, dagg, gself, index_lists, returned):

time: 67.8 us -> 67.8 us (level)
  no operation moved by 1% of the time
where the time goes in v5:
time: 67.8 us; the launch traced here: 67.4 us
  starting transfers between devices  42.8 us (63%)
  Pallas kernels  14 us (21%)
  waiting for transfers between devices  8.98 us (13%)
  between operations  0.86 us (1%)
  local copies, waits for them, and re-layouts  0.76 us (1%)
    ppermute x12, starting transfers between devices, swapped(): lax.ppermute(block, AXES, [(low, low ^ 1 << bit) for low in range(count)])  25.7 us
    all_to_all x2, starting transfers between devices, per_device(): pieces = lax.all_to_all(pieces, PLANE, 0, 0, tiled=True)  13.8 us
    all_to_all x2, waiting for transfers between devices, per_device(): pieces = lax.all_to_all(pieces, PLANE, 0, 0, tiled=True)  6.36 us
    pallas_call x1, Pallas kernels, finish(): pl.pallas_call(finish_kernel, in_specs=[ANY] + [VMEM] * (3 + len(returned...  4.57 us
    pallas_call x1, Pallas kernels, middle(): pl.pallas_call(functools.partial(middle_kernel, turns), in_specs=[VMEM] *...  3.42 us
    all_to_all x1, starting transfers between devices, per_device(): pieces = lax.all_to_all(pieces, AXES[:1], 0, 0, tiled=True)  3.36 us
    pallas_call x1, Pallas kernels, gather_rows(): pl.pallas_call(functools.partial(gather_kernel, rounds), in_specs=[ANY, A...  2.65 us
    pallas_call x1, Pallas kernels, early_sum(): pl.pallas_call(functools.partial(early_kernel, turns), out_shape=jax.Shap...  2.02 us
  transfers between devices with their start and end apart: 15, of which 4 were waited for; matrix products, arithmetic and copies ran while one was open for 0% of the time, Pallas kernels for 12%

profile of v5, /device:TPU:1, one launch (start us, length us, event | category | flops | bytes accessed | tf_op | source)
XLA Modules:
  0.0 67.4 jit_solution(11601038965187421996)
XLA Ops:
  0.6 2.7 %gather_rows.1 = (bf16[256,128]{1,0:T(8,128)(2,1)S(1)}, bf16[256,128]{1,0:T(8,128)(2,1)S(1)}, bf16[256,128]{1,0:T(8,128)(2,1)S(1)}, bf16[256,128]{1,0:T(8,128)(2...) custom-call(bf16[1536,128]{1,0:T(8,128)(2,1)} %feats_hbm.1, ...), custom_call_target="tpu_custom_call" | custom-call | flops 603979776 | bytes 393216 | tf_op jit(solution)/shard_map/gather_rows/pallas_call | solution.py:72
  3.3 2.6 %collective-permute-start = (bf16[256,128]{1,0:T(8,128)(2,1)S(1)}, bf16[256,128]{1,0:T(8,128)(2,1)S(1)}, u32[]{:S(2)}, u32[]{:S(2)}) collective-permute-start(bf16[256,128]{1,0:T(8,128)(2,1)S(1)} %get-tuple-element.27), channel_id=1, source_target_pairs={{0,32},{1,33},{2,34},{3,35},{4,36},{5,37},{6,38},{7,39},{8,40},{9,... | collective-permute-start | bytes 196616 | tf_op jit(solution)/shard_map/ppermute | solution.py:270
  5.9 2.9 %collective-permute-start.1 = (bf16[256,128]{1,0:T(8,128)(2,1)S(1)}, bf16[256,128]{1,0:T(8,128)(2,1)S(1)}, u32[]{:S(2)}, u32[]{:S(2)}) collective-permute-start(bf16[256,128]{1,0:T(8,128)(2,1)S(1)} %get-tuple-element.28), channel_id=1, source_target_pairs={{0,16},{1,17},{2,18},{3,19},{4,20},{5,21},{6,22},{7,23},{8,24},{9,... | collective-permute-start | bytes 196616 | tf_op jit(solution)/shard_map/ppermute | solution.py:270
  8.8 3.0 %collective-permute-start.2 = (bf16[256,128]{1,0:T(8,128)(2,1)S(1)}, bf16[256,128]{1,0:T(8,128)(2,1)S(1)}, u32[]{:S(2)}, u32[]{:S(2)}) collective-permute-start(bf16[256,128]{1,0:T(8,128)(2,1)S(1)} %get-tuple-element.29), channel_id=1, source_target_pairs={{0,64},{1,65},{2,66},{3,67},{4,68},{5,69},{6,70},{7,71},{8,72},{9,... | collective-permute-start | bytes 196616 | tf_op jit(solution)/shard_map/ppermute | solution.py:270
  11.8 4.2 %collective-permute-start.3 = (bf16[256,128]{1,0:T(8,128)(2,1)S(1)}, bf16[256,128]{1,0:T(8,128)(2,1)S(1)}, u32[]{:S(2)}, u32[]{:S(2)}) collective-permute-start(bf16[256,128]{1,0:T(8,128)(2,1)S(1)} %get-tuple-element.30), channel_id=1, source_target_pairs={{0,128},{1,129},{2,130},{3,131},{4,132},{5,133},{6,134},{7,135},{8... | collective-permute-start | bytes 196616 | tf_op jit(solution)/shard_map/ppermute | solution.py:270
  16.0 2.7 %collective-permute-start.4 = (bf16[256,128]{1,0:T(8,128)(2,1)S(1)}, bf16[256,128]{1,0:T(8,128)(2,1)S(1)}, u32[]{:S(2)}, u32[]{:S(2)}) collective-permute-start(bf16[256,128]{1,0:T(8,128)(2,1)S(1)} %get-tuple-element.31), channel_id=1, source_target_pairs={{0,4},{1,5},{2,6},{3,7},{4,0},{5,1},{6,2},{7,3},{8,12},{9,13},{10,... | collective-permute-start | bytes 196616 | tf_op jit(solution)/shard_map/ppermute | solution.py:270
  18.7 0.0 collective-permute-done.refs_0_
  18.7 0.4 collective-permute-start.5
  19.1 0.0 copy-start.2
  19.1 0.0 copy-start.3
  19.2 0.0 copy-start.4
  19.2 0.0 copy-start.5
  19.2 2.0 %early_sum.1.refs_0_ = f32[1536,256]{1,0:T(8,128)S(1)} custom-call(bf16[1536,1536]{1,0:T(8,128)(2,1)S(1)} %get-tuple-element.25.adj_ref, bf16[1536,256]{1,0:T(8,128)(2,1)S(1)} %get-tuple-element.26.wide_ref.refs_2_, bf16[6,1536,256]{2,1,0:T(8,128)(2,1)S(1)} %bitcast.6, bf16[256,128]{1,0:T(8,128)(2,1)S(1)} %collective-permute-done.refs_0_, ...), custom_call_target="tpu_custom_call" | custom-call | flops 1207959552 | bytes 4718592 | tf_op jit(solution)/shard_map/early_sum/pallas_call | solution.py:109
  21.2 0.9 %collective-permute-done.5.refs_9_ = bf16[256,128]{1,0:T(8,128)(2,1)S(1)} collective-permute-done((bf16[256,128]{1,0:T(8,128)(2,1)S(1)}, bf16[256,128]{1,0:T(8,128)(2,1)S(1)}, u32[]{:S(2)}, u32[]{:S(2)}) %collective-permute-start.5) | collective-permute-done | bytes 65568 | tf_op jit(solution)/shard_map/ppermute | solution.py:270
  22.2 0.0 copy-start.1
  22.2 3.4 %middle.1 = (bf16[1536,256]{1,0:T(8,128)(2,1)}, bf16[1536,128]{1,0:T(8,128)(2,1)S(1)}, f32[1536,128]{1,0:T(8,128)S(1)}, bf16[2,256,128]{2,1,0:T(8,128)(2,1)}, bf...) custom-call(f32[1536,256]{1,0:T(8,128)S(1)} %early_sum.1.refs_0_, ...), custom_call_target="tpu_custom_call" | custom-call | flops 2415919104 | bytes 4718592 | tf_op jit(solution)/shard_map/middle/pallas_call | solution.py:169
  25.6 6.5 %all-to-all-start = ((bf16[32,16,128]{2,1,0:T(8,128)(2,1)}), bf16[32,16,128]{2,1,0:T(8,128)(2,1)S(1)}, u32[]{:S(2)}, u32[]{:S(2)}) async-start(bf16[32,16,128]{2,1,0:T(8,128)(2,1)} %bitcast.13), calls=%async_computation | async-start | bytes 262144 | tf_op jit(solution)/shard_map/all_to_all | solution.py:300
  32.0 2.2 %collective-permute-start.6 = (bf16[256,128]{1,0:T(8,128)(2,1)S(1)}, bf16[256,128]{1,0:T(8,128)(2,1)S(1)}, u32[]{:S(2)}, u32[]{:S(2)}) collective-permute-start(bf16[256,128]{1,0:T(8,128)(2,1)S(1)} %get-tuple-element.36), channel_id=1, source_target_pairs={{0,128},{1,129},{2,130},{3,131},{4,132},{5,133},{6,134},{7,135},{8... | collective-permute-start | bytes 196616 | tf_op jit(solution)/shard_map/ppermute | solution.py:270
  34.3 0.8 %collective-permute-start.7 = (bf16[256,128]{1,0:T(8,128)(2,1)S(1)}, bf16[256,128]{1,0:T(8,128)(2,1)S(1)}, u32[]{:S(2)}, u32[]{:S(2)}) collective-permute-start(bf16[256,128]{1,0:T(8,128)(2,1)S(1)} %get-tuple-element.38), channel_id=1, source_target_pairs={{0,32},{1,33},{2,34},{3,35},{4,36},{5,37},{6,38},{7,39},{8,40},{9,... | collective-permute-start | bytes 196616 | tf_op jit(solution)/shard_map/ppermute | solution.py:270
  35.0 1.4 %collective-permute-start.8 = (bf16[256,128]{1,0:T(8,128)(2,1)S(1)}, bf16[256,128]{1,0:T(8,128)(2,1)S(1)}, u32[]{:S(2)}, u32[]{:S(2)}) collective-permute-start(bf16[256,128]{1,0:T(8,128)(2,1)S(1)} %get-tuple-element.39), channel_id=1, source_target_pairs={{0,8},{1,9},{2,10},{3,11},{4,12},{5,13},{6,14},{7,15},{8,0},{9,1},... | collective-permute-start | bytes 196616 | tf_op jit(solution)/shard_map/ppermute | solution.py:270
  36.4 3.4 %all-to-all-done.parts_ref = bf16[32,16,128]{2,1,0:T(8,128)(2,1)S(1)} async-done(((bf16[32,16,128]{2,1,0:T(8,128)(2,1)}), bf16[32,16,128]{2,1,0:T(8,128)(2,1)S(1)}, u32[]{:S(2)}, u32[]{:S(2)}) %all-to-all-start) | async-done | bytes 131104 | tf_op jit(solution)/shard_map/all_to_all | solution.py:300
  39.8 0.7 %sum_and_spread.2 = f32[8,16,128]{2,1,0:T(8,128)} custom-call(bf16[32,16,128]{2,1,0:T(8,128)(2,1)S(1)} %all-to-all-done.parts_ref), custom_call_target="tpu_custom_call" | custom-call | tf_op jit(solution)/shard_map/sum_and_spread/pallas_call | solution.py:219
  40.5 3.4 %all-to-all-start.1 = ((f32[8,16,128]{2,1,0:T(8,128)}), f32[8,16,128]{2,1,0:T(8,128)S(1)}, u32[]{:S(2)}, u32[]{:S(2)}) async-start(f32[8,16,128]{2,1,0:T(8,128)} %sum_and_spread.2), calls=%async_computation.1 | async-start | bytes 131072 | tf_op jit(solution)/shard_map/all_to_all | solution.py:305
  43.9 2.4 %collective-permute-start.9 = (bf16[256,128]{1,0:T(8,128)(2,1)S(1)}, bf16[256,128]{1,0:T(8,128)(2,1)S(1)}, u32[]{:S(2)}, u32[]{:S(2)}) collective-permute-start(bf16[256,128]{1,0:T(8,128)(2,1)S(1)} %get-tuple-element.40), channel_id=1, source_target_pairs={{0,64},{1,65},{2,66},{3,67},{4,68},{5,69},{6,70},{7,71},{8,72},{9,... | collective-permute-start | bytes 196616 | tf_op jit(solution)/shard_map/ppermute | solution.py:270
  46.3 1.0 %collective-permute-start.10 = (bf16[256,128]{1,0:T(8,128)(2,1)S(1)}, bf16[256,128]{1,0:T(8,128)(2,1)S(1)}, u32[]{:S(2)}, u32[]{:S(2)}) collective-permute-start(bf16[256,128]{1,0:T(8,128)(2,1)S(1)} %get-tuple-element.42), channel_id=1, source_target_pairs={{0,16},{1,17},{2,18},{3,19},{4,20},{5,21},{6,22},{7,23},{8,24},{9,... | collective-permute-start | bytes 196616 | tf_op jit(solution)/shard_map/ppermute | solution.py:270
  47.3 2.0 %collective-permute-start.11 = (bf16[256,128]{1,0:T(8,128)(2,1)S(1)}, bf16[256,128]{1,0:T(8,128)(2,1)S(1)}, u32[]{:S(2)}, u32[]{:S(2)}) collective-permute-start(bf16[256,128]{1,0:T(8,128)(2,1)S(1)} %get-tuple-element.44), channel_id=1, source_target_pairs={{0,4},{1,5},{2,6},{3,7},{4,0},{5,1},{6,2},{7,3},{8,12},{9,13},{10,... | collective-permute-start | bytes 196616 | tf_op jit(solution)/shard_map/ppermute | solution.py:270
  49.3 1.7 %all-to-all-done.1.parts_ref = f32[8,16,128]{2,1,0:T(8,128)S(1)} async-done(((f32[8,16,128]{2,1,0:T(8,128)}), f32[8,16,128]{2,1,0:T(8,128)S(1)}, u32[]{:S(2)}, u32[]{:S(2)}) %all-to-all-start.1) | async-done | bytes 65568 | tf_op jit(solution)/shard_map/all_to_all | solution.py:305
  51.0 0.7 %sum_and_spread.3 = bf16[32,16,128]{2,1,0:T(8,128)(2,1)} custom-call(f32[8,16,128]{2,1,0:T(8,128)S(1)} %all-to-all-done.1.parts_ref), custom_call_target="tpu_custom_call" | custom-call | tf_op jit(solution)/shard_map/sum_and_spread/pallas_call | solution.py:219
  51.7 7.3 %all-to-all-start.2 = ((bf16[32,16,128]{2,1,0:T(8,128)(2,1)}), bf16[32,16,128]{2,1,0:T(8,128)(2,1)S(1)}, u32[]{:S(2)}, u32[]{:S(2)}) async-start(bf16[32,16,128]{2,1,0:T(8,128)(2,1)} %sum_and_spread.3), calls=%async_computation.2 | async-start | bytes 262144 | tf_op jit(solution)/shard_map/all_to_all | solution.py:310
  59.1 4.6 %finish.1 = bf16[1536,128]{1,0:T(8,128)(2,1)} custom-call(bf16[1536,1536]{1,0:T(8,128)(2,1)} %adj_hbm.3, bf16[1536,128]{1,0:T(8,128)(2,1)S(1)} %get-tuple-element.34.dagg_ref, f32[1536,128]{1,0:T(8,128)S(1)} %get-tuple-element.35.gself_ref, s32[6,1,256]{2,1,0:T(1,128)S(1)} %bitcast.9, bf16[256,128]{1,0:T(8,128)(2,1)S(1)} %collective-permute-done.6.refs_0_, ...), custom_call_target="tpu_custom_call" | custom-call | flops 1207959552 | bytes 4718592 | tf_op jit(solution)/shard_map/finish/pallas_call | solution.py:253
  63.7 3.0 %all-to-all-done.2 = bf16[32,16,128]{2,1,0:T(8,128)(2,1)S(1)} async-done(((bf16[32,16,128]{2,1,0:T(8,128)(2,1)}), bf16[32,16,128]{2,1,0:T(8,128)(2,1)S(1)}, u32[]{:S(2)}, u32[]{:S(2)}) %all-to-all-start.2) | async-done | bytes 131104 | tf_op jit(solution)/shard_map/all_to_all | solution.py:310
  66.7 0.7 %fusion = (f32[128,256]{1,0:T(8,128)}, f32[128,256]{1,0:T(8,128)}) fusion(f32[256,256]{1,0:T(8,128)S(1)} %maximum_convert_fusion), kind=kLoop, calls=%fused_computation.1 | loop fusion | bytes 524288 | tf_op jit(solution)/shard_map/slice | solution.py:315
  (19 shorter events, 0.1 us)
Async XLA Ops:
  0.6 18.5 %copy-start = (bf16[1,6,1536,256]{3,2,1,0:T(8,128)(2,1)S(1)}, bf16[1,6,1536,256]{3,2,1,0:T(8,128)(2,1)}, u32[]{:S(2)}) copy-start(bf16[1,6,1536,256]{3,2,1,0:T(8,128)(2,1)} %param.10) | copy-start | bytes 14155780
  3.3 15.4 %collective-permute-start = (bf16[256,128]{1,0:T(8,128)(2,1)S(1)}, bf16[256,128]{1,0:T(8,128)(2,1)S(1)}, u32[]{:S(2)}, u32[]{:S(2)}) collective-permute-start(bf16[256,128]{1,0:T(8,128)(2,1)S(1)} %get-tuple-element.27), channel_id=1, source_target_pairs={{0,32},{1,33},{2,34},{3,35},{4,36},{5,37},{6,38},{7,39},{8,40},{9,... | collective-permute-start | bytes 196616 | tf_op jit(solution)/shard_map/ppermute | solution.py:270
  5.9 13.3 %collective-permute-start.1 = (bf16[256,128]{1,0:T(8,128)(2,1)S(1)}, bf16[256,128]{1,0:T(8,128)(2,1)S(1)}, u32[]{:S(2)}, u32[]{:S(2)}) collective-permute-start(bf16[256,128]{1,0:T(8,128)(2,1)S(1)} %get-tuple-element.28), channel_id=1, source_target_pairs={{0,16},{1,17},{2,18},{3,19},{4,20},{5,21},{6,22},{7,23},{8,24},{9,... | collective-permute-start | bytes 196616 | tf_op jit(solution)/shard_map/ppermute | solution.py:270
  8.8 10.4 %collective-permute-start.2 = (bf16[256,128]{1,0:T(8,128)(2,1)S(1)}, bf16[256,128]{1,0:T(8,128)(2,1)S(1)}, u32[]{:S(2)}, u32[]{:S(2)}) collective-permute-start(bf16[256,128]{1,0:T(8,128)(2,1)S(1)} %get-tuple-element.29), channel_id=1, source_target_pairs={{0,64},{1,65},{2,66},{3,67},{4,68},{5,69},{6,70},{7,71},{8,72},{9,... | collective-permute-start | bytes 196616 | tf_op jit(solution)/shard_map/ppermute | solution.py:270
  11.8 9.4 %collective-permute-start.3 = (bf16[256,128]{1,0:T(8,128)(2,1)S(1)}, bf16[256,128]{1,0:T(8,128)(2,1)S(1)}, u32[]{:S(2)}, u32[]{:S(2)}) collective-permute-start(bf16[256,128]{1,0:T(8,128)(2,1)S(1)} %get-tuple-element.30), channel_id=1, source_target_pairs={{0,128},{1,129},{2,130},{3,131},{4,132},{5,133},{6,134},{7,135},{8... | collective-permute-start | bytes 196616 | tf_op jit(solution)/shard_map/ppermute | solution.py:270
  16.0 5.2 %collective-permute-start.4 = (bf16[256,128]{1,0:T(8,128)(2,1)S(1)}, bf16[256,128]{1,0:T(8,128)(2,1)S(1)}, u32[]{:S(2)}, u32[]{:S(2)}) collective-permute-start(bf16[256,128]{1,0:T(8,128)(2,1)S(1)} %get-tuple-element.31), channel_id=1, source_target_pairs={{0,4},{1,5},{2,6},{3,7},{4,0},{5,1},{6,2},{7,3},{8,12},{9,13},{10,... | collective-permute-start | bytes 196616 | tf_op jit(solution)/shard_map/ppermute | solution.py:270
  18.7 3.4 %collective-permute-start.5 = (bf16[256,128]{1,0:T(8,128)(2,1)S(1)}, bf16[256,128]{1,0:T(8,128)(2,1)S(1)}, u32[]{:S(2)}, u32[]{:S(2)}) collective-permute-start(bf16[256,128]{1,0:T(8,128)(2,1)S(1)} %get-tuple-element.32), channel_id=1, source_target_pairs={{0,8},{1,9},{2,10},{3,11},{4,12},{5,13},{6,14},{7,15},{8,0},{9,1},... | collective-permute-start | bytes 196616 | tf_op jit(solution)/shard_map/ppermute | solution.py:270
  19.1 3.0 %copy-start.2 = (bf16[1536,256]{1,0:T(8,128)(2,1)S(1)}, bf16[1536,256]{1,0:T(8,128)(2,1)}, u32[]{:S(2)}) copy-start(bf16[1536,256]{1,0:T(8,128)(2,1)} %refs_3_.1) | copy-start | bytes 2359300
  19.1 3.0 %copy-start.3 = (bf16[128,256]{1,0:T(8,128)(2,1)S(1)}, bf16[128,256]{1,0:T(8,128)(2,1)}, u32[]{:S(2)}) copy-start(bf16[128,256]{1,0:T(8,128)(2,1)} %refs_4_.1) | copy-start | bytes 196612
  19.2 3.0 %copy-start.4 = (bf16[128,256]{1,0:T(8,128)(2,1)S(1)}, bf16[128,256]{1,0:T(8,128)(2,1)}, u32[]{:S(2)}) copy-start(bf16[128,256]{1,0:T(8,128)(2,1)} %refs_5_.1) | copy-start | bytes 196612
  19.2 3.0 %copy-start.5 = (f32[256]{0:T(256)S(1)}, f32[256]{0:T(256)}, u32[]{:S(2)}) copy-start(f32[256]{0:T(256)} %param.14) | copy-start | bytes 3076
  22.2 36.9 %copy-start.1 = (s32[1,6,256]{2,0,1:T(1,128)S(1)}, s32[1,6,256]{2,0,1:T(1,128)}, u32[]{:S(2)}) copy-start(s32[1,6,256]{2,0,1:T(1,128)} %param.11) | copy-start | bytes 18436
  25.6 14.2 %all-to-all-start = ((bf16[32,16,128]{2,1,0:T(8,128)(2,1)}), bf16[32,16,128]{2,1,0:T(8,128)(2,1)S(1)}, u32[]{:S(2)}, u32[]{:S(2)}) async-start(bf16[32,16,128]{2,1,0:T(8,128)(2,1)} %bitcast.13), calls=%async_computation | async-start | bytes 262144 | tf_op jit(solution)/shard_map/all_to_all | solution.py:300
  32.0 11.8 %collective-permute-start.6 = (bf16[256,128]{1,0:T(8,128)(2,1)S(1)}, bf16[256,128]{1,0:T(8,128)(2,1)S(1)}, u32[]{:S(2)}, u32[]{:S(2)}) collective-permute-start(bf16[256,128]{1,0:T(8,128)(2,1)S(1)} %get-tuple-element.36), channel_id=1, source_target_pairs={{0,128},{1,129},{2,130},{3,131},{4,132},{5,133},{6,134},{7,135},{8... | collective-permute-start | bytes 196616 | tf_op jit(solution)/shard_map/ppermute | solution.py:270
  34.3 9.6 %collective-permute-start.7 = (bf16[256,128]{1,0:T(8,128)(2,1)S(1)}, bf16[256,128]{1,0:T(8,128)(2,1)S(1)}, u32[]{:S(2)}, u32[]{:S(2)}) collective-permute-start(bf16[256,128]{1,0:T(8,128)(2,1)S(1)} %get-tuple-element.38), channel_id=1, source_target_pairs={{0,32},{1,33},{2,34},{3,35},{4,36},{5,37},{6,38},{7,39},{8,40},{9,... | collective-permute-start | bytes 196616 | tf_op jit(solution)/shard_map/ppermute | solution.py:270
  35.0 8.8 %collective-permute-start.8 = (bf16[256,128]{1,0:T(8,128)(2,1)S(1)}, bf16[256,128]{1,0:T(8,128)(2,1)S(1)}, u32[]{:S(2)}, u32[]{:S(2)}) collective-permute-start(bf16[256,128]{1,0:T(8,128)(2,1)S(1)} %get-tuple-element.39), channel_id=1, source_target_pairs={{0,8},{1,9},{2,10},{3,11},{4,12},{5,13},{6,14},{7,15},{8,0},{9,1},... | collective-permute-start | bytes 196616 | tf_op jit(solution)/shard_map/ppermute | solution.py:270
  40.5 10.5 %all-to-all-start.1 = ((f32[8,16,128]{2,1,0:T(8,128)}), f32[8,16,128]{2,1,0:T(8,128)S(1)}, u32[]{:S(2)}, u32[]{:S(2)}) async-start(f32[8,16,128]{2,1,0:T(8,128)} %sum_and_spread.2), calls=%async_computation.1 | async-start | bytes 131072 | tf_op jit(solution)/shard_map/all_to_all | solution.py:305
  43.9 15.2 %collective-permute-start.9 = (bf16[256,128]{1,0:T(8,128)(2,1)S(1)}, bf16[256,128]{1,0:T(8,128)(2,1)S(1)}, u32[]{:S(2)}, u32[]{:S(2)}) collective-permute-start(bf16[256,128]{1,0:T(8,128)(2,1)S(1)} %get-tuple-element.40), channel_id=1, source_target_pairs={{0,64},{1,65},{2,66},{3,67},{4,68},{5,69},{6,70},{7,71},{8,72},{9,... | collective-permute-start | bytes 196616 | tf_op jit(solution)/shard_map/ppermute | solution.py:270
  46.3 12.8 %collective-permute-start.10 = (bf16[256,128]{1,0:T(8,128)(2,1)S(1)}, bf16[256,128]{1,0:T(8,128)(2,1)S(1)}, u32[]{:S(2)}, u32[]{:S(2)}) collective-permute-start(bf16[256,128]{1,0:T(8,128)(2,1)S(1)} %get-tuple-element.42), channel_id=1, source_target_pairs={{0,16},{1,17},{2,18},{3,19},{4,20},{5,21},{6,22},{7,23},{8,24},{9,... | collective-permute-start | bytes 196616 | tf_op jit(solution)/shard_map/ppermute | solution.py:270
  47.3 11.8 %collective-permute-start.11 = (bf16[256,128]{1,0:T(8,128)(2,1)S(1)}, bf16[256,128]{1,0:T(8,128)(2,1)S(1)}, u32[]{:S(2)}, u32[]{:S(2)}) collective-permute-start(bf16[256,128]{1,0:T(8,128)(2,1)S(1)} %get-tuple-element.44), channel_id=1, source_target_pairs={{0,4},{1,5},{2,6},{3,7},{4,0},{5,1},{6,2},{7,3},{8,12},{9,13},{10,... | collective-permute-start | bytes 196616 | tf_op jit(solution)/shard_map/ppermute | solution.py:270
  51.7 15.0 %all-to-all-start.2 = ((bf16[32,16,128]{2,1,0:T(8,128)(2,1)}), bf16[32,16,128]{2,1,0:T(8,128)(2,1)S(1)}, u32[]{:S(2)}, u32[]{:S(2)}) async-start(bf16[32,16,128]{2,1,0:T(8,128)(2,1)} %sum_and_spread.3), calls=%async_computation.2 | async-start | bytes 262144 | tf_op jit(solution)/shard_map/all_to_all | solution.py:310
